TPU v7x, 32 devices: a whole 2x2x4 slice. The times are simulated.
32 devices in a mesh: dp: 4 (over z), fsdp: 8 (over y, x, core).
Axes of the slice: x: 2, y: 2, z: 4, core: 2. Of those that a mesh axis runs over, the one named last changes fastest.
Arguments:
- layer_input: bfloat16 [4, 2048, 2048], P('dp', 'fsdp'), may hold values from -6 to 6
- doc_starts: int32 [4, 6], P('dp'), may hold values from 0 to 2047, as said below
- norm1_gain: bfloat16 [2048], P(('dp', 'fsdp')), may hold values from 0.099609375 to 1.8984375
- w_query: bfloat16 [2048, 256], P(('dp', 'fsdp')), may hold values from -0.125 to 0.125
- w_key: bfloat16 [2048, 256], P(('dp', 'fsdp')), may hold values from -0.125 to 0.125
- w_value: bfloat16 [2048, 2048], P(('dp', 'fsdp')), may hold values from -0.125 to 0.125
- w_out: bfloat16 [2048, 2048], P(('dp', 'fsdp')), may hold values from -1 to 1
- norm2_gain: bfloat16 [2048], P(('dp', 'fsdp')), may hold values from 0.099609375 to 1.8984375
- w_gate: bfloat16 [2048, 5504], P(('dp', 'fsdp')), may hold values from -0.125 to 0.125
- w_up: bfloat16 [2048, 5504], P(('dp', 'fsdp')), may hold values from -0.125 to 0.125
- w_down: bfloat16 [5504, 2048], P(None, ('dp', 'fsdp')), may hold values from -0.078125 to 0.078125
- cotangent: bfloat16 [4, 2048, 2048], P('dp', 'fsdp'), may hold values from -6 to 6
Outputs:
- out_act: bfloat16 [4, 2048, 2048], P('dp', 'fsdp')
- grad_input: float32 [4, 2048, 2048], P('dp', 'fsdp')
- grad_norm1: float32 [2048], P(('dp', 'fsdp'))
- grad_query: float32 [2048, 256], P(('dp', 'fsdp'))
- grad_key: float32 [2048, 256], P(('dp', 'fsdp'))
- grad_value: float32 [2048, 2048], P(('dp', 'fsdp'))
- grad_out: float32 [2048, 2048], P(('dp', 'fsdp'))
- grad_norm2: float32 [2048], P(('dp', 'fsdp'))
- grad_gate: float32 [2048, 5504], P(('dp', 'fsdp'))
- grad_up: float32 [2048, 5504], P(('dp', 'fsdp'))
- grad_down: float32 [5504, 2048], P(None, ('dp', 'fsdp'))
Inputs may be any that keep to these rules, and one draw needn't show every extreme that they name: `doc_starts`: in each row the six starts rise strictly from 0; the second and third are below 256, the last three are 1793 or more, so that one document runs from the row's first device to its last.
All inputs are finite; a program needn't handle non-finite values.
Results may differ from a plain program's by a relative error of at most 0.012.
Values may be sent and summed in bfloat16 or wider, within the bound.
A program may use at most 312 MiB of HBM per device.

v0:
```python
import math

import jax
import jax.numpy as jnp
from jax import lax
from jax.sharding import PartitionSpec as P

FEAT = 16


EPS = 1e-05
HIGH = lax.Precision.HIGHEST
FIRST_DIMS = (((0,), (0,)), ((), ()))
LAST_DIMS = (((1,), (1,)), ((), ()))


def prefix(shard, axis, combine, identity):
    peers, here = (lax.axis_size(axis), lax.axis_index(axis))
    everything = jax.tree.map(lambda part: lax.all_gather(part, axis), shard)
    start = jax.tree.map(
        lambda part, zero: jnp.broadcast_to(jnp.asarray(zero, part.dtype), part.shape),
        shard,
        identity,
    )

    def lap(k, before):
        reached = k < here
        new = combine(before, jax.tree.map(lambda part: part[k], everything))
        return jax.tree.map(lambda a, b: jnp.where(reached, a, b), new, before)

    return lax.fori_loop(0, peers, lap, start)


def prefix_2(shard, axis, join, neutral):
    count = lax.axis_size(axis)
    place = lax.axis_index(axis)
    ahead = count - 1 - place
    gathered = jax.tree.map(
        lambda a, kind: lax.all_gather(a.astype(kind), axis),
        shard,
        jax.tree.map(lambda a: jnp.bfloat16 if a.dtype == jnp.float32 else a.dtype, shard),
    )
    state = jax.tree.map(lambda a, e: jnp.zeros_like(a) + jnp.asarray(e, a.dtype), shard, neutral)

    def one(lap, state):
        source = count - 1 - lap
        return join(
            state,
            jax.tree.map(
                lambda a, own: lax.dynamic_index_in_dim(a, source, 0, False).astype(own.dtype),
                gathered,
                shard,
            ),
        )

    return lax.fori_loop(0, ahead, one, state)


def rms_apply(values, gain):
    factor = lax.rsqrt(jnp.mean(values * values, -1, keepdims=True) + EPS)
    return (values * factor * gain, factor)


def rms_back(grad, values, factor, gain):
    normed = values * factor
    grad_gain = jnp.sum(grad * normed, 0)
    inner = grad * gain
    grad_in = factor * (inner - normed * jnp.mean(inner * normed, -1, keepdims=True))
    return (grad_in, grad_gain)


def taylor_parts(flat):
    tokens = flat.shape[0]
    heads = flat.shape[1] // FEAT
    per_head = jnp.transpose(flat.reshape(tokens, heads, FEAT), (1, 0, 2))
    linear = per_head / FEAT**0.25
    square = (per_head[..., :, None] * per_head[..., None, :]).reshape(heads, tokens, FEAT * FEAT)
    return (linear, square / math.sqrt(2.0 * FEAT))


def combine(earlier, later):
    keep_late = later[-1]
    joined = tuple((late + keep_late * early for early, late in zip(earlier[:-1], later[:-1])))
    return joined + (earlier[-1] * keep_late,)


def contract_low(form, left, right):
    return jnp.einsum(form, left, right, preferred_element_type=jnp.float32)


def contract_high(form, left, right):
    return jnp.einsum(form, left, right, precision=HIGH, preferred_element_type=jnp.float32)


def reduce_mlp(terms):
    return (
        lax.psum_scatter(terms[0], ("dp", "fsdp"), scatter_dimension=0, tiled=True),
        lax.psum_scatter(terms[1], ("dp", "fsdp"), scatter_dimension=0, tiled=True),
        lax.psum_scatter(terms[2], ("dp", "fsdp"), scatter_dimension=0, tiled=True),
    )


def reduce_attn(terms):
    return (
        lax.psum_scatter(terms[0], ("dp", "fsdp"), scatter_dimension=0, tiled=True),
        lax.psum_scatter(terms[1], ("dp", "fsdp"), scatter_dimension=0, tiled=True),
        lax.psum_scatter(terms[2], ("dp", "fsdp"), scatter_dimension=0, tiled=True),
        lax.psum_scatter(terms[3], ("dp", "fsdp"), scatter_dimension=0, tiled=True),
        lax.psum_scatter(terms[4], ("dp", "fsdp"), scatter_dimension=0, tiled=True),
    )


def on_device(
    layer_input,
    doc_starts,
    norm1_gain,
    w_query,
    w_key,
    w_value,
    w_out,
    norm2_gain,
    w_gate,
    w_up,
    w_down,
    cotangent,
):
    gain_one, query_full, key_full, value_full, out_full = (
        lax.all_gather(norm1_gain, ("dp", "fsdp"), axis=0, tiled=True),
        lax.all_gather(w_query, ("dp", "fsdp"), axis=0, tiled=True),
        lax.all_gather(w_key, ("dp", "fsdp"), axis=0, tiled=True),
        lax.all_gather(w_value, ("dp", "fsdp"), axis=0, tiled=True),
        lax.all_gather(w_out, ("dp", "fsdp"), axis=0, tiled=True),
    )
    gain_two, gate_full, up_full, down_full = (
        lax.all_gather(norm2_gain, ("dp", "fsdp"), axis=0, tiled=True),
        lax.all_gather(w_gate, ("dp", "fsdp"), axis=0, tiled=True),
        lax.all_gather(w_up, ("dp", "fsdp"), axis=0, tiled=True),
        lax.all_gather(w_down, ("dp", "fsdp"), axis=1, tiled=True),
    )
    inputs = layer_input[0].astype(jnp.float32)
    tokens, width = inputs.shape
    heads = query_full.shape[1] // FEAT
    head_width = width // heads
    block_start = lax.axis_index("fsdp") * tokens
    local_places = jnp.arange(tokens, dtype=jnp.int32)
    position = block_start + local_places
    starts = doc_starts[0]
    segment = jnp.sum((starts[None, :] <= position[:, None]).astype(jnp.int32), 1)
    seg_before = jnp.sum((starts <= block_start - 1).astype(jnp.int32))
    seg_final = segment[tokens - 1]
    reach_in = (segment == seg_before).astype(jnp.float32)
    reach_out = (segment == seg_final).astype(jnp.float32)
    keep_flag = (seg_final == seg_before).astype(jnp.float32)
    local_mask = (
        (segment[:, None] == segment[None, :]) & (local_places[None, :] <= local_places[:, None])
    ).astype(jnp.float32)
    normed_one, factor_one = rms_apply(inputs, gain_one.astype(jnp.float32))
    act_one = normed_one.astype(jnp.bfloat16)
    queries = jnp.dot(act_one, query_full, preferred_element_type=jnp.float32)
    keys_proj = jnp.dot(act_one, key_full, preferred_element_type=jnp.float32)
    q_lin, q_sq = taylor_parts(queries)
    k_lin, k_sq = taylor_parts(keys_proj)
    q_lin_low, q_sq_low = (q_lin.astype(jnp.bfloat16), q_sq.astype(jnp.bfloat16))
    k_lin_low, k_sq_low = (k_lin.astype(jnp.bfloat16), k_sq.astype(jnp.bfloat16))
    q_lin_f, q_sq_f = (q_lin_low.astype(jnp.float32), q_sq_low.astype(jnp.float32))
    k_lin_f, k_sq_f = (k_lin_low.astype(jnp.float32), k_sq_low.astype(jnp.float32))
    values = jnp.dot(act_one, value_full, preferred_element_type=jnp.float32).astype(jnp.bfloat16)
    value_heads = jnp.transpose(values.reshape(tokens, heads, head_width), (1, 0, 2))
    value_f = value_heads.astype(jnp.float32)
    scores = (
        1.0
        + contract_low("htf,hsf->hts", q_lin_low, k_lin_low)
        + contract_low("htg,hsg->hts", q_sq_low, k_sq_low)
    )
    weights = scores * local_mask[None]
    out_gate = reach_out[None, :, None]
    in_gate = reach_in[None, :, None]
    out_low = out_gate.astype(jnp.bfloat16)
    k_lin_out = k_lin_low * out_low
    k_sq_out = k_sq_low * out_low
    sum_vals = jnp.sum(value_f * out_gate, 1)
    sum_lin = contract_low("hsf,hsc->hfc", k_lin_out, value_heads)
    sum_sq = contract_low("hsg,hsc->hgc", k_sq_out, value_heads)
    count_keys = jnp.sum(reach_out) * jnp.ones((heads,), jnp.float32)
    norm_lin = jnp.sum(k_lin_out.astype(jnp.float32), 1)
    norm_sq = jnp.sum(k_sq_out.astype(jnp.float32), 1)
    sent = (sum_vals, sum_lin, sum_sq, count_keys, norm_lin, norm_sq, keep_flag)
    neutral = tuple((jnp.zeros_like(t) for t in sent[:-1])) + (jnp.ones((), jnp.float32),)
    arriving = prefix(sent, "fsdp", combine, neutral)
    in_vals, in_lin, in_sq, in_count, in_norm_lin, in_norm_sq = arriving[:6]
    numer = contract_high("hts,hsc->htc", weights, value_f) + in_gate * (
        in_vals[:, None, :]
        + contract_high("htf,hfc->htc", q_lin_f, in_lin)
        + contract_high("htg,hgc->htc", q_sq_f, in_sq)
    )
    denom = jnp.sum(weights, -1) + reach_in[None, :] * (
        in_count[:, None]
        + contract_high("htf,hf->ht", q_lin_f, in_norm_lin)
        + contract_high("htg,hg->ht", q_sq_f, in_norm_sq)
    )
    attended = numer / denom[..., None]
    mixed_heads = jnp.transpose(attended, (1, 0, 2)).reshape(tokens, width).astype(jnp.bfloat16)
    residual = inputs + jnp.dot(mixed_heads, out_full, preferred_element_type=jnp.float32)
    normed_two, factor_two = rms_apply(residual, gain_two.astype(jnp.float32))
    act_two = normed_two.astype(jnp.bfloat16)
    gate_pre = jnp.dot(act_two, gate_full, preferred_element_type=jnp.float32)
    upward = jnp.dot(act_two, up_full, preferred_element_type=jnp.float32)
    sigma = jax.nn.sigmoid(gate_pre)
    swish = gate_pre * sigma
    hidden = (swish * upward).astype(jnp.bfloat16)
    result = residual + jnp.dot(hidden, down_full, preferred_element_type=jnp.float32)
    output = result.astype(jnp.bfloat16)[None]
    gain_two, gate_full, up_full, down_full = (
        lax.all_gather(norm2_gain, ("dp", "fsdp"), axis=0, tiled=True),
        lax.all_gather(w_gate, ("dp", "fsdp"), axis=0, tiled=True),
        lax.all_gather(w_up, ("dp", "fsdp"), axis=0, tiled=True),
        lax.all_gather(w_down, ("dp", "fsdp"), axis=1, tiled=True),
    )
    gain_one, query_full, key_full, value_full, out_full = (
        lax.all_gather(norm1_gain, ("dp", "fsdp"), axis=0, tiled=True),
        lax.all_gather(w_query, ("dp", "fsdp"), axis=0, tiled=True),
        lax.all_gather(w_key, ("dp", "fsdp"), axis=0, tiled=True),
        lax.all_gather(w_value, ("dp", "fsdp"), axis=0, tiled=True),
        lax.all_gather(w_out, ("dp", "fsdp"), axis=0, tiled=True),
    )
    grad_top = cotangent[0]
    grad_top_f = grad_top.astype(jnp.float32)
    down_rows = lax.psum_scatter(
        lax.dot_general(grad_top, hidden, FIRST_DIMS, preferred_element_type=jnp.float32),
        ("dp", "fsdp"),
        scatter_dimension=0,
        tiled=True,
    )
    grad_down = down_rows.T
    grad_hidden = lax.dot_general(
        grad_top, down_full, LAST_DIMS, preferred_element_type=jnp.float32
    )
    grad_gate_pre = (grad_hidden * upward * sigma * (1.0 + gate_pre * (1.0 - sigma))).astype(
        jnp.bfloat16
    )
    grad_upward = (grad_hidden * swish).astype(jnp.bfloat16)
    gate_term = lax.dot_general(
        act_two, grad_gate_pre, FIRST_DIMS, preferred_element_type=jnp.float32
    )
    up_term = lax.dot_general(act_two, grad_upward, FIRST_DIMS, preferred_element_type=jnp.float32)
    grad_act_two = lax.dot_general(
        grad_gate_pre, gate_full, LAST_DIMS, preferred_element_type=jnp.float32
    ) + lax.dot_general(grad_upward, up_full, LAST_DIMS, preferred_element_type=jnp.float32)
    grad_resid_norm, gain_two_term = rms_back(
        grad_act_two, residual, factor_two, gain_two.astype(jnp.float32)
    )
    grad_resid = grad_top_f + grad_resid_norm
    gain_two_part, gate_part, up_part = reduce_mlp((gain_two_term, gate_term, up_term))
    grad_proj = grad_resid.astype(jnp.bfloat16)
    out_term = lax.dot_general(
        mixed_heads, grad_proj, FIRST_DIMS, preferred_element_type=jnp.float32
    )
    grad_mixed = lax.dot_general(
        grad_proj, out_full, LAST_DIMS, preferred_element_type=jnp.float32
    ).astype(jnp.bfloat16)
    grad_heads = jnp.transpose(
        grad_mixed.astype(jnp.float32).reshape(tokens, heads, head_width), (1, 0, 2)
    )
    grad_numer = grad_heads / denom[..., None]
    grad_denom = -jnp.sum(grad_heads * attended, -1) / denom
    q_lin_in = q_lin_f * in_gate
    q_sq_in = q_sq_f * in_gate
    grad_sent = (
        jnp.sum(grad_numer * in_gate, 1),
        contract_high("htf,htc->hfc", q_lin_in, grad_numer),
        contract_high("htg,htc->hgc", q_sq_in, grad_numer),
        jnp.sum(grad_denom * reach_in[None, :], 1),
        contract_high("htf,ht->hf", q_lin_in, grad_denom),
        contract_high("htg,ht->hg", q_sq_in, grad_denom),
        keep_flag,
    )
    leaving = prefix_2(grad_sent, "fsdp", combine, neutral)
    back_vals, back_lin, back_sq, back_count, back_norm_lin, back_norm_sq = leaving[:6]
    grad_weights = local_mask[None] * (
        contract_high("htc,hsc->hts", grad_numer, value_f) + grad_denom[..., None]
    )
    grad_value_heads = contract_high("hts,htc->hsc", weights, grad_numer) + out_gate * (
        back_vals[:, None, :]
        + contract_high("hsf,hfc->hsc", k_lin_f, back_lin)
        + contract_high("hsg,hgc->hsc", k_sq_f, back_sq)
    )
    grad_k_lin = contract_high("hts,htf->hsf", grad_weights, q_lin_f) + out_gate * (
        contract_high("hfc,hsc->hsf", back_lin, value_f) + back_norm_lin[:, None, :]
    )
    grad_k_sq = contract_high("hts,htg->hsg", grad_weights, q_sq_f) + out_gate * (
        contract_high("hgc,hsc->hsg", back_sq, value_f) + back_norm_sq[:, None, :]
    )
    grad_q_lin = contract_high("hts,hsf->htf", grad_weights, k_lin_f) + in_gate * (
        contract_high("hfc,htc->htf", in_lin, grad_numer)
        + grad_denom[..., None] * in_norm_lin[:, None, :]
    )
    grad_q_sq = contract_high("hts,hsg->htg", grad_weights, k_sq_f) + in_gate * (
        contract_high("hgc,htc->htg", in_sq, grad_numer)
        + grad_denom[..., None] * in_norm_sq[:, None, :]
    )
    _, query_pull = jax.vjp(taylor_parts, queries)
    grad_queries = query_pull((grad_q_lin, grad_q_sq))[0].astype(jnp.bfloat16)
    _, key_pull = jax.vjp(taylor_parts, keys_proj)
    grad_keys = key_pull((grad_k_lin, grad_k_sq))[0].astype(jnp.bfloat16)
    grad_values = (
        jnp.transpose(grad_value_heads, (1, 0, 2)).reshape(tokens, width).astype(jnp.bfloat16)
    )
    query_term = lax.dot_general(
        act_one, grad_queries, FIRST_DIMS, preferred_element_type=jnp.float32
    )
    key_term = lax.dot_general(act_one, grad_keys, FIRST_DIMS, preferred_element_type=jnp.float32)
    value_term = lax.dot_general(
        act_one, grad_values, FIRST_DIMS, preferred_element_type=jnp.float32
    )
    grad_act_one = lax.dot_general(
        grad_queries, query_full, LAST_DIMS, preferred_element_type=jnp.float32
    )
    grad_act_one = grad_act_one + lax.dot_general(
        grad_keys, key_full, LAST_DIMS, preferred_element_type=jnp.float32
    )
    grad_act_one = grad_act_one + lax.dot_general(
        grad_values, value_full, LAST_DIMS, preferred_element_type=jnp.float32
    )
    grad_in_norm, gain_one_term = rms_back(
        grad_act_one, inputs, factor_one, gain_one.astype(jnp.float32)
    )
    grad_input = (grad_resid + grad_in_norm)[None]
    gain_one_part, query_part, key_part, value_part, out_part = reduce_attn(
        (gain_one_term, query_term, key_term, value_term, out_term)
    )
    return (
        output,
        grad_input,
        gain_one_part,
        query_part,
        key_part,
        value_part,
        out_part,
        gain_two_part,
        gate_part,
        up_part,
        grad_down,
    )


def solution(mesh):
    return jax.shard_map(
        on_device,
        mesh=mesh,
        in_specs=(
            P("dp", "fsdp", None),
            P("dp", None),
            P(("dp", "fsdp")),
            P(("dp", "fsdp"), None),
            P(("dp", "fsdp"), None),
            P(("dp", "fsdp"), None),
            P(("dp", "fsdp"), None),
            P(("dp", "fsdp")),
            P(("dp", "fsdp"), None),
            P(("dp", "fsdp"), None),
            P(None, ("dp", "fsdp")),
            P("dp", "fsdp", None),
        ),
        out_specs=(
            P("dp", "fsdp", None),
            P("dp", "fsdp", None),
            P(("dp", "fsdp")),
            P(("dp", "fsdp"), None),
            P(("dp", "fsdp"), None),
            P(("dp", "fsdp"), None),
            P(("dp", "fsdp"), None),
            P(("dp", "fsdp")),
            P(("dp", "fsdp"), None),
            P(("dp", "fsdp"), None),
            P(None, ("dp", "fsdp")),
        ),
        check_vma=False,
    )
```

profile of v0, /device:TPU:0, one launch (start us, length us, event | category | flops | bytes accessed | tf_op | source)
XLA Modules:
  0.0 3079.1 jit_solution(10961607278426447977)
XLA Ops:
  11.9 42.1 %all-reduce.9 = (bf16[2048]{0:T(1024)(128)(2,1)S(1)}, bf16[2048]{0:T(1024)(128)(2,1)}) all-reduce(bf16[2048]{0:T(1024)(128)(2,1)S(1)} %dynamic-update-slice, bf16[2048]{0:T(1024)(128)(2,1)S(1)} %dynamic-update-slice.3), channel_id=1, replica_groups=mesh['dp'=4,'fsdp'=8] {'dp','fsdp'}, use_global_device_ids=true, to_apply=%add | all-reduce | flops 4096 | bytes 16384
  59.3 7.9 all-gather.22.cloned.1.call-done
  70.0 76.6 %all-gather.24.cloned.1.call-done = bf16[2048,2048]{1,0:T(8,128)(2,1)} async-done(((bf16[64,2048]{1,0:T(8,128)(2,1)}), bf16[2048,2048]{1,0:T(8,128)(2,1)}) %all-gather.24.cloned.1.call-update) | async-done | bytes 8388624 | tf_op jit(solution)/shard_map/all_gather | solution.py:131
  146.6 5.8 convolution_convert_fusion.1
  166.5 14.0 all-reduce.8
  182.0 19.8 all-gather.20.cloned.1.call-done
  205.7 10.1 all-gather.3
  215.8 10.3 all_gather.131
  233.3 9.8 all-gather
  243.2 3.0 fusion.105
  246.2 72.3 %all-gather.36.cloned.1.call-done = f32[128,256,128]{2,1,0:T(8,128)} async-done(((f32[16,256,128]{2,1,0:T(8,128)}), f32[128,256,128]{2,1,0:T(8,128)}) %all-gather.36.cloned.1.call-update) | async-done | bytes 16777232 | tf_op jit(solution)/shard_map/all_gather | solution.py:19
  319.8 104.5 %while.48 = (s32[]{:T(128)}, f32[16,128]{1,0:T(8,128)}, f32[16,16,128]{2,1,0:T(8,128)S(1)}, f32[16,256,128]{2,1,0:T(8,128)S(1)}, f32[16]{0:T(128)}, /*index=5*/f...) while((s32[]{:T(128)}, f32[16,128]{1,0:T(8,128)}, ...), condition=%wide.region_8.9_spmd.clone, body=%wide.region_7.8_spmd.clone.sunk | while | flops 2253892 | bytes 6770735 | solution.py:31
  325.0 4.1 fusion.186
  338.0 4.1 fusion.186
  351.0 4.1 fusion.186
  364.0 4.1 fusion.186
  377.1 4.1 fusion.186
  390.1 4.1 fusion.186
  403.1 4.1 fusion.186
  416.1 4.1 fusion.186
  425.6 2.7 fusion.89
  429.4 4.1 fusion.35
  433.6 6.2 multiply_reduce_fusion.8
  442.3 99.9 %all-gather.28.cloned.1.call-done = bf16[2048,5504]{1,0:T(8,128)(2,1)} async-done(((bf16[64,5504]{1,0:T(8,128)(2,1)}), bf16[2048,5504]{1,0:T(8,128)(2,1)}) %all-gather.28.cloned.1.call-update) | async-done | bytes 22544400 | tf_op jit(solution)/shard_map/all_gather | solution.py:136
  542.2 12.5 fusion.108
  554.7 130.6 %all-gather.30.cloned.1.call-done = bf16[2048,5504]{1,0:T(8,128)(2,1)} async-done(((bf16[64,5504]{1,0:T(8,128)(2,1)}), bf16[2048,5504]{1,0:T(8,128)(2,1)}) %all-gather.30.cloned.1.call-update) | async-done | bytes 22544400 | tf_op jit(solution)/shard_map/all_gather | solution.py:137
  685.3 12.6 fusion.109
  697.9 130.5 %all-gather.32.cloned.1.call-done = bf16[5504,2048]{0,1:T(8,128)(2,1)} async-done(((bf16[5504,64]{0,1:T(8,128)(2,1)}), bf16[5504,2048]{0,1:T(8,128)(2,1)}) %all-gather.32.cloned.1.call-update) | async-done | bytes 22544400 | tf_op jit(solution)/shard_map/all_gather | solution.py:138
  828.4 16.3 multiply_convert_fusion
  844.7 13.0 fusion.110
  857.7 14.6 multiply_reduce_fusion.4
  873.0 3.1 multiply_add_fusion
  877.4 7.0 fusion.23
  884.4 2.9 copy.118
  887.3 7.3 fusion.48
  897.1 14.1 all-reduce.4
  911.2 3.7 multiply_reduce_fusion.6
  915.4 3.9 fusion.8
  919.2 10.0 all-gather.7
  929.2 9.3 all-gather.4
  938.5 10.1 all-gather.8
  950.4 10.1 all-gather.5
  963.9 3.7 fusion.100
  967.6 3.4 add_multiply_fusion.1
  977.6 6.7 fusion.12
  985.9 53.6 %while.47 = (s32[]{:T(128)}, f32[16,128]{1,0:T(8,128)}, f32[16,16,128]{2,1,0:T(8,128)S(1)}, f32[16,256,128]{2,1,0:T(8,128)S(1)}, f32[16,16]{1,0:T(8,128)}, /*ind...) while((s32[]{:T(128)}, f32[16,128]{1,0:T(8,128)}, ...), condition=%wide.region_17.18_spmd, body=%wide.region_16.17_spmd.sunk | while | flops 1690375 | bytes 5643073 | solution.py:56
  1041.3 4.2 add_multiply_fusion
  1052.7 10.2 fusion.76
  1063.6 7.5 fusion.99
  1076.1 8.4 fusion.69
  1085.6 19.4 fusion.114
  1105.1 19.4 fusion.115
  1125.7 19.3 convolution_bitcast_fusion
  1145.0 44.0 %copy.167 = f32[2048,5504]{1,0:T(8,128)} copy(f32[2048,5504]{0,1:T(8,128)} %convolution_bitcast_fusion) | data formatting | bytes 90177536
  1189.9 3.0 fusion.111
  1192.9 12.2 fusion.24
  1205.2 6.3 fusion.113
  1213.8 38.4 %all-reduce.7 = (f32[2048]{0:T(1024)S(1)}, f32[2048]{0:T(1024)S(1)}) all-reduce(f32[2048]{0:T(1024)S(1)} %get-tuple-element.573, f32[2048]{0:T(1024)S(1)} %copy-done.75), channel_id=12, replica_groups=mesh['dp'=4,'fsdp'=8] {'dp','fsdp'}, use_global_device_ids=true, to_apply=%region_22.23.clone | all-reduce | flops 4096 | bytes 32768
  1253.4 3.5 fusion.30
  1256.9 179.7 %reduce-scatter.16.cloned.1.call-done = f32[64,2048]{1,0:T(8,128)} async-done(((f32[2048,2048]{1,0:T(8,128)}), f32[64,2048]{1,0:T(8,128)}) %reduce-scatter.16.cloned.1.call-update) | async-done | bytes 524304 | tf_op jit(solution)/shard_map/reduce_scatter | solution.py:109
  1436.6 187.9 %reduce-scatter.14.cloned.1.call-done = f32[64,2048]{1,0:T(8,128)} async-done(((f32[2048,2048]{1,0:T(8,128)}), f32[64,2048]{1,0:T(8,128)}) %reduce-scatter.14.cloned.1.call-update) | async-done | bytes 524304 | tf_op jit(solution)/shard_map/reduce_scatter | solution.py:108
  1624.5 478.0 %reduce-scatter.18.cloned.1.call-done = f32[64,5504]{1,0:T(8,128)} async-done(((f32[2048,5504]{1,0:T(8,128)}), f32[64,5504]{1,0:T(8,128)}) %reduce-scatter.18.cloned.1.call-update) | async-done | bytes 1409040 | tf_op jit(solution)/shard_map/reduce_scatter | solution.py:98
  2102.5 485.0 %reduce-scatter.20.cloned.1.call-done = f32[64,5504]{1,0:T(8,128)} async-done(((f32[2048,5504]{1,0:T(8,128)}), f32[64,5504]{1,0:T(8,128)}) %reduce-scatter.20.cloned.1.call-update) | async-done | bytes 1409040 | tf_op jit(solution)/shard_map/reduce_scatter | solution.py:99
  2587.5 484.9 %reduce-scatter.22.cloned.1.call-done = f32[64,5504]{1,0:T(8,128)} async-done(((f32[2048,5504]{1,0:T(8,128)}), f32[64,5504]{1,0:T(8,128)}) %reduce-scatter.22.cloned.1.call-update) | async-done | bytes 1409040
  (443 shorter events, 202.9 us)
Async XLA Ops:
  7.2 61.6 %copy-start.2 = (bf16[1,256,2048]{2,1,0:T(8,128)(2,1)S(1)}, bf16[1,256,2048]{2,1,0:T(8,128)(2,1)}, u32[]{:S(2)}) copy-start(bf16[1,256,2048]{2,1,0:T(8,128)(2,1)} %param.16) | copy-start | bytes 3145732
  7.2 60.1 %all-gather.22.cloned.1.call-start = ((), (), s32[]{:S(2)}) async-start(), calls=%async_computation.8 | async-start | bytes 1081344 | tf_op jit(solution)/shard_map/all_gather | solution.py:130
  7.9 138.7 %all-gather.24.cloned.1.call-start = ((), (), s32[]{:S(2)}) async-start(), calls=%async_computation.9 | async-start | bytes 8650752 | tf_op jit(solution)/shard_map/all_gather | solution.py:131
  8.7 193.1 %all-gather.20.cloned.1.call-start = ((), (), s32[]{:S(2)}) async-start(), calls=%async_computation.7 | async-start | bytes 1081344 | tf_op jit(solution)/shard_map/all_gather | solution.py:129
  9.4 236.8 %all-gather.34.cloned.1.call-start = ((), (), s32[]{:S(2)}) async-start(), calls=%async_computation.20 | async-start | bytes 1179648 | tf_op jit(solution)/shard_map/all_gather | solution.py:19
  10.2 57.1 %copy-start.71 = (s32[256]{0:T(256)}, s32[256]{0:T(256)S(1)}, u32[]{:S(2)}) copy-start(s32[256]{0:T(256)S(1)} %convert_reduce_fusion.2) | copy-start | bytes 3076
  54.1 92.6 %copy-start.50 = (f32[2048]{0:T(1024)}, f32[2048]{0:T(1024)S(1)}, u32[]{:S(2)}) copy-start(f32[2048]{0:T(1024)S(1)} %convert_element_type.263) | copy-start | bytes 24580
  57.5 89.2 %copy-start.62 = (f32[256]{0:T(256)}, f32[256]{0:T(256)S(1)}, u32[]{:S(2)}) copy-start(f32[256]{0:T(256)S(1)} %add_rsqrt_fusion.1) | copy-start | bytes 3076
  59.3 10.7 copy-start.76
  59.3 104.4 %copy-start.65 = (f32[256]{0:T(256)}, f32[256]{0:T(256)S(1)}, u32[]{:S(2)}) copy-start(f32[256]{0:T(256)S(1)} %get-tuple-element.646) | copy-start | bytes 3076
  70.0 82.9 %copy-start.32 = (bf16[16,256,16]{1,2,0:T(8,128)(2,1)}, bf16[16,256,16]{1,2,0:T(8,128)(2,1)S(1)}, u32[]{:S(2)}) copy-start(bf16[16,256,16]{1,2,0:T(8,128)(2,1)S(1)} %get-tuple-element.644) | copy-start | bytes 393220
  70.0 84.2 %copy-start.26 = (f32[16,256,16]{1,2,0:T(8,128)}, f32[16,256,16]{1,2,0:T(8,128)S(1)}, u32[]{:S(2)}) copy-start(f32[16,256,16]{1,2,0:T(8,128)S(1)} %get-tuple-element.655) | copy-start | bytes 786436
  154.1 164.4 %all-gather.36.cloned.1.call-start = ((), (), s32[]{:S(2)}) async-start(), calls=%async_computation.21 | async-start | bytes 18874368 | tf_op jit(solution)/shard_map/all_gather | solution.py:19
  159.0 4.2 copy-start.79
  159.0 21.5 copy-start.78
  159.0 274.6 %all-gather.26.cloned.1.call-start = ((), (), s32[]{:S(2)}) async-start(), calls=%async_computation.10 | async-start | bytes 8650752 | tf_op jit(solution)/shard_map/all_gather | solution.py:132
  159.6 382.6 %all-gather.28.cloned.1.call-start = ((), (), s32[]{:S(2)}) async-start(), calls=%async_computation.11 | async-start | bytes 23248896 | tf_op jit(solution)/shard_map/all_gather | solution.py:136
  160.3 525.0 %all-gather.30.cloned.1.call-start = ((), (), s32[]{:S(2)}) async-start(), calls=%async_computation.12 | async-start | bytes 23248896 | tf_op jit(solution)/shard_map/all_gather | solution.py:137
  161.1 667.3 %all-gather.32.cloned.1.call-start = ((), (), s32[]{:S(2)}) async-start(), calls=%async_computation.13 | async-start | bytes 23248896 | tf_op jit(solution)/shard_map/all_gather | solution.py:138
  161.8 822.7 %all-gather.38.cloned.1.call-start = ((), (), s32[]{:S(2)}) async-start(), calls=%async_computation.22 | async-start | bytes 9437184 | tf_op jit(solution)/shard_map/all_gather | solution.py:39
  233.0 10.2 copy-start.12
  325.0 4.1 copy-start.68
  325.0 5.5 copy-start.56
  338.0 4.1 copy-start.68
  338.0 5.5 copy-start.56
  351.0 4.1 copy-start.68
  351.0 5.5 copy-start.56
  364.0 4.1 copy-start.68
  364.0 5.5 copy-start.56
  377.1 4.1 copy-start.68
  377.1 5.5 copy-start.56
  390.1 4.1 copy-start.68
  390.1 5.5 copy-start.56
  403.1 4.1 copy-start.68
  403.1 5.5 copy-start.56
  416.1 4.1 copy-start.68
  416.1 5.5 copy-start.56
  424.3 3.9 copy-start.61
  424.4 3.9 copy-start.70
  424.4 3.9 copy-start.72
  424.4 4.0 copy-start.37
  425.6 3.9 copy-start.14
  425.6 3.9 copy-start.31
  433.6 7.5 copy-start.60
  844.7 13.0 copy-start.30
  894.6 362.3 %reduce-scatter.10.cloned.1.call-start = ((), (), s32[]{:S(2)}) async-start(), calls=%async_computation.14 | async-start | bytes 2162688 | tf_op jit(solution)/shard_map/reduce_scatter | solution.py:106
  911.2 4.1 copy-start.15
  914.9 33.7 %copy-start.3 = (f32[256,2048]{0,1:T(8,128)S(1)}, f32[256,2048]{0,1:T(8,128)}, u32[]{:S(2)}) copy-start(f32[256,2048]{0,1:T(8,128)} %copy.118) | copy-start | bytes 6291460
  915.0 58.3 %copy-start.47 = (f32[16,256]{1,0:T(8,128)}, f32[16,256]{1,0:T(8,128)S(1)}, u32[]{:S(2)}) copy-start(f32[16,256]{1,0:T(8,128)S(1)} %negate_divide_fusion) | copy-start | bytes 49156
  948.6 11.9 copy-start.58
  963.9 9.4 copy-start
  984.4 272.5 %reduce-scatter.12.cloned.1.call-start = ((), (), s32[]{:S(2)}) async-start(), calls=%async_computation.15 | async-start | bytes 2162688 | tf_op jit(solution)/shard_map/reduce_scatter | solution.py:107
  1041.3 4.2 copy-start.27
  1052.7 383.9 %reduce-scatter.16.cloned.1.call-start = ((), (), s32[]{:S(2)}) async-start(), calls=%async_computation.17 | async-start | bytes 17301504 | tf_op jit(solution)/shard_map/reduce_scatter | solution.py:109
  1063.0 8.2 copy-start.35
  1063.0 561.5 %reduce-scatter.14.cloned.1.call-start = ((), (), s32[]{:S(2)}) async-start(), calls=%async_computation.16 | async-start | bytes 17301504 | tf_op jit(solution)/shard_map/reduce_scatter | solution.py:108
  1084.4 1018.1 %reduce-scatter.18.cloned.1.call-start = ((), (), s32[]{:S(2)}) async-start(), calls=%async_computation.18 | async-start | bytes 46497792 | tf_op jit(solution)/shard_map/reduce_scatter | solution.py:98
  1105.0 1482.4 %reduce-scatter.20.cloned.1.call-start = ((), (), s32[]{:S(2)}) async-start(), calls=%async_computation.19 | async-start | bytes 46497792 | tf_op jit(solution)/shard_map/reduce_scatter | solution.py:99
  1124.5 1947.8 %reduce-scatter.22.cloned.1.call-start = ((), (), s32[]{:S(2)}) async-start(), calls=%async_computation.23 | async-start | bytes 46497792
  1189.0 3.9 copy-start.20
  1205.2 6.3 copy-start.22
  1205.2 6.3 copy-start.25
  1205.2 6.3 copy-start.41
  1211.5 41.9 %copy-start.18 = (f32[256,2048]{1,0:T(8,128)S(1)}, f32[256,2048]{1,0:T(8,128)}, u32[]{:S(2)}) copy-start(f32[256,2048]{1,0:T(8,128)} %copy-done.17) | copy-start | bytes 6291460
  (73 other events, 138.1 us)
Sparse Core Ops, SparseCore 0:
  10.9 56.3 all-gather.21
  70.1 76.4 all-gather.23
  149.5 52.2 all-gather.19
  204.1 22.8 all-gather.33
  228.7 89.6 all-gather.35
  321.2 77.4 all-gather.25
  401.5 140.6 all-gather.27
  545.0 140.1 all-gather.29
  688.2 140.1 all-gather.31
  894.8 52.8 all-gather.37
  984.5 134.7 reduce-scatter.9
  1122.1 132.7 reduce-scatter.11
  1257.8 178.7 reduce-scatter.15
  1439.3 185.0 reduce-scatter.13
  1627.2 475.2 reduce-scatter.17
  2105.2 482.1 reduce-scatter.19
  2590.2 482.0 reduce-scatter.21
where the time goes:
time: 3100 us; the launch traced here: 3080 us
  waiting for transfers between devices  2360 us (76%)
  matrix products  264 us (9%)
  blocking collectives  178 us (6%)
  other arithmetic  160 us (5%)
  local copies, waits for them, and re-layouts  94.5 us (3%)
    unnamed x18, waiting for transfers between devices  490 us
    reduce_scatter x1, waiting for transfers between devices, reduce_mlp(): lax.psum_scatter(terms[2], ('dp', 'fsdp'), scatter_dimension=0, tiled=True)  485 us
    reduce_scatter x1, waiting for transfers between devices, reduce_mlp(): lax.psum_scatter(terms[1], ('dp', 'fsdp'), scatter_dimension=0, tiled=True)  478 us
    reduce_scatter x1, waiting for transfers between devices, reduce_attn(): lax.psum_scatter(terms[3], ('dp', 'fsdp'), scatter_dimension=0, tiled=True)  188 us
    reduce_scatter x1, waiting for transfers between devices, reduce_attn(): lax.psum_scatter(terms[4], ('dp', 'fsdp'), scatter_dimension=0, tiled=True)  180 us
    all_gather x1, waiting for transfers between devices, on_device(): lax.all_gather(w_up, ('dp', 'fsdp'), axis=0, tiled=True)  131 us
    all_gather x1, waiting for transfers between devices, on_device(): lax.all_gather(w_down, ('dp', 'fsdp'), axis=1, tiled=True)  131 us
    unnamed x4, blocking collectives  109 us
  transfers between devices with their start and end apart: 17, of which 12 were waited for; matrix products, arithmetic and copies ran while one was open for 14% of the time, Pallas kernels for 0%

commit v1 on v0

v1 whole, which is shorter than its diff:
```python
import functools

import jax
import jax.numpy as jnp
from jax import lax
from jax.experimental import pallas as pl
from jax.experimental.pallas import tpu as pltpu
from jax.sharding import PartitionSpec as P

FEAT = 16
EPS = 1e-05
BLK = 256
F32 = jnp.float32
BF16 = jnp.bfloat16
NT = (((1,), (1,)), ((), ()))
TN = (((0,), (0,)), ((), ()))
VMEM = pltpu.VMEM
ALL = ("dp", "fsdp")


def dot(a, b):
    return jnp.dot(a, b, preferred_element_type=F32)


def dot_nt(a, b):
    return lax.dot_general(a, b, NT, preferred_element_type=F32)


def dot_tn(a, b):
    return lax.dot_general(a, b, TN, preferred_element_type=F32)


def rms_apply(values, gain):
    factor = lax.rsqrt(jnp.mean(values * values, -1, keepdims=True) + EPS)
    return values * factor * gain, factor


def rms_back(grad, values, factor, gain):
    normed = values * factor
    grad_gain = jnp.sum(grad * normed, 0)
    inner = grad * gain
    grad_in = factor * (inner - normed * jnp.mean(inner * normed, -1, keepdims=True))
    return grad_in, grad_gain


def pair_mask(seg_rows, seg_cols, block, other):
    rows = lax.broadcasted_iota(jnp.int32, (BLK, BLK), 0) + block * BLK
    cols = lax.broadcasted_iota(jnp.int32, (BLK, BLK), 1) + other * BLK
    return (seg_rows == seg_cols) & (cols <= rows)


def attend_kernel(heads, wide, q_ref, k_ref, v_ref, sc_ref, sr_ref, att_ref, full_ref, den_ref):
    block = pl.program_id(0)
    seg_rows = sc_ref[...]
    for h in range(heads):
        feat = slice(h * FEAT, (h + 1) * FEAT)
        entry = slice(h * wide, (h + 1) * wide)
        q = q_ref[:, feat]

        def step(c, carry):
            num, den = carry
            here = pl.ds(pl.multiple_of(c * BLK, BLK), BLK)
            x = dot_nt(q, k_ref[here, feat]) * 0.25
            w = jnp.where(pair_mask(seg_rows, sr_ref[c], block, c), 1.0 + x + 0.5 * x * x, 0.0)
            num = num + dot(w.astype(BF16), v_ref[here, entry])
            return num, den + jnp.sum(w, 1, keepdims=True)

        num, den = lax.fori_loop(
            0, block + 1, step, (jnp.zeros((BLK, wide), F32), jnp.zeros((BLK, 1), F32))
        )
        att = num / den
        att_ref[:, entry] = att.astype(BF16)
        full_ref[:, entry] = att
        den_ref[:, h : h + 1] = den


def attend_back_kernel(
    heads, wide, blocks, q_ref, k_ref, v_ref, sc_ref, sr_ref, da_ref, full_ref, den_ref,
    dq_ref, dk_ref, dv_ref, dk_acc, dv_acc,
):
    block = pl.program_id(0)
    seg_rows = sc_ref[...]

    @pl.when(block == 0)
    def _():
        dk_acc[...] = jnp.zeros_like(dk_acc)
        dv_acc[...] = jnp.zeros_like(dv_acc)

    for h in range(heads):
        feat = slice(h * FEAT, (h + 1) * FEAT)
        entry = slice(h * wide, (h + 1) * wide)
        q = q_ref[:, feat]
        inv = 1.0 / den_ref[:, h : h + 1]
        da = da_ref[:, entry].astype(F32)
        dn = (da * inv).astype(BF16)
        dd = -jnp.sum(da * full_ref[:, entry], 1, keepdims=True) * inv

        def step(c, dq):
            here = pl.ds(pl.multiple_of(c * BLK, BLK), BLK)
            k = k_ref[here, feat]
            x = dot_nt(q, k) * 0.25
            mask = pair_mask(seg_rows, sr_ref[c], block, c)
            slope = 1.0 + x
            w = jnp.where(mask, slope + 0.5 * x * x, 0.0).astype(BF16)
            dw = dot_nt(dn, v_ref[here, entry]) + dd
            ds = jnp.where(mask, dw * slope * 0.25, 0.0).astype(BF16)
            dv_acc[here, entry] += dot_tn(w, dn)
            dk_acc[here, feat] += dot_tn(ds, q)
            return dq + dot(ds, k)

        dq_ref[:, feat] = lax.fori_loop(
            0, block + 1, step, jnp.zeros((BLK, FEAT), F32)
        ).astype(BF16)

    @pl.when(block == blocks - 1)
    def _():
        dk_ref[...] = dk_acc[...].astype(BF16)
        dv_ref[...] = dv_acc[...].astype(BF16)


def per_block(lanes):
    return pl.BlockSpec((BLK, lanes), lambda b: (b, 0))


def attend(q, k, v, seg):
    length, width = v.shape
    heads = q.shape[1] // FEAT
    blocks = length // BLK
    sc = seg[:, None]
    sr = seg.reshape(blocks, 1, BLK)
    whole = pl.BlockSpec(memory_space=VMEM)
    return pl.pallas_call(
        functools.partial(attend_kernel, heads, width // heads),
        grid=(blocks,),
        out_shape=(
            jax.ShapeDtypeStruct((length, width), BF16),
            jax.ShapeDtypeStruct((length, width), F32),
            jax.ShapeDtypeStruct((length, heads), F32),
        ),
        in_specs=[per_block(heads * FEAT), whole, whole, per_block(1), whole],
        out_specs=(per_block(width), per_block(width), per_block(heads)),
        compiler_params=pltpu.CompilerParams(vmem_limit_bytes=32 << 20),
        cost_estimate=pl.CostEstimate(
            flops=heads * length * length * 300, bytes_accessed=length * width * 8, transcendentals=0
        ),
    )(q, k, v, sc, sr)


def attend_back(q, k, v, seg, da, full, den):
    length, width = v.shape
    heads = q.shape[1] // FEAT
    blocks = length // BLK
    sc = seg[:, None]
    sr = seg.reshape(blocks, 1, BLK)
    whole = pl.BlockSpec(memory_space=VMEM)
    return pl.pallas_call(
        functools.partial(attend_back_kernel, heads, width // heads, blocks),
        grid=(blocks,),
        out_shape=(
            jax.ShapeDtypeStruct((length, heads * FEAT), BF16),
            jax.ShapeDtypeStruct((length, heads * FEAT), BF16),
            jax.ShapeDtypeStruct((length, width), BF16),
        ),
        in_specs=[per_block(heads * FEAT), whole, whole, per_block(1), whole, per_block(width),
                  per_block(width), per_block(heads)],
        out_specs=(per_block(heads * FEAT), whole, whole),
        scratch_shapes=[VMEM((length, heads * FEAT), F32), VMEM((length, width), F32)],
        compiler_params=pltpu.CompilerParams(vmem_limit_bytes=40 << 20),
        cost_estimate=pl.CostEstimate(
            flops=heads * length * length * 700, bytes_accessed=length * width * 14, transcendentals=0
        ),
    )(q, k, v, sc, sr, da, full, den)


def swap(parts, axis="fsdp"):
    return lax.all_to_all(parts, axis, 1, 0, tiled=True)


def group_columns(arrays, groups):
    return jnp.concatenate([a.reshape(a.shape[0], groups, -1) for a in arrays], -1).reshape(
        arrays[0].shape[0], -1
    )


def split_groups(array, groups, widths):
    parts = array.reshape(array.shape[0], groups, -1)
    out, at = [], 0
    for w in widths:
        out.append(parts[:, :, at : at + w].reshape(array.shape[0], groups * w))
        at += w
    return out


def on_device(
    layer_input, doc_starts, norm1_gain, w_query, w_key, w_value, w_out, norm2_gain,
    w_gate, w_up, w_down, cotangent,
):
    n_f, n_d = lax.axis_size("fsdp"), lax.axis_size("dp")
    x = layer_input[0].astype(F32)
    cot = cotangent[0]
    tokens, width = x.shape
    length = tokens * n_f
    kv = w_query.shape[1]
    rows = w_query.shape[0]
    ff = w_gate.shape[1]
    ff_own = ff // n_f
    qk_own, v_own = kv // n_f, width // n_f

    gains = jnp.stack([norm1_gain, norm2_gain], 1)
    pad = jnp.zeros((rows, 126), BF16)
    mats = lax.all_gather(
        jnp.concatenate([w_query, w_key, w_value, gains, pad], 1), ALL, axis=0, tiled=True
    )
    out_full = lax.all_gather(w_out, ALL, axis=0, tiled=True)
    w_qkv = mats[:, : 2 * kv + width]
    gain_one = mats[:, 2 * kv + width].astype(F32)
    gain_two = mats[:, 2 * kv + width + 1].astype(F32)
    ffn = lax.all_gather(swap(group_columns([w_gate, w_up, w_down.T], n_f)), "dp", axis=0, tiled=True)
    w_gu, w_dt = ffn[:, : 2 * ff_own], ffn[:, 2 * ff_own :]
    cot_all = lax.all_gather(cot, "fsdp", axis=0, tiled=True)

    places = jnp.arange(length, dtype=jnp.int32)
    seg = jnp.sum((doc_starts[0][None, :] <= places[:, None]).astype(jnp.int32), 1)

    normed_one, factor_one = rms_apply(x, gain_one)
    act_one = normed_one.astype(BF16)
    qkv = dot(act_one, w_qkv).astype(BF16)
    q, k, v = qkv[:, :kv], qkv[:, kv : 2 * kv], qkv[:, 2 * kv :]
    own = swap(group_columns([q, k, v], n_f))
    q_own, k_own, val_own = own[:, :qk_own], own[:, qk_own : 2 * qk_own], own[:, 2 * qk_own :]
    att_own, full_own, den_own = attend(q_own, k_own, val_own, seg)
    mixed = lax.all_to_all(att_own, "fsdp", 0, 1, tiled=True)
    resid = x + dot(mixed, out_full)
    normed_two, factor_two = rms_apply(resid, gain_two)
    act_two = lax.all_gather(normed_two.astype(BF16), "fsdp", axis=0, tiled=True)

    gate_up = dot(act_two, w_gu)
    gate, up = gate_up[:, :ff_own], gate_up[:, ff_own:]
    sigma = jax.nn.sigmoid(gate)
    swish = gate * sigma
    hidden = (swish * up).astype(BF16)
    out_part = dot_nt(hidden, w_dt).astype(BF16)
    out_sum = lax.psum_scatter(out_part, "fsdp", scatter_dimension=0, tiled=True)
    output = (resid + out_sum.astype(F32)).astype(BF16)[None]

    d_hidden = dot(cot_all, w_dt)
    d_gate = (d_hidden * up * sigma * (1.0 + gate * (1.0 - sigma))).astype(BF16)
    d_up = (d_hidden * swish).astype(BF16)
    d_gu = jnp.concatenate([d_gate, d_up], 1)
    d_act_two_part = dot_nt(d_gu, w_gu).astype(BF16)
    d_act_two = lax.psum_scatter(d_act_two_part, "fsdp", scatter_dimension=0, tiled=True).astype(F32)
    g_ffn = jnp.concatenate([dot_tn(act_two, d_gu).astype(BF16), dot_tn(cot_all, hidden).astype(BF16)], 1)
    g_ffn = lax.psum_scatter(g_ffn, "dp", scatter_dimension=0, tiled=True)
    g_ffn = lax.all_to_all(g_ffn, "fsdp", 0, 1, tiled=True)
    grad_gate, grad_up, grad_dt = [
        g.astype(F32) for g in split_groups(g_ffn, n_f, [ff_own] * 3)
    ]

    d_norm, gain_two_term = rms_back(d_act_two, resid, factor_two, gain_two)
    d_resid = cot.astype(F32) + d_norm
    d_proj = d_resid.astype(BF16)
    out_term = dot_tn(mixed, d_proj).astype(BF16)
    grad_out = lax.psum_scatter(out_term, ALL, scatter_dimension=0, tiled=True).astype(F32)
    d_att = swap(dot_nt(d_proj, out_full).astype(BF16))
    dq, dk, dv = attend_back(q_own, k_own, val_own, seg, d_att, full_own, den_own)
    back = lax.all_to_all(jnp.concatenate([dq, dk, dv], 1), "fsdp", 0, 1, tiled=True)
    d_qkv = jnp.concatenate(split_groups(back, n_f, [qk_own, qk_own, v_own]), 1)
    d_act_one = dot_nt(d_qkv, w_qkv)
    d_norm, gain_one_term = rms_back(d_act_one, x, factor_one, gain_one)
    grad_input = (d_resid + d_norm)[None]
    terms = jnp.concatenate(
        [
            dot_tn(act_one, d_qkv).astype(BF16),
            gain_one_term[:, None].astype(BF16),
            gain_two_term[:, None].astype(BF16),
            jnp.zeros((width, 126), BF16),
        ],
        1,
    )
    grads = lax.psum_scatter(terms, ALL, scatter_dimension=0, tiled=True).astype(F32)
    return (
        output,
        grad_input,
        grads[:, 2 * kv + width],
        grads[:, :kv],
        grads[:, kv : 2 * kv],
        grads[:, 2 * kv : 2 * kv + width],
        grad_out,
        grads[:, 2 * kv + width + 1],
        grad_gate,
        grad_up,
        grad_dt.T,
    )


def solution(mesh):
    rows, cols = P(ALL, None), P(None, ALL)
    toks = P("dp", "fsdp", None)
    return jax.shard_map(
        on_device,
        mesh=mesh,
        in_specs=(toks, P("dp", None), P(ALL), rows, rows, rows, rows, P(ALL), rows, rows, cols, toks),
        out_specs=(toks, toks, P(ALL), rows, rows, rows, rows, P(ALL), rows, rows, cols),
        check_vma=False,
    )
```

time: 3100 us -> 1120 us (0.36)
  waiting for transfers between devices: 2360 us -> 699 us
  other arithmetic: 160 us -> 29.9 us
  matrix products: 264 us -> 137 us
  blocking collectives: 178 us -> 61.3 us
  Pallas kernels: 0 us -> 76.7 us
    reduce_scatter x6 -> x5, waiting for transfers between devices: 1330 us -> 343 us  [the longest x1 145 us: on_device(): lax.psum_scatter(out_term, ALL, scatter_dimension=0, tiled=True).astype(F32)]
    unnamed x18 -> x10, waiting for transfers between devices: 490 us -> 1.36 us
    all_gather x10 -> x5, waiting for transfers between devices: 538 us -> 282 us  [the longest x1 138 us: on_device(): lax.all_gather(swap(group_columns([w_gate, w_up, w_down.T], n_f)), 'dp',...]
    dot_general x46 -> x12, matrix products: 264 us -> 137 us  [the longest x4 49.7 us: dot(): return jnp.dot(a, b, preferred_element_type=F32)]
    unnamed x4 -> x0, blocking collectives: 109 us -> none
    select_n x48 -> x0, other arithmetic: 94.2 us -> none  [lap(): return jax.tree.map(lambda a, b: jnp.where(reached, a, b), new, before)]
    pallas_call x0 -> x2, Pallas kernels: none -> 76.7 us  [the longest x1 47 us: attend_back(): pl.pallas_call(functools.partial(attend_back_kernel, heads, width // head...]
    all_to_all x0 -> x4, waiting for transfers between devices: none -> 72.7 us  [the longest x1 24.6 us: on_device(): g_ffn = lax.all_to_all(g_ffn, 'fsdp', 0, 1, tiled=True)]
  transfers between devices with their start and end apart: 17 -> 14, of which waited for: 12 -> 14; matrix products, arithmetic and copies ran while one was open for 14% -> 17% of each run, Pallas kernels for 0% -> 7%
where the time goes in v1:
time: 1120 us; the launch traced here: 1110 us
  waiting for transfers between devices  699 us (62%)
  matrix products  137 us (12%)
  Pallas kernels  76.7 us (7%)
  local copies, waits for them, and re-layouts  69.4 us (6%)
  blocking collectives  61.3 us (5%)
  other arithmetic  29.9 us (3%)
  starting transfers between devices  16.6 us (1%)
  between operations  15.1 us (1%)
    reduce_scatter x1, waiting for transfers between devices, on_device(): lax.psum_scatter(out_term, ALL, scatter_dimension=0, tiled=True).astype(F32)  145 us
    all_gather x1, waiting for transfers between devices, on_device(): lax.all_gather(swap(group_columns([w_gate, w_up, w_down.T], n_f)), 'dp',...  138 us
    reduce_scatter x1, waiting for transfers between devices, on_device(): lax.psum_scatter(terms, ALL, scatter_dimension=0, tiled=True).astype(F32)  98.3 us
    reduce_scatter x1, waiting for transfers between devices, on_device(): lax.psum_scatter(out_part, 'fsdp', scatter_dimension=0, tiled=True)  72.5 us
    all_to_all x2, blocking collectives, swap(): return lax.all_to_all(parts, axis, 1, 0, tiled=True)  61.3 us
    all_gather x1, waiting for transfers between devices, on_device(): lax.all_gather(normed_two.astype(BF16), 'fsdp', axis=0, tiled=True)  54.9 us
    dot_general x4, matrix products, dot(): return jnp.dot(a, b, preferred_element_type=F32)  49.7 us
    pallas_call x1, Pallas kernels, attend_back(): pl.pallas_call(functools.partial(attend_back_kernel, heads, width // head...  47 us
  transfers between devices with their start and end apart: 14, of which 14 were waited for; matrix products, arithmetic and copies ran while one was open for 17% of the time, Pallas kernels for 7%

profile of v1, /device:TPU:0, one launch (start us, length us, event | category | flops | bytes accessed | tf_op | source)
XLA Modules:
  0.0 1105.0 jit_solution(10981656780630356323)
XLA Ops:
  8.8 1.8 concatenate.24
  11.5 2.5 reshape.151
  14.1 1.4 reshape.152
  16.5 1.4 reshape.150
  18.9 4.0 concatenate.26
  23.0 43.1 %all_to_all.102 = bf16[64,8,2064]{2,0,1:T(8,128)(2,1)} all-to-all(bf16[64,8,2064]{2,0,1:T(8,128)(2,1)S(1)} %concatenate.26), channel_id=1, replica_groups=mesh['dp'=4,'fsdp'=8] {'fsdp'}, dimensions={1} | all-to-all | bytes 4227072 | tf_op jit(solution)/shard_map/all_to_all | solution.py:176
  66.4 46.9 %all-gather.7.cloned.1.call-done = bf16[2048,2688]{1,0:T(8,128)(2,1)} async-done(((bf16[64,2688]{1,0:T(8,128)(2,1)}), bf16[2048,2688]{1,0:T(8,128)(2,1)}) %all-gather.7.cloned.1.call-update) | async-done | bytes 11010064 | tf_op jit(solution)/shard_map/all_gather | solution.py:211
  113.3 1.8 convert_reduce_fusion
  115.2 6.9 fusion.16
  124.1 3.6 all-to-all-start
  128.2 19.9 %all-to-all-done = bf16[256,8,320]{0,2,1:T(8,128)(2,1)S(1)} async-done(((bf16[256,8,320]{0,2,1:T(8,128)(2,1)}), bf16[256,8,320]{0,2,1:T(8,128)(2,1)S(1)}, u32[]{:S(2)}, u32[]{:S(2)}) %all-to-all-start) | async-done | bytes 1310752 | tf_op jit(solution)/shard_map/all_to_all | solution.py:176
  149.1 1.8 copy.96
  151.7 29.8 %shard_map.203 = (bf16[2048,256]{1,0:T(8,128)(2,1)S(1)}, f32[2048,256]{1,0:T(8,128)S(1)}, f32[2048,2]{1,0:T(8,128)S(1)}) custom-call(bf16[2048,32]{1,0:T(8,128)(2,1)S(1)} %get-tuple-element.40.q_ref, bf16[2048,32]{1,0:T(8,128)(2,1)S(1)} %get-tuple-element.39.k_ref, bf16[2048,256]{1,0:T(8,128)(2,1)S(1)} %slice.103.v_ref, s32[2048,1]{1,0:T(8,128)S(1)} %copy.97.sc_ref, ...), custom_call_target="tpu_custom_call" | custom-call | flops 2516582400 | bytes 4194304 | tf_op jit(solution)/shard_map/pallas_call | solution.py:132
  181.5 1.3 copy-done.6
  182.8 1.3 copy.98
  184.1 4.4 all-to-all-start.1
  188.6 4.9 all-gather.9.cloned.1.call-done
  193.4 10.5 all-to-all-done.1
  203.9 6.9 multiply_reduce_fusion
  210.9 1.3 copy-done.8
  212.2 1.2 multiply_convert_fusion.1
  214.3 137.7 %all-gather.13.cloned.1.call-done = bf16[2048,2064]{1,0:T(8,128)(2,1)} async-done(((bf16[512,2064]{1,0:T(8,128)(2,1)}), bf16[2048,2064]{1,0:T(8,128)(2,1)}) %all-gather.13.cloned.1.call-update) | async-done | bytes 8454160 | tf_op jit(solution)/shard_map/all_gather | solution.py:218
  351.9 54.9 %all-gather.11.cloned.1.call-done = bf16[2048,2048]{1,0:T(8,128)(2,1)} async-done(((bf16[256,2048]{1,0:T(8,128)(2,1)}), bf16[2048,2048]{1,0:T(8,128)(2,1)}) %all-gather.11.cloned.1.call-update) | async-done | bytes 8388624 | tf_op jit(solution)/shard_map/all_gather | solution.py:235
  406.9 18.5 %fusion.14 = f32[2048,1376]{0,1:T(8,128)} fusion(bf16[2048,2048]{1,0:T(8,128)(2,1)} %all-gather.11.cloned.1.call-done, bf16[2048,2064]{1,0:T(8,128)(2,1)} %all-gather.13.cloned.1.call-done), kind=kOutput, calls=%fused_computation.25 | convolution fusion | flops 11542724608 | bytes 25427968 | tf_op jit(solution)/shard_map/dot_general | solution.py:22
  425.3 37.7 %all-gather.15.cloned.1.call-done = bf16[1,2048,2048]{2,1,0:T(8,128)(2,1)} async-done(((bf16[1,256,2048]{2,1,0:T(8,128)(2,1)}), bf16[1,2048,2048]{2,1,0:T(8,128)(2,1)}) %all-gather.15.cloned.1.call-update) | async-done | bytes 8388624 | tf_op jit(solution)/shard_map/all_gather | solution.py:220
  463.0 17.4 %fusion.10 = (bf16[2048,688]{0,1:T(8,128)(2,1)S(1)}, bf16[2048,688]{0,1:T(8,128)(2,1)S(1)}, bf16[2048,688]{0,1:T(8,128)(2,1)}) fusion(f32[2048,1376]{0,1:T(8,128)} %fusion.14, bf16[1,2048,2048]{2,1,0:T(8,128)(2,1)} %all-gather.15.cloned.1.call-done, bf16[2048,2064]{1,0:T(8,128)(2,1)} %all-gather.13.cloned.1.call-done), kind=kOutput, calls=%fused_computation.19 | convolution fusion | flops 5792497664 | bytes 31260672 | tf_op jit(solution)/shard_map/dot_general | solution.py:22
  480.5 1.6 copy-done.23
  483.0 18.1 %convolution_convert_fusion.4 = bf16[2048,2048]{1,0:T(8,128)(2,1)} fusion(bf16[2048,2064]{1,0:T(8,128)(2,1)} %all-gather.13.cloned.1.call-done, bf16[2048,688]{0,1:T(8,128)(2,1)S(1)} %get-tuple-element.32, bf16[2048,688]{0,1:T(8,128)(2,1)S(1)} %get-tuple-element.31), kind=kOutput, calls=%fused_computation.13 | convolution fusion | flops 11558191104 | bytes 19791872 | tf_op jit(solution)/shard_map/dot_general | solution.py:26
  501.2 13.1 %convolution_convert_fusion.1 = bf16[2048,2048]{1,0:T(8,128)(2,1)} fusion(bf16[2048,688]{0,1:T(8,128)(2,1)} %get-tuple-element.33, bf16[2048,2064]{1,0:T(8,128)(2,1)} %all-gather.13.cloned.1.call-done), kind=kOutput, calls=%fused_computation.10 | convolution fusion | flops 5775556608 | bytes 14352384 | tf_op jit(solution)/shard_map/dot_general | solution.py:26
  514.3 11.6 %fusion.26 = bf16[2048,688]{0,1:T(8,128)(2,1)} fusion(bf16[2048,688]{0,1:T(8,128)(2,1)} %get-tuple-element.33, bf16[1,2048,2048]{2,1,0:T(8,128)(2,1)} %all-gather.15.cloned.1.call-done), kind=kOutput, calls=%fused_computation.36 | convolution fusion | flops 5772771328 | bytes 14024704 | tf_op jit(solution)/shard_map/dot_general | solution.py:30
  525.9 16.4 %convolution_convert_fusion.2 = bf16[2048,1376]{0,1:T(8,128)(2,1)} fusion(bf16[2048,2048]{1,0:T(8,128)(2,1)} %all-gather.11.cloned.1.call-done, bf16[2048,688]{0,1:T(8,128)(2,1)S(1)} %copy-done.26, bf16[2048,688]{0,1:T(8,128)(2,1)S(1)} %copy-done.24), kind=kOutput, calls=%fused_computation.11 | convolution fusion | flops 11556814848 | bytes 19660800 | tf_op jit(solution)/shard_map/dot_general | solution.py:30
  542.3 8.6 pad_maximum_fusion
  550.9 21.7 %reduce-scatter.8.cloned.1.call-done = bf16[256,2048]{1,0:T(8,128)(2,1)} async-done(((bf16[2048,2048]{1,0:T(8,128)(2,1)}), bf16[256,2048]{1,0:T(8,128)(2,1)}) %reduce-scatter.8.cloned.1.call-update) | async-done | bytes 1048592 | tf_op jit(solution)/shard_map/reduce_scatter | solution.py:251
  572.6 2.7 fusion.36
  575.3 72.5 %reduce-scatter.6.cloned.1.call-done = bf16[256,2048]{1,0:T(8,128)(2,1)} async-done(((bf16[2048,2048]{1,0:T(8,128)(2,1)}), bf16[256,2048]{1,0:T(8,128)(2,1)}) %reduce-scatter.6.cloned.1.call-update) | async-done | bytes 1048592 | tf_op jit(solution)/shard_map/reduce_scatter | solution.py:243
  647.7 4.1 fusion.35
  651.8 1.3 copy-done.9
  653.1 6.2 convolution_convert_fusion.5
  659.5 18.3 %all_to_all.103 = bf16[256,8,256]{2,0,1:T(8,128)(2,1)S(1)} all-to-all(bf16[256,8,256]{2,0,1:T(8,128)(2,1)S(1)} %bitcast.98), channel_id=1, replica_groups=mesh['dp'=4,'fsdp'=8] {'fsdp'}, dimensions={1} | all-to-all | bytes 2097152 | tf_op jit(solution)/shard_map/all_to_all | solution.py:176
  677.7 47.0 %shard_map.204 = (bf16[2048,32]{1,0:T(8,128)(2,1)S(1)}, bf16[2048,32]{1,0:T(8,128)(2,1)S(1)}, bf16[2048,256]{1,0:T(8,128)(2,1)S(1)}) custom-call(bf16[2048,32]{1,0:T(8,128)(2,1)S(1)} %copy-done.5, bf16[2048,32]{1,0:T(8,128)(2,1)S(1)} %copy-done.3, bf16[2048,256]{1,0:T(8,128)(2,1)S(1)} %copy-done.1, s32[2048,1]{1,0:T(8,128)S(1)} %copy.97.sc_ref, ...), custom_call_target="tpu_custom_call" | custom-call | flops 5872025600 | bytes 7340032 | tf_op jit(solution)/shard_map/pallas_call | solution.py:156
  725.9 1.6 copy.104
  727.5 3.7 all-to-all-start.4
  731.5 17.8 %all-to-all-done.4 = bf16[8,256,320]{1,2,0:T(8,128)(2,1)S(1)} async-done(((bf16[8,256,320]{1,2,0:T(8,128)(2,1)}), bf16[8,256,320]{1,2,0:T(8,128)(2,1)S(1)}, u32[]{:S(2)}, u32[]{:S(2)}) %all-to-all-start.4) | async-done | bytes 1310752 | tf_op jit(solution)/shard_map/all_to_all | solution.py:266
  749.4 8.6 fusion.43
  758.4 6.2 convolution_convert_fusion
  764.7 17.0 %concatenate.30 = bf16[2048,2688]{1,0:T(8,128)(2,1)} concatenate(bf16[2048,2560]{1,0:T(8,128)(2,1)} %convolution_convert_fusion, bf16[2048,1]{1,0:T(8,128)(2,1)S(1)} %convert_element_type.179, bf16[2048,1]{1,0:T(8,128)(2,1)S(1)} %convert_element_type.180, bf16[2048,126]{1,0:T(8,128)(2,1)S(1)} %broadcast_in_dim.14), dimensions={1} | concatenate | bytes 22020096 | tf_op jit(solution)/shard_map/concatenate | solution.py:271
  781.8 1.5 copy-done.10
  783.3 6.8 convolution_convert_fusion.3
  790.1 5.5 reduce-scatter.14.cloned.1.call-done
  795.6 4.3 copy.107
  799.9 4.4 all-to-all-start.5
  804.3 3.5 fusion.42
  807.7 24.6 %all-to-all-done.5 = bf16[8,64,2064]{2,1,0:T(8,128)(2,1)} async-done(((bf16[8,64,2064]{2,1,0:T(8,128)(2,1)}), bf16[8,64,2064]{2,1,0:T(8,128)(2,1)}, u32[]{:S(2)}, u32[]{:S(2)}) %all-to-all-start.5) | async-done | bytes 2113568 | tf_op jit(solution)/shard_map/all_to_all | solution.py:254
  832.3 2.5 slice_convert_fusion
  834.9 2.1 copy.110
  837.0 2.9 reshape.161
  839.9 2.1 copy.108
  842.0 2.9 reshape.159
  845.8 1.7 reshape.160
  847.5 98.3 %reduce-scatter.10.cloned.1.call-done = bf16[64,2688]{1,0:T(8,128)(2,1)} async-done(((bf16[2048,2688]{1,0:T(8,128)(2,1)}), bf16[64,2688]{1,0:T(8,128)(2,1)}) %reduce-scatter.10.cloned.1.call-update) | async-done | bytes 344080 | tf_op jit(solution)/shard_map/reduce_scatter | solution.py:280
  946.9 1.8 slice.115
  949.4 1.4 fusion.57
  950.8 145.2 %reduce-scatter.12.cloned.1.call-done = bf16[64,2048]{1,0:T(8,128)(2,1)} async-done(((bf16[2048,2048]{1,0:T(8,128)(2,1)}), bf16[64,2048]{1,0:T(8,128)(2,1)}) %reduce-scatter.12.cloned.1.call-update) | async-done | bytes 262160 | tf_op jit(solution)/shard_map/reduce_scatter | solution.py:263
  1096.0 1.8 convert_element_type.164
  (100 shorter events, 16.0 us)
Async XLA Ops:
  7.2 6.9 copy-start.16
  7.2 106.1 %all-gather.7.cloned.1.call-start = ((), (), s32[]{:S(2)}) async-start(), calls=%async_computation.11 | async-start | bytes 11354112 | tf_op jit(solution)/shard_map/all_gather | solution.py:211
  10.7 182.8 %all-gather.9.cloned.1.call-start = ((), (), s32[]{:S(2)}) async-start(), calls=%async_computation.12 | async-start | bytes 8650752 | tf_op jit(solution)/shard_map/all_gather | solution.py:214
  11.4 340.5 %all-gather.13.cloned.1.call-start = ((), (), s32[]{:S(2)}) async-start(), calls=%async_computation.14 | async-start | bytes 11141120 | tf_op jit(solution)/shard_map/all_gather | solution.py:218
  13.9 2.6 copy-start.17
  22.9 43.1 %copy-start.11 = (bf16[1,256,2048]{2,1,0:T(8,128)(2,1)S(1)}, bf16[1,256,2048]{2,1,0:T(8,128)(2,1)}, u32[]{:S(2)}) copy-start(bf16[1,256,2048]{2,1,0:T(8,128)(2,1)} %param.12) | copy-start | bytes 3145732
  66.3 55.7 %copy-start.20 = (f32[256]{0:T(256)}, f32[256]{0:T(256)S(1)}, u32[]{:S(2)}) copy-start(f32[256]{0:T(256)S(1)} %add_rsqrt_fusion.1) | copy-start | bytes 3076
  115.1 6.9 copy-start.18
  123.0 4.7 copy-start.22
  124.1 23.9 %all-to-all-start = ((bf16[256,8,320]{0,2,1:T(8,128)(2,1)}), bf16[256,8,320]{0,2,1:T(8,128)(2,1)S(1)}, u32[]{:S(2)}, u32[]{:S(2)}) async-start(bf16[256,8,320]{0,2,1:T(8,128)(2,1)} %pad_maximum_fusion.5), calls=%async_computation | async-start | bytes 2621440 | tf_op jit(solution)/shard_map/all_to_all | solution.py:176
  148.1 1.1 copy-start.14
  151.4 30.1 %copy-start = (bf16[2048,256]{1,0:T(8,128)(2,1)}, bf16[2048,256]{1,0:T(8,128)(2,1)S(1)}, u32[]{:S(2)}) copy-start(bf16[2048,256]{1,0:T(8,128)(2,1)S(1)} %slice.103.v_ref) | copy-start | bytes 3145732
  151.7 29.8 %copy-start.2 = (bf16[2048,32]{1,0:T(8,128)(2,1)}, bf16[2048,32]{1,0:T(8,128)(2,1)S(1)}, u32[]{:S(2)}) copy-start(bf16[2048,32]{1,0:T(8,128)(2,1)S(1)} %get-tuple-element.39.k_ref) | copy-start | bytes 393220
  151.7 29.8 %copy-start.4 = (bf16[2048,32]{1,0:T(8,128)(2,1)}, bf16[2048,32]{1,0:T(8,128)(2,1)S(1)}, u32[]{:S(2)}) copy-start(bf16[2048,32]{1,0:T(8,128)(2,1)S(1)} %get-tuple-element.40.q_ref) | copy-start | bytes 393220
  181.5 1.3 copy-start.6
  184.1 19.8 %copy-start.12 = (bf16[1,256,2048]{2,1,0:T(8,128)(2,1)S(1)}, bf16[1,256,2048]{2,1,0:T(8,128)(2,1)}, u32[]{:S(2)}) copy-start(bf16[1,256,2048]{2,1,0:T(8,128)(2,1)} %param.12) | copy-start | bytes 3145732
  184.1 19.8 %all-to-all-start.1 = ((bf16[8,256,256]{1,2,0:T(8,128)(2,1)}), bf16[8,256,256]{1,2,0:T(8,128)(2,1)}, u32[]{:S(2)}, u32[]{:S(2)}) async-start(bf16[8,256,256]{1,2,0:T(8,128)(2,1)} %copy.98), calls=%async_computation.1 | async-start | bytes 2097152 | tf_op jit(solution)/shard_map/all_to_all | solution.py:232
  188.5 218.3 %all-gather.11.cloned.1.call-start = ((), (), s32[]{:S(2)}) async-start(), calls=%async_computation.13 | async-start | bytes 9437184 | tf_op jit(solution)/shard_map/all_gather | solution.py:235
  210.8 1.3 copy-start.8
  213.4 249.6 %all-gather.15.cloned.1.call-start = ((), (), s32[]{:S(2)}) async-start(), calls=%async_computation.20 | async-start | bytes 9437184 | tf_op jit(solution)/shard_map/all_gather | solution.py:220
  214.0 358.6 %reduce-scatter.8.cloned.1.call-start = ((), (), s32[]{:S(2)}) async-start(), calls=%async_computation.16 | async-start | bytes 9437184 | tf_op jit(solution)/shard_map/reduce_scatter | solution.py:251
  480.5 1.6 copy-start.23
  480.5 2.5 copy-start.25
  501.1 146.6 %reduce-scatter.6.cloned.1.call-start = ((), (), s32[]{:S(2)}) async-start(), calls=%async_computation.15 | async-start | bytes 9437184 | tf_op jit(solution)/shard_map/reduce_scatter | solution.py:243
  514.3 281.4 %reduce-scatter.14.cloned.1.call-start = ((), (), s32[]{:S(2)}) async-start(), calls=%async_computation.19 | async-start | bytes 10567680 | tf_op jit(solution)/shard_map/reduce_scatter | solution.py:253
  514.3 11.6 %copy-start.24 = (bf16[2048,688]{0,1:T(8,128)(2,1)S(1)}, bf16[2048,688]{0,1:T(8,128)(2,1)}, u32[]{:S(2)}) copy-start(bf16[2048,688]{0,1:T(8,128)(2,1)} %copy-done.23) | copy-start | bytes 8454148
  514.3 11.6 %copy-start.26 = (bf16[2048,688]{0,1:T(8,128)(2,1)S(1)}, bf16[2048,688]{0,1:T(8,128)(2,1)}, u32[]{:S(2)}) copy-start(bf16[2048,688]{0,1:T(8,128)(2,1)} %copy-done.25) | copy-start | bytes 8454148
  550.9 96.9 %copy-start.15 = (bf16[1,256,2048]{2,1,0:T(8,128)(2,1)S(1)}, bf16[1,256,2048]{2,1,0:T(8,128)(2,1)}, u32[]{:S(2)}) copy-start(bf16[1,256,2048]{2,1,0:T(8,128)(2,1)} %param.23) | copy-start | bytes 3145732
  651.8 1.3 copy-start.9
  659.3 18.4 %copy-start.1 = (bf16[2048,256]{1,0:T(8,128)(2,1)S(1)}, bf16[2048,256]{1,0:T(8,128)(2,1)}, u32[]{:S(2)}) copy-start(bf16[2048,256]{1,0:T(8,128)(2,1)} %copy-done) | copy-start | bytes 3145732
  659.3 18.4 %copy-start.3 = (bf16[2048,32]{1,0:T(8,128)(2,1)S(1)}, bf16[2048,32]{1,0:T(8,128)(2,1)}, u32[]{:S(2)}) copy-start(bf16[2048,32]{1,0:T(8,128)(2,1)} %copy-done.2) | copy-start | bytes 393220
  659.4 18.4 %copy-start.5 = (bf16[2048,32]{1,0:T(8,128)(2,1)S(1)}, bf16[2048,32]{1,0:T(8,128)(2,1)}, u32[]{:S(2)}) copy-start(bf16[2048,32]{1,0:T(8,128)(2,1)} %copy-done.4) | copy-start | bytes 393220
  659.4 18.4 %copy-start.7 = (f32[2048,256]{1,0:T(8,128)S(1)}, f32[2048,256]{1,0:T(8,128)}, u32[]{:S(2)}) copy-start(f32[2048,256]{1,0:T(8,128)} %copy-done.6) | copy-start | bytes 6291460
  727.4 22.0 %copy-start.13 = (bf16[1,256,2048]{2,1,0:T(8,128)(2,1)S(1)}, bf16[1,256,2048]{2,1,0:T(8,128)(2,1)}, u32[]{:S(2)}) copy-start(bf16[1,256,2048]{2,1,0:T(8,128)(2,1)} %param.12) | copy-start | bytes 3145732
  727.4 22.0 %copy-start.19 = (f32[2048]{0:T(1024)S(1)}, f32[2048]{0:T(1024)}, u32[]{:S(2)}) copy-start(f32[2048]{0:T(1024)} %copy-done.18) | copy-start | bytes 24580
  727.4 22.0 %copy-start.21 = (f32[256]{0:T(256)S(1)}, f32[256]{0:T(256)}, u32[]{:S(2)}) copy-start(f32[256]{0:T(256)} %copy-done.20) | copy-start | bytes 3076
  727.5 21.9 %all-to-all-start.4 = ((bf16[8,256,320]{1,2,0:T(8,128)(2,1)}), bf16[8,256,320]{1,2,0:T(8,128)(2,1)S(1)}, u32[]{:S(2)}, u32[]{:S(2)}) async-start(bf16[8,256,320]{1,2,0:T(8,128)(2,1)} %copy.104), calls=%async_computation.6 | async-start | bytes 2621440 | tf_op jit(solution)/shard_map/all_to_all | solution.py:266
  731.2 214.7 %reduce-scatter.10.cloned.1.call-start = ((), (), s32[]{:S(2)}) async-start(), calls=%async_computation.17 | async-start | bytes 11354112 | tf_op jit(solution)/shard_map/reduce_scatter | solution.py:280
  781.7 1.6 copy-start.10
  781.7 314.3 %reduce-scatter.12.cloned.1.call-start = ((), (), s32[]{:S(2)}) async-start(), calls=%async_computation.18 | async-start | bytes 8650752 | tf_op jit(solution)/shard_map/reduce_scatter | solution.py:263
  799.9 32.4 %all-to-all-start.5 = ((bf16[8,64,2064]{2,1,0:T(8,128)(2,1)}), bf16[8,64,2064]{2,1,0:T(8,128)(2,1)}, u32[]{:S(2)}, u32[]{:S(2)}) async-start(bf16[8,64,2064]{2,1,0:T(8,128)(2,1)} %bitcast.88), calls=%async_computation.10 | async-start | bytes 4456448 | tf_op jit(solution)/shard_map/all_to_all | solution.py:254
Sparse Core Ops, SparseCore 0:
  11.5 101.7 all-gather.6
  116.2 77.2 all-gather.8
  195.0 156.8 all-gather.12
  354.2 52.5 all-gather.10
  408.6 54.3 all-gather.14
  501.2 71.2 reduce-scatter.7
  576.4 71.2 reduce-scatter.5
  650.1 145.4 reduce-scatter.13
  801.6 144.2 reduce-scatter.9
  948.0 147.9 reduce-scatter.11

commit v2 on v1

v2 whole, which is shorter than its diff:
```python
import functools

import jax
import jax.numpy as jnp
from jax import lax
from jax.experimental import pallas as pl
from jax.experimental.pallas import tpu as pltpu
from jax.sharding import PartitionSpec as P

FEAT = 16
EPS = 1e-05
BLK = 256
F32 = jnp.float32
BF16 = jnp.bfloat16
NT = (((1,), (1,)), ((), ()))
TN = (((0,), (0,)), ((), ()))
VMEM = pltpu.VMEM
ALL = ("dp", "fsdp")
MESH = pl.DeviceIdType.MESH


def dot(a, b):
    return jnp.dot(a, b, preferred_element_type=F32)


def dot_nt(a, b):
    return lax.dot_general(a, b, NT, preferred_element_type=F32)


def dot_tn(a, b):
    return lax.dot_general(a, b, TN, preferred_element_type=F32)


def rms_apply(values, gain):
    factor = lax.rsqrt(jnp.mean(values * values, -1, keepdims=True) + EPS)
    return values * factor * gain, factor


def rms_back(grad, values, factor, gain):
    normed = values * factor
    grad_gain = jnp.sum(grad * normed, 0)
    inner = grad * gain
    grad_in = factor * (inner - normed * jnp.mean(inner * normed, -1, keepdims=True))
    return grad_in, grad_gain


def neighbours():
    me = lax.axis_index("fsdp")
    core, side, line = lax.rem(me, 2), lax.rem(me // 2, 2), me // 4

    def at(y, x, c):
        return 4 * y + 2 * x + c

    return (
        me,
        at(line, side, 1 - core),
        at(line, 1 - side, core),
        at(1 - line, side, core),
        at(1 - line, 1 - side, core),
        1 - 2 * core,
    )


def greet(others):
    barrier = pltpu.get_barrier_semaphore()
    for other in others:
        pl.semaphore_signal(barrier, inc=1, device_id={"fsdp": other}, device_id_type=MESH)
    pl.semaphore_wait(barrier, len(others))


def push(src, dst, send, recv, to):
    return pltpu.make_async_remote_copy(
        src_ref=src, dst_ref=dst, send_sem=send, recv_sem=recv,
        device_id={"fsdp": to}, device_id_type=MESH,
    )


class Gather:
    COPIES = 13

    def __init__(self, x_ref, o_ref, send, recv, local):
        me, sib, xn, yn, dg, _ = neighbours()
        half = x_ref.shape[0] // 2
        lo, hi = pl.ds(0, half), pl.ds(half, half)

        def own(part, to, k):
            return push(x_ref.at[part], o_ref.at[me, part], send.at[k], recv.at[k], to)

        def on(who, part, to, k):
            spot = o_ref.at[who, part]
            return push(spot, spot, send.at[k], recv.at[k], to)

        self.keep = pltpu.make_async_copy(x_ref, o_ref.at[me], local)
        self.x_hi, self.y_lo = own(hi, xn, 0), own(lo, yn, 1)
        self.x_lo, self.y_hi = own(lo, xn, 2), own(hi, yn, 3)
        self.whole = push(x_ref, o_ref.at[me], send.at[4], recv.at[4], sib)
        self.over_x, self.over_y = on(yn, lo, xn, 5), on(xn, hi, yn, 7)
        self.core = [
            on(yn, lo, sib, 6), on(xn, hi, sib, 8), on(xn, lo, sib, 9),
            on(yn, hi, sib, 10), on(dg, lo, sib, 11), on(dg, hi, sib, 12),
        ]

    def start(self):
        self.keep.start()
        for copy in (self.x_hi, self.y_lo, self.x_lo, self.y_hi, self.whole):
            copy.start()

    def turn(self):
        self.y_lo.wait_recv()
        self.over_x.start()
        self.core[0].start()
        self.x_hi.wait_recv()
        self.over_y.start()
        self.core[1].start()

    def rest(self):
        self.x_lo.wait_recv()
        self.core[2].start()
        self.y_hi.wait_recv()
        self.core[3].start()

    def across(self):
        self.over_x.wait_recv()
        self.core[4].start()
        self.over_y.wait_recv()
        self.core[5].start()

    def finish(self):
        self.whole.wait_recv()
        for copy in self.core:
            copy.wait_recv()
        self.close()

    def close(self):
        for copy in [self.x_hi, self.y_lo, self.x_lo, self.y_hi, self.whole, self.over_x, self.over_y] + self.core:
            copy.wait_send()
        self.keep.wait()


def gather_scratch():
    dma = pltpu.SemaphoreType.DMA
    return [dma((Gather.COPIES,)), dma((Gather.COPIES,)), dma(())]


def gather_kernel(x_ref, o_ref, send, recv, local):
    _, sib, xn, yn, _, _ = neighbours()
    greet([sib, xn, yn])
    g = Gather(x_ref, o_ref, send, recv, local)
    g.start()
    g.turn()
    g.rest()
    g.across()
    g.finish()


ANY = pl.BlockSpec(memory_space=pl.ANY)
LINKED = pl.CostEstimate(flops=45 * 10**9, bytes_accessed=10**8, transcendentals=0)
WHOLE = pl.BlockSpec(memory_space=VMEM)


def row_gather(x, cid):
    rows, cols = x.shape
    return pl.pallas_call(
        gather_kernel,
        out_shape=jax.ShapeDtypeStruct((8, rows, cols), x.dtype),
        in_specs=[ANY],
        out_specs=ANY,
        scratch_shapes=gather_scratch(),
        compiler_params=pltpu.CompilerParams(collective_id=cid, has_side_effects=True),
        cost_estimate=LINKED,
        name="row_gather",
    )(x).reshape(8 * rows, cols)


class Sum:
    COPIES = 10

    def __init__(self, mine, got, away, ex, ey, fx, fy, total, send, recv):
        me, sib, xn, yn, dg, self.flip = neighbours()
        half = fx.shape[0] // 2
        self.lo, self.hi = lo, hi = pl.ds(0, half), pl.ds(half, half)
        self.order = [dg, xn, yn, me]
        self.mine, self.got, self.ex, self.ey, self.fx, self.fy, self.total = mine, got, ex, ey, fx, fy, total
        self.swaps = [push(away(k), got.at[k], send.at[k], recv.at[k], sib) for k in range(4)]
        self.a = push(mine.at[0, lo], ey, send.at[4], recv.at[4], yn)
        self.b = push(mine.at[0, hi], ex, send.at[5], recv.at[5], xn)
        self.c = push(mine.at[1, hi], fx.at[hi], send.at[6], recv.at[6], xn)
        self.d = push(mine.at[2, lo], fy.at[lo], send.at[7], recv.at[7], yn)
        self.e = push(mine.at[1, lo], fx.at[lo], send.at[8], recv.at[8], xn)
        self.f = push(mine.at[2, hi], fy.at[hi], send.at[9], recv.at[9], yn)

    def add(self, k, part, more=None):
        value = self.mine[k, part].astype(F32) + self.got[k, part].astype(F32)
        if more is not None:
            value = value + more[...].astype(F32)
        self.mine[k, part] = value.astype(BF16)

    def over(self):
        self.swaps[0].wait_recv()
        self.add(0, self.lo)
        self.a.start()
        self.add(0, self.hi)
        self.b.start()

    def along_x(self):
        self.swaps[1].wait_recv()
        self.add(1, self.hi)
        self.c.start()

    def along_y(self):
        self.swaps[2].wait_recv()
        self.add(2, self.lo)
        self.d.start()

    def second(self):
        self.a.wait_recv()
        self.add(1, self.lo, self.ey)
        self.e.start()
        self.b.wait_recv()
        self.add(2, self.hi, self.ex)
        self.f.start()

    def own(self):
        self.swaps[3].wait_recv()
        self.total[...] = self.mine[3].astype(F32) + self.got[3].astype(F32)

    def finish(self):
        for copy in (self.c, self.d, self.e, self.f):
            copy.wait_recv()
        self.total[...] += self.fx[...].astype(F32) + self.fy[...].astype(F32)
        for copy in self.swaps + [self.a, self.b, self.c, self.d, self.e, self.f]:
            copy.wait_send()


def sum_scratch(rows, cols):
    dma = pltpu.SemaphoreType.DMA
    return [
        VMEM((4, rows, cols), BF16), VMEM((4, rows, cols), BF16), VMEM((rows // 2, cols), BF16),
        VMEM((rows // 2, cols), BF16), VMEM((rows, cols), BF16), VMEM((rows, cols), BF16),
        dma((Sum.COPIES,)), dma((Sum.COPIES,)),
    ]


def product_sum_kernel(turned, l_ref, r_ref, o_ref, out, mine, got, ex, ey, fx, fy, send, recv):
    _, sib, xn, yn, _, _ = neighbours()
    rows, cols = o_ref.shape
    greet([sib, xn, yn])
    s = Sum(mine, got, out.at.__getitem__, ex, ey, fx, fy, o_ref, send, recv)

    def block(q, to):
        left = l_ref[pl.ds(pl.multiple_of(q * rows, rows), rows), :]

        @pl.loop(0, cols // 256)
        def _(n):
            here = pl.ds(pl.multiple_of(n * 256, 256), 256)
            part = dot_nt(left, r_ref[here, :]) if turned else dot(left, r_ref[:, here])
            to[:, here] = part.astype(BF16)

    def away(k):
        block(s.order[k] + s.flip, out.at[k])
        s.swaps[k].start()

    def home(k):
        block(s.order[k], mine.at[k])

    away(0)
    home(0)
    away(1)
    s.over()
    home(1)
    s.along_x()
    away(2)
    home(2)
    s.along_y()
    away(3)
    s.second()
    home(3)
    s.own()
    s.finish()


def product_sum(left, right, turned, cid):
    if lax.axis_size("fsdp") != 8:
        part = (dot_nt(left, right) if turned else dot(left, right)).astype(BF16)
        return lax.psum_scatter(part, "fsdp", scatter_dimension=0, tiled=True).astype(F32)
    rows, cols = left.shape[0] // 8, right.shape[0 if turned else 1]
    return pl.pallas_call(
        functools.partial(product_sum_kernel, turned),
        out_shape=jax.ShapeDtypeStruct((rows, cols), F32),
        in_specs=[WHOLE, WHOLE],
        out_specs=WHOLE,
        scratch_shapes=[VMEM((4, rows, cols), BF16)] + sum_scratch(rows, cols),
        compiler_params=pltpu.CompilerParams(
            collective_id=cid, has_side_effects=True, vmem_limit_bytes=56 << 20
        ),
        cost_estimate=LINKED,
        name="product_sum",
    )(left, right)


def start_kernel(x_ref, a_ref, ox_ref, oa_ref, send, recv, local, a_send, a_recv, keep):
    me = lax.axis_index("fsdp")
    others = [lax.rem(me + r, 8) for r in range(1, 8)]
    greet(others)
    g = Gather(x_ref, ox_ref, send, recv, local)
    g.start()
    moves = []
    for r, to in enumerate(others):
        moves.append(push(a_ref.at[to], oa_ref.at[me], a_send.at[r], a_recv.at[r], to))
    stay = [pltpu.make_async_copy(a_ref.at[me], oa_ref.at[me], keep)]
    for copy in moves + stay:
        copy.start()
    g.turn()
    g.rest()
    g.across()
    g.finish()
    for copy in moves + stay:
        copy.wait()


def start_exchange(x, a, cid):
    if lax.axis_size("fsdp") != 8:
        return (
            lax.all_gather(x, "fsdp", axis=0, tiled=True),
            lax.all_to_all(a, "fsdp", 0, 0, tiled=True),
        )
    dma = pltpu.SemaphoreType.DMA
    x_all, a = pl.pallas_call(
        start_kernel,
        out_shape=(
            jax.ShapeDtypeStruct((8,) + x.shape, x.dtype),
            jax.ShapeDtypeStruct(a.shape, a.dtype),
        ),
        in_specs=[ANY] * 2,
        out_specs=(ANY,) * 2,
        scratch_shapes=gather_scratch() + [dma((7,))] * 2 + [dma(())],
        compiler_params=pltpu.CompilerParams(collective_id=cid, has_side_effects=True),
        cost_estimate=LINKED,
        name="start_exchange",
    )(x, a)
    return x_all.reshape(-1, x.shape[1]), a


def same_or_later(seg_rows, seg_cols):
    rows = lax.broadcasted_iota(jnp.int32, (BLK, BLK), 0)
    cols = lax.broadcasted_iota(jnp.int32, (BLK, BLK), 1)
    return (seg_rows == seg_cols) & (cols <= rows)


def spot(b):
    return pl.ds(b * BLK, BLK)


def moving(c):
    return pl.ds(pl.multiple_of(c * BLK, BLK), BLK)


def lanes_of(h, heads):
    lane = lax.broadcasted_iota(jnp.int32, (BLK, 128), 1)
    at = (heads + h) * FEAT
    return (lane >= at) & (lane < at + FEAT)


def lay_out(heads, wide, blocks, qkv_ref, edge_ref, qz, vx):
    first = (lax.broadcasted_iota(jnp.int32, (BLK, wide), 1) == 0).astype(F32)

    @pl.loop(0, blocks)
    def _(b):
        here = moving(b)
        tile = qkv_ref[here, heads * wide :].astype(F32)
        turned = pltpu.roll(tile, heads * FEAT, 1) * 0.25
        edge = edge_ref[here, :]
        for h in range(heads):
            qz[b, h * BLK : (h + 1) * BLK, :] = jnp.where(lanes_of(h, heads), turned, 0.0).astype(BF16)
            vx[h, here, :wide] = (qkv_ref[here, h * wide : (h + 1) * wide].astype(F32) * edge).astype(BF16)
            vx[h, here, wide:] = (first * edge).astype(BF16)


def attend_kernel(heads, wide, blocks, qkv_ref, sc_ref, sr_ref, edge_ref, att_ref, full_ref, den_ref, qz, vx):
    lay_out(heads, wide, blocks, qkv_ref, edge_ref, qz, vx)
    one = (lax.broadcasted_iota(jnp.int32, (BLK, wide), 1) == 0).astype(BF16)
    for b in range(blocks):
        here = spot(b)

        def weigh(c):
            s = dot_nt(qz[b], qkv_ref[c, heads * wide :]) + 1.0
            return s * s + 1.0

        def step(c, sums):
            at = moving(c)
            w = weigh(at).astype(BF16)
            return tuple(
                sums[h] + dot(w[h * BLK : (h + 1) * BLK], vx[h, at, :]) for h in range(heads)
            )

        sums = lax.fori_loop(0, b, step, (jnp.zeros((BLK, 2 * wide), F32),) * heads)
        if b == blocks - 1:
            sums = tuple(s * edge_ref[here, :] for s in sums)
        mask = same_or_later(sc_ref[here, :], sr_ref[b])
        w = weigh(here)
        for h in range(heads):
            entry = slice(h * wide, (h + 1) * wide)
            near = jnp.where(mask, w[h * BLK : (h + 1) * BLK], 0.0).astype(BF16)
            value = jnp.concatenate([qkv_ref[here, entry], one], 1)
            total = sums[h] + dot(near, value)
            den = total[:, wide : wide + 1]
            att = total[:, :wide] / den
            att_ref[here, entry] = att.astype(BF16)
            full_ref[here, entry] = att
            den_ref[here, h : h + 1] = den


def attend_back_kernel(heads, wide, blocks, with_sum, *refs):
    qkv_ref, sc_ref, sr_ref, edge_ref, da_ref, full_ref, den_ref = refs[:7]
    refs = refs[7:]
    if with_sum:
        part_ref, d_ref, o_ref, qz, vx, near_dn, far_dn, qk_acc, v_acc = refs[:9]
        mine, got, ex, ey, fx, fy, send, recv, local = refs[9:]
        _, sib, xn, yn, _, flip = neighbours()
        greet([sib, xn, yn])
        s = Sum(
            mine, got, lambda k: part_ref.at[neighbours()[(4, 2, 3, 0)[k]] + flip], ex, ey, fx, fy, o_ref, send, recv
        )
        loads = [pltpu.make_async_copy(part_ref.at[s.order[k]], mine.at[k], local.at[k]) for k in range(4)]
        for k in range(4):
            s.swaps[k].start()
            loads[k].start()

        def first():
            loads[0].wait()
            s.over()

        def second():
            loads[1].wait()
            s.along_x()
            loads[2].wait()
            s.along_y()

        def fourth():
            loads[3].wait()
            s.own()

        turns = {blocks - 1: first, blocks - 2: second, blocks - 3: s.second, blocks - 4: fourth}
    else:
        d_ref, qz, vx, near_dn, far_dn, qk_acc, v_acc = refs
        turns = {}
    lay_out(heads, wide, blocks, qkv_ref, edge_ref, qz, vx)
    qk_acc[...] = jnp.zeros_like(qk_acc)
    v_acc[...] = jnp.zeros_like(v_acc)
    one = (lax.broadcasted_iota(jnp.int32, (BLK, wide), 1) == 0).astype(F32)
    unit = one.astype(BF16)
    for b in reversed(range(blocks)):
        here = spot(b)
        for h in range(heads):
            entry = slice(h * wide, (h + 1) * wide)
            inv = 1.0 / den_ref[here, h : h + 1]
            da = da_ref[here, entry].astype(F32)
            dn = da * inv
            dd = -jnp.sum(dn * full_ref[here, entry], 1, keepdims=True)
            rows = slice(h * BLK, (h + 1) * BLK)
            near_dn[rows, :wide] = dn.astype(BF16)
            near_dn[rows, wide:] = (dd * one).astype(BF16)
            if b == blocks - 1:
                edge = edge_ref[here, :]
                far_dn[rows, :wide] = (dn * edge).astype(BF16)
                far_dn[rows, wide:] = (dd * edge * one).astype(BF16)

        far = far_dn if b == blocks - 1 else near_dn

        def pair(c, grads, values, mask):
            keys = qkv_ref[c, heads * wide :]
            t = dot_nt(qz[b], keys) + 1.0
            out, parts = [], []
            for h in range(heads):
                rows = slice(h * BLK, (h + 1) * BLK)
                t_h = t[rows]
                w = t_h * t_h + 1.0
                ds = dot_nt(grads[rows, :], values(h)) * t_h
                if mask is not None:
                    w = jnp.where(mask, w, 0.0)
                    ds = jnp.where(mask, ds, 0.0)
                ds = ds.astype(BF16)
                parts.append(ds)
                v_acc[c, h * wide : (h + 1) * wide] += dot_tn(w.astype(BF16), grads[rows, :wide])
                out.append(dot(ds, keys))
            qk_acc[c, :] += dot_tn(jnp.concatenate(parts, 0), qz[b])
            return out

        def step(c, dq):
            at = moving(c)
            return tuple(
                a + g for a, g in zip(dq, pair(at, far, lambda h: vx[h, at, :], None))
            )

        dq = lax.fori_loop(0, b, step, (jnp.zeros((BLK, 128), F32),) * heads)
        if b == 0:
            v_acc[here, :] = v_acc[here, :] * edge_ref[here, :]
        near = pair(
            here, near_dn,
            lambda h: jnp.concatenate([qkv_ref[here, h * wide : (h + 1) * wide], unit], 1),
            same_or_later(sc_ref[here, :], sr_ref[b]),
        )
        total = jnp.zeros((BLK, 128), F32)
        for h in range(heads):
            total = jnp.where(lanes_of(h, heads), dq[h] + near[h], total)
        back = pltpu.roll(total, 128 - heads * FEAT, 1) * 0.5
        d_ref[here, heads * wide :] = back.astype(BF16)
        if b in turns:
            turns[b]()
    for b in range(blocks):
        here = spot(b)
        d_ref[here, : heads * wide] = v_acc[here, :].astype(BF16)
        queries = d_ref[here, heads * wide :].astype(F32)
        d_ref[here, heads * wide :] = (queries + 2.0 * qk_acc[here, :]).astype(BF16)
    if with_sum:
        s.finish()


def marks(seg):
    length = seg.shape[0]
    edge = (seg == seg[BLK - 1]).astype(F32)
    return seg[:, None], seg.reshape(length // BLK, 1, BLK), edge[:, None]


def attend(qkv, seg, heads, wide):
    length = qkv.shape[0]
    blocks = length // BLK
    width = heads * wide
    return pl.pallas_call(
        functools.partial(attend_kernel, heads, wide, blocks),
        out_shape=(
            jax.ShapeDtypeStruct((length, width), BF16),
            jax.ShapeDtypeStruct((length, width), F32),
            jax.ShapeDtypeStruct((length, heads), F32),
        ),
        in_specs=[WHOLE] * 4,
        out_specs=(WHOLE,) * 3,
        scratch_shapes=[VMEM((blocks, heads * BLK, 128), BF16), VMEM((heads, length, 2 * wide), BF16)],
        compiler_params=pltpu.CompilerParams(vmem_limit_bytes=48 << 20),
        cost_estimate=pl.CostEstimate(flops=2 * 10**10, bytes_accessed=4 * 10**7, transcendentals=0),
        name="attend",
    )(qkv, *marks(seg))


def attend_back(qkv, seg, heads, wide, da, full, den, part, cid):
    length, columns = qkv.shape
    blocks = length // BLK
    width = heads * wide
    with_sum = lax.axis_size("fsdp") == 8
    args = [qkv, *marks(seg), da, full, den]
    specs = [WHOLE] * 7
    outs = [jax.ShapeDtypeStruct((length, columns), BF16)]
    scratch = [
        VMEM((blocks, heads * BLK, 128), BF16), VMEM((heads, length, 2 * wide), BF16),
        VMEM((heads * BLK, 2 * wide), BF16), VMEM((heads * BLK, 2 * wide), BF16),
        VMEM((length, 128), F32), VMEM((length, width), F32),
    ]
    if with_sum:
        rows, cols = length // 8, part.shape[1]
        args.append(part.reshape(8, rows, cols))
        specs.append(ANY)
        outs.append(jax.ShapeDtypeStruct((rows, cols), F32))
        scratch += sum_scratch(rows, cols) + [pltpu.SemaphoreType.DMA((4,))]
        params = pltpu.CompilerParams(
            vmem_limit_bytes=60 << 20, collective_id=cid, has_side_effects=True
        )
    else:
        params = pltpu.CompilerParams(vmem_limit_bytes=60 << 20)
    got = pl.pallas_call(
        functools.partial(attend_back_kernel, heads, wide, blocks, with_sum),
        out_shape=outs,
        in_specs=specs,
        out_specs=[WHOLE] * len(outs),
        scratch_shapes=scratch,
        compiler_params=params,
        cost_estimate=LINKED,
        name="attend_back",
    )(*args)
    if with_sum:
        return got
    return got[0], lax.psum_scatter(part, "fsdp", scatter_dimension=0, tiled=True).astype(F32)


def row_all(part, cid):
    if lax.axis_size("fsdp") == 8:
        return row_gather(part, cid)
    return lax.all_gather(part, "fsdp", axis=0, tiled=True)


def group(arrays, groups):
    parts = jnp.concatenate([a.reshape(a.shape[0], groups, -1) for a in arrays], -1)
    return jnp.transpose(parts, (1, 0, 2))


def over_rows(own):
    return lax.all_gather(own.reshape(-1, own.shape[-1]), "dp", axis=0, tiled=True)


def sum_rows(array):
    return lax.psum_scatter(array, "dp", scatter_dimension=0, tiled=True)


def to_owners(part, groups):
    part = part.reshape(groups, part.shape[0] // groups, -1)
    return jnp.transpose(lax.all_to_all(part, "fsdp", 0, 0, tiled=True), (1, 0, 2)).astype(F32)


def columns(array, lo, hi):
    return array[:, :, lo:hi].reshape(array.shape[0], -1)


def after(value, *others):
    return lax.optimization_barrier((value,) + others)[0]


def on_device(
    layer_input, doc_starts, norm1_gain, w_query, w_key, w_value, w_out, norm2_gain,
    w_gate, w_up, w_down, cotangent,
):
    n_f = lax.axis_size("fsdp")
    x = layer_input[0]
    cot = cotangent[0]
    tokens, width = x.shape
    length = tokens * n_f
    kv = w_query.shape[1]
    rows = w_query.shape[0]
    ff = w_gate.shape[1]
    ff_own, qk_own, v_own = ff // n_f, kv // n_f, width // n_f
    heads = qk_own // FEAT
    wide = v_own // heads
    used = v_own + 2 * qk_own
    gain_at = used
    qkv_cols = v_own + 128
    att_cols = qkv_cols + v_own

    def each(vec):
        return jnp.broadcast_to(vec[:, None, None], (rows, n_f, 1))

    attn = group(
        [w_value, w_query, w_key, each(norm1_gain), each(norm2_gain),
         jnp.zeros((rows, n_f, qkv_cols - used - 2), BF16), w_out],
        n_f,
    )
    attn = over_rows(lax.all_to_all(attn, "fsdp", 0, 0, tiled=True))
    x_all, gu_part = start_exchange(x, group([w_gate, w_up], n_f), 0)
    w_gu = over_rows(gu_part)
    dt_part = lax.all_to_all(after(group([w_down.T], n_f), x_all), "fsdp", 0, 0, tiled=True)
    w_dt = over_rows(after(dt_part, w_gu))
    gain_one = attn[:, gain_at].astype(F32)
    gain_two = attn[:, gain_at + 1].astype(F32)
    keep = (jnp.arange(qkv_cols) < used)[None, :]
    w_qkv = jnp.where(keep, attn[:, :qkv_cols], jnp.zeros((), BF16))
    w_o = lax.all_to_all(attn[:, qkv_cols:], "fsdp", 0, 1, tiled=True)

    places = jnp.arange(length, dtype=jnp.int32)
    seg = jnp.sum((doc_starts[0][None, :] <= places[:, None]).astype(jnp.int32), 1)

    normed_one, _ = rms_apply(x_all.astype(F32), gain_one)
    act_one = normed_one.astype(BF16)
    qkv = dot(act_one, w_qkv).astype(BF16)
    mixed, full, den = attend(qkv, seg, heads, wide)
    x_f = x.astype(F32)
    resid = x_f + product_sum(mixed, w_o, False, 2)
    normed_two, factor_two = rms_apply(resid, gain_two)
    act_two = row_all(normed_two.astype(BF16), 3)

    gate_up = dot(act_two, w_gu)
    gate, up = gate_up[:, :ff_own], gate_up[:, ff_own:]
    sigma = jax.nn.sigmoid(gate)
    swish = gate * sigma
    hidden = (swish * up).astype(BF16)
    cot_all = row_all(after(cot, hidden), 1)
    g_dt = dot_tn(cot_all, hidden).astype(BF16)
    d_hidden = dot(cot_all, w_dt)
    d_gate = (d_hidden * up * sigma * (1.0 + gate * (1.0 - sigma))).astype(BF16)
    d_up = (d_hidden * swish).astype(BF16)
    d_gu = jnp.concatenate([d_gate, d_up], 1)
    g_gu = dot_tn(act_two, d_gu).astype(BF16)
    d_act_two = product_sum(after(d_gu, g_gu, g_dt), w_gu, True, 4)
    g_dt = sum_rows(g_dt)
    g_gu = sum_rows(after(g_gu, g_dt))
    d_act_two = after(d_act_two, g_dt)
    out_part = dot_nt(hidden, w_dt).astype(BF16)

    d_norm, _ = rms_back(d_act_two, resid, factor_two, gain_two)
    d_resid = cot.astype(F32) + d_norm
    d_proj = row_all(d_resid.astype(BF16), 5)
    d_att = dot_nt(d_proj, w_o).astype(BF16)
    g_out = dot_tn(mixed, d_proj).astype(BF16)
    d_qkv, out_sum = attend_back(qkv, seg, heads, wide, d_att, full, den, out_part, 7)
    g_qkv = dot_tn(act_one, d_qkv).astype(BF16)
    d_act_one = product_sum(after(d_qkv, g_qkv, g_gu), w_qkv, True, 6)

    g_out = sum_rows(after(lax.all_to_all(g_out, "fsdp", 1, 0, tiled=True), g_gu))
    g_qkv = sum_rows(after(g_qkv, g_out))
    own_rows = lax.axis_index("dp") * (width // lax.axis_size("dp"))

    def gain_grad(weights, grads, gain):
        part = lax.dynamic_slice_in_dim(weights, own_rows, grads.shape[0], 0)
        inner = jnp.sum(part.astype(F32) * grads.astype(F32), 1)
        return inner / lax.dynamic_slice_in_dim(gain, own_rows, grads.shape[0], 0)

    gains = jnp.stack([gain_grad(w_qkv, g_qkv, gain_one), gain_grad(w_gu, g_gu, gain_two)], 1)
    g_qkv = jnp.concatenate([g_qkv[:, :used], gains.astype(BF16)], 1)
    g_dt = to_owners(g_dt, n_f)
    g_gu = to_owners(g_gu, n_f)
    g_out = to_owners(g_out, n_f)
    g_qkv = to_owners(g_qkv, n_f)
    output = (resid + out_sum).astype(BF16)[None]
    factor_one = lax.rsqrt(jnp.mean(x_f * x_f, -1, keepdims=True) + EPS)
    d_norm, _ = rms_back(d_act_one, x_f, factor_one, gain_one)
    grad_input = (d_resid + d_norm)[None]
    return (
        output,
        grad_input,
        jnp.sum(g_qkv[:, :, gain_at], 1),
        columns(g_qkv, v_own, v_own + qk_own),
        columns(g_qkv, v_own + qk_own, used),
        columns(g_qkv, 0, v_own),
        columns(g_out, 0, v_own),
        jnp.sum(g_qkv[:, :, gain_at + 1], 1),
        columns(g_gu, 0, ff_own),
        columns(g_gu, ff_own, 2 * ff_own),
        columns(g_dt, 0, ff_own).T,
    )


def solution(mesh):
    rows, cols = P(ALL, None), P(None, ALL)
    toks = P("dp", "fsdp", None)
    return jax.shard_map(
        on_device,
        mesh=mesh,
        in_specs=(toks, P("dp", None), P(ALL), rows, rows, rows, rows, P(ALL), rows, rows, cols, toks),
        out_specs=(toks, toks, P(ALL), rows, rows, rows, rows, P(ALL), rows, rows, cols),
        check_vma=False,
    )
```

time: 1120 us -> 667 us (0.60)
  waiting for transfers between devices: 699 us -> 30.9 us
  Pallas kernels: 76.7 us -> 398 us
  blocking collectives: 61.3 us -> 0 us
  matrix products: 137 us -> 101 us
  local copies, waits for them, and re-layouts: 69.4 us -> 40.7 us
  starting transfers between devices: 16.6 us -> 32.9 us
    reduce_scatter x5 -> x4, waiting for transfers between devices: 343 us -> 19.2 us  [sum_rows(): return lax.psum_scatter(array, 'dp', scatter_dimension=0, tiled=True)]
    pallas_call x2 -> x9, Pallas kernels: 76.7 us -> 398 us  [the longest x3 154 us: product_sum(): pl.pallas_call(functools.partial(product_sum_kernel, turned), out_shape=j...]
    all_gather x5 -> x3, waiting for transfers between devices: 282 us -> 0.06 us  [over_rows(): lax.all_gather(own.reshape(-1, own.shape[-1]), 'dp', axis=0, tiled=True)]
    all_to_all x4 -> x8, waiting for transfers between devices: 72.7 us -> 10.4 us  [the longest x1 6.45 us: on_device(): attn = over_rows(lax.all_to_all(attn, 'fsdp', 0, 0, tiled=True))]
    all_to_all x2 -> x0, blocking collectives: 61.3 us -> none  [swap(): return lax.all_to_all(parts, axis, 1, 0, tiled=True)]
    dot_general x4 -> x2, matrix products: 46 us -> 18.3 us  [dot_nt(): return lax.dot_general(a, b, NT, preferred_element_type=F32)]
    concatenate x3 -> x1, local copies, waits for them, and re-layouts: 22.9 us -> 1.15 us  [group(): jnp.concatenate([a.reshape(a.shape[0], groups, -1) for a in arrays], -1)]
    all_to_all x4 -> x8, starting transfers between devices: 16 us -> 32.2 us  [the longest x4 15.3 us: to_owners(): lax.all_to_all(part, 'fsdp', 0, 0, tiled=True)]
  transfers between devices with their start and end apart: 14 -> 15, of which waited for: 14 -> 4; matrix products, arithmetic and copies ran while one was open for 17% -> 25% of each run, Pallas kernels for 7% -> 60%
where the time goes in v2:
time: 667 us; the launch traced here: 660 us
  Pallas kernels  398 us (60%)
  matrix products  101 us (15%)
  local copies, waits for them, and re-layouts  40.7 us (6%)
  other arithmetic  40.7 us (6%)
  starting transfers between devices  32.9 us (5%)
  waiting for transfers between devices  30.9 us (5%)
  between operations  15.6 us (2%)
    pallas_call x3, Pallas kernels, product_sum(): pl.pallas_call(functools.partial(product_sum_kernel, turned), out_shape=j...  154 us
    pallas_call x3, Pallas kernels, row_gather(): pl.pallas_call(gather_kernel, out_shape=jax.ShapeDtypeStruct((8, rows, co...  119 us
    pallas_call x1, Pallas kernels, start_exchange(): pl.pallas_call(start_kernel, out_shape=(jax.ShapeDtypeStruct((8,) + x.sha...  55.6 us
    pallas_call x1, Pallas kernels, attend_back(): pl.pallas_call(functools.partial(attend_back_kernel, heads, wide, blocks,...  52 us
    dot_general x4, matrix products, dot_tn(): return lax.dot_general(a, b, TN, preferred_element_type=F32)  42.6 us
    dot_general x3, matrix products, dot(): return jnp.dot(a, b, preferred_element_type=F32)  40.3 us
    reduce_scatter x4, waiting for transfers between devices, sum_rows(): return lax.psum_scatter(array, 'dp', scatter_dimension=0, tiled=True)  19.2 us
    dot_general x2, matrix products, dot_nt(): return lax.dot_general(a, b, NT, preferred_element_type=F32)  18.3 us
  transfers between devices with their start and end apart: 15, of which 4 were waited for; matrix products, arithmetic and copies ran while one was open for 25% of the time, Pallas kernels for 60%

profile of v2, /device:TPU:0, one launch (start us, length us, event | category | flops | bytes accessed | tf_op | source)
XLA Modules:
  0.0 659.8 jit_solution(8436200376883015278)
XLA Ops:
  7.2 0.9 copy.191
  9.3 1.1 copy_bitcast_fusion.2
  11.9 1.1 concatenate.14
  13.0 5.2 all-to-all-start
  18.3 1.4 reshape.189
  19.8 1.4 reshape.190
  21.4 1.6 maximum_bitcast_fusion.a_ref
  22.9 6.5 all-to-all-done
  30.3 55.6 %start_exchange.1 = (bf16[8,256,2048]{2,1,0:T(8,128)(2,1)}, bf16[8,64,1376]{2,1,0:T(8,128)(2,1)}) custom-call(bf16[256,2048]{1,0:T(8,128)(2,1)} %bitcast.110, bf16[8,64,1376]{2,1,0:T(8,128)(2,1)} %maximum_bitcast_fusion.a_ref), custom_call_target="tpu_custom_call" | custom-call | flops 44999999488 | bytes 100000000 | tf_op jit(solution)/shard_map/start_exchange/pallas_call | solution.py:328
  86.7 1.4 reshape.201
  88.1 1.0 copy.236
  89.5 5.6 multiply_reduce_fusion
  95.9 2.7 slice.64
  98.6 4.0 all-to-all-start.1
  102.7 2.0 fusion.11
  104.7 1.6 slice_select_fusion.r_ref
  106.2 8.7 %convolution_convert_fusion.4.qkv_ref.refs_0_ = bf16[2048,384]{1,0:T(8,128)(2,1)S(1)} fusion(bf16[2048,384]{1,0:T(8,128)(2,1)S(1)} %slice_select_fusion.r_ref, bf16[2048,2048]{1,0:T(8,128)(2,1)} %bitcast.113, f32[2048]{0:T(1024)S(1)} %get-tuple-element.110, f32[2048]{0:T(1024)S(1)} %bitcast.136), kind=kOutput, calls=%fused_computation.17 | convolution fusion | flops 3238789120 | bytes 11550720 | tf_op jit(solution)/shard_map/dot_general | solution.py:23
  115.0 17.9 %attend.1 = (bf16[2048,256]{1,0:T(8,128)(2,1)S(1)}, f32[2048,256]{1,0:T(8,128)}, f32[2048,2]{1,0:T(8,128)S(1)}) custom-call(bf16[2048,384]{1,0:T(8,128)(2,1)S(1)} %convolution_convert_fusion.4.qkv_ref.refs_0_, s32[2048,1]{1,0:T(8,128)S(1)} %copy.199.sc_ref.refs_1_, s32[8,1,256]{2,1,0:T(1,128)S(1)} %bitcast.108, ...), custom_call_target="tpu_custom_call" | custom-call | flops 20000000000 | bytes 40000000 | tf_op jit(solution)/shard_map/attend/pallas_call | solution.py:529
  132.9 1.0 copy-done.1
  133.8 1.9 slice_convert_fusion.1
  137.3 4.2 all-to-all-start.2
  141.7 1.1 copy.227
  142.8 46.8 %product_sum.3 = f32[256,2048]{1,0:T(8,128)} custom-call(bf16[2048,256]{1,0:T(8,128)(2,1)} %copy-done.1, bf16[256,2048]{1,0:T(8,128)(2,1)} %bitcast.125), custom_call_target="tpu_custom_call" | custom-call | flops 44999999488 | bytes 100000000 | tf_op jit(solution)/shard_map/product_sum/pallas_call | solution.py:287
  189.6 2.1 multiply_reduce_fusion.3
  191.8 1.3 multiply_convert_fusion.6.x_ref
  193.2 39.4 %row_gather.3 = bf16[8,256,2048]{2,1,0:T(8,128)(2,1)} custom-call(bf16[256,2048]{1,0:T(8,128)(2,1)} %multiply_convert_fusion.6.x_ref), custom_call_target="tpu_custom_call" | custom-call | flops 44999999488 | bytes 100000000 | tf_op jit(solution)/shard_map/row_gather/pallas_call | solution.py:163
  233.6 17.2 %fusion.15 = f32[2048,1376]{1,0:T(8,128)S(1)} fusion(bf16[2048,2048]{1,0:T(8,128)(2,1)} %bitcast.139, bf16[2048,1376]{1,0:T(8,128)(2,1)} %all-gather.6.cloned.1.call-done.r_ref), kind=kOutput, calls=%fused_computation.68 | convolution fusion | flops 11542724608 | bytes 25296896 | tf_op jit(solution)/shard_map/dot_general | solution.py:23
  250.8 2.7 multiply_convert_fusion.3
  253.5 1.6 copy-done.15
  255.1 39.9 %row_gather.4 = bf16[8,256,2048]{2,1,0:T(8,128)(2,1)} custom-call(bf16[256,2048]{1,0:T(8,128)(2,1)} %bitcast.115), custom_call_target="tpu_custom_call" | custom-call | flops 44999999488 | bytes 100000000 | tf_op jit(solution)/shard_map/row_gather/pallas_call | solution.py:163
  295.0 9.6 %convolution_convert_fusion.2 = bf16[2048,688]{0,1:T(8,128)(2,1)} fusion(bf16[2048,2048]{1,0:T(8,128)(2,1)} %bitcast.142, bf16[2048,688]{1,0:T(8,128)(2,1)S(1)} %multiply_convert_fusion.3), kind=kOutput, calls=%fused_computation.10 | convolution fusion | flops 5772771328 | bytes 14024704 | tf_op jit(solution)/shard_map/dot_general | solution.py:31
  304.9 14.4 %multiply_convert_fusion.2 = (bf16[2048,688]{1,0:T(8,128)(2,1)S(1)}, bf16[2048,688]{1,0:T(8,128)(2,1)S(1)}) fusion(f32[2048,1376]{1,0:T(8,128)} %copy-done.15, bf16[2048,2048]{1,0:T(8,128)(2,1)} %bitcast.143, bf16[2048,688]{1,0:T(8,128)(2,1)} %all-gather.8.cloned.1.call-done), kind=kOutput, calls=%fused_computation.5 | convolution fusion | flops 5789679616 | bytes 28114944 | tf_op jit(solution)/shard_map/dot_general | solution.py:23
  319.4 1.9 pad_maximum_fusion.l_ref
  321.2 2.5 copy-done.17
  323.7 17.3 %convolution_convert_fusion.1 = bf16[2048,1376]{1,0:T(8,128)(2,1)} fusion(bf16[2048,2048]{1,0:T(8,128)(2,1)} %bitcast.140, bf16[2048,1376]{1,0:T(8,128)(2,1)S(1)} %pad_maximum_fusion.l_ref), kind=kOutput, calls=%fused_computation.3 | convolution fusion | flops 11545542656 | bytes 19660800 | tf_op jit(solution)/shard_map/dot_general | solution.py:31
  341.0 19.2 %reduce-scatter.5.cloned.1.call-done = bf16[512,688]{0,1:T(8,128)(2,1)} async-done(((bf16[2048,688]{0,1:T(8,128)(2,1)}), bf16[512,688]{0,1:T(8,128)(2,1)}) %reduce-scatter.5.cloned.1.call-update) | async-done | bytes 704528 | tf_op jit(solution)/shard_map/reduce_scatter | solution.py:600
  360.3 53.6 %product_sum.4 = f32[256,2048]{1,0:T(8,128)} custom-call(bf16[2048,1376]{1,0:T(8,128)(2,1)} %copy-done.17, bf16[2048,1376]{1,0:T(8,128)(2,1)} %all-gather.6.cloned.1.call-done.r_ref), custom_call_target="tpu_custom_call" | custom-call | flops 44999999488 | bytes 100000000 | tf_op jit(solution)/shard_map/product_sum/pallas_call | solution.py:287
  414.0 2.4 fusion.8
  417.0 1.7 fusion.12.x_ref
  418.7 39.2 %row_gather.5 = bf16[8,256,2048]{2,1,0:T(8,128)(2,1)} custom-call(bf16[256,2048]{1,0:T(8,128)(2,1)} %fusion.12.x_ref), custom_call_target="tpu_custom_call" | custom-call | flops 44999999488 | bytes 100000000 | tf_op jit(solution)/shard_map/row_gather/pallas_call | solution.py:163
  457.9 5.7 convolution_convert_fusion.5
  463.7 1.1 copy.235
  464.7 3.6 all-to-all-start.3
  468.3 11.5 %convolution_convert_fusion = bf16[2048,2048]{1,0:T(8,128)(2,1)} fusion(bf16[2048,688]{1,0:T(8,128)(2,1)} %copy-done.22, bf16[2048,688]{1,0:T(8,128)(2,1)} %all-gather.8.cloned.1.call-done), kind=kOutput, calls=%fused_computation.2 | convolution fusion | flops 5775556608 | bytes 14024704 | tf_op jit(solution)/shard_map/dot_general | solution.py:27
  479.9 1.1 copy.217
  481.0 6.7 %convolution_convert_fusion.6.refs_4_ = bf16[2048,256]{1,0:T(8,128)(2,1)} fusion(bf16[2048,2048]{1,0:T(8,128)(2,1)} %bitcast.112, bf16[256,2048]{1,0:T(8,128)(2,1)S(1)} %bitcast.126), kind=kOutput, calls=%fused_computation.19 | convolution fusion | flops 2148007936 | bytes 10485760 | tf_op jit(solution)/shard_map/dot_general | solution.py:27
  487.7 4.1 all-to-all-start.7
  492.5 52.0 %attend_back.1 = (bf16[2048,384]{1,0:T(8,128)(2,1)}, f32[256,2048]{1,0:T(8,128)}) custom-call(bf16[2048,384]{1,0:T(8,128)(2,1)} %copy-done.5, s32[2048,1]{1,0:T(8,128)} %copy-done, s32[8,1,256]{2,1,0:T(1,128)} %bitcast.109, f32[2048,1]{1,0:T(8,128)} %copy-done.3, bf16[2048,256]{1,0:T(8,128)(2,1)} %convolution_convert_fusion.6.refs_4_, ...), custom_call_target="tpu_custom_call" | custom-call | flops 44999999488 | bytes 100000000 | tf_op jit(solution)/shard_map/attend_back/pallas_call | solution.py:569
  544.5 10.0 %convolution_convert_fusion.3 = bf16[2048,384]{1,0:T(8,128)(2,1)} fusion(bf16[2048,384]{1,0:T(8,128)(2,1)} %get-tuple-element.40.l_ref, bf16[2048,2048]{1,0:T(8,128)(2,1)} %bitcast.114, f32[2048]{0:T(1024)S(1)} %copy-done.37, f32[2048]{0:T(1024)S(1)} %bitcast.137), kind=kOutput, calls=%fused_computation.16 | convolution fusion | flops 3238789120 | bytes 11550720 | tf_op jit(solution)/shard_map/dot_general | solution.py:31
  555.5 1.7 reshape.220
  557.2 4.3 all-to-all-start.6
  562.3 53.4 %product_sum.5 = f32[256,2048]{1,0:T(8,128)} custom-call(bf16[2048,384]{1,0:T(8,128)(2,1)} %get-tuple-element.40.l_ref, bf16[2048,384]{1,0:T(8,128)(2,1)} %copy-done.24), custom_call_target="tpu_custom_call" | custom-call | flops 44999999488 | bytes 100000000 | tf_op jit(solution)/shard_map/product_sum/pallas_call | solution.py:287
  615.8 2.4 multiply_reduce_fusion.1
  618.4 2.1 fusion.3
  620.5 4.8 fusion.7
  625.3 1.6 convert_bitcast_fusion
  626.9 3.4 all-to-all-start.5
  630.4 1.3 multiply_reduce_fusion.4
  631.8 1.9 pad_maximum_fusion.1
  633.7 3.5 all-to-all-done.5
  637.2 3.5 all-to-all-start.4
  640.7 1.7 fusion.13
  643.3 1.7 reshape.214
  645.9 1.7 reshape.213
  (159 shorter events, 18.8 us)
Async XLA Ops:
  7.2 11.1 %copy-start.29 = (bf16[64,5504]{1,0:T(8,128)(2,1)S(1)}, bf16[64,5504]{1,0:T(8,128)(2,1)}, u32[]{:S(2)}) copy-start(bf16[64,5504]{1,0:T(8,128)(2,1)} %param.20) | copy-start | bytes 2113540
  11.9 7.9 %copy-start.30 = (bf16[64,5504]{1,0:T(8,128)(2,1)S(1)}, bf16[64,5504]{1,0:T(8,128)(2,1)}, u32[]{:S(2)}) copy-start(bf16[64,5504]{1,0:T(8,128)(2,1)} %param.21) | copy-start | bytes 2113540
  13.0 16.3 %all-to-all-start = ((bf16[8,64,640]{2,1,0:T(8,128)(2,1)}), bf16[8,64,640]{2,1,0:T(8,128)(2,1)S(1)}, u32[]{:S(2)}, u32[]{:S(2)}) async-start(bf16[8,64,640]{2,1,0:T(8,128)(2,1)} %bitcast.5), calls=%async_computation | async-start | bytes 1310720 | tf_op jit(solution)/shard_map/all_to_all | solution.py:644
  18.2 77.7 %all-gather.4.cloned.1.call-start = ((), (), s32[]{:S(2)}) async-start(), calls=%async_computation.12 | async-start | bytes 3276800 | tf_op jit(solution)/shard_map/all_gather | solution.py:596
  29.4 0.8 copy-start.23
  30.2 202.4 %all-gather.6.cloned.1.call-start = ((), (), s32[]{:S(2)}) async-start(), calls=%async_computation.13 | async-start | bytes 7208960 | tf_op jit(solution)/shard_map/all_gather | solution.py:596
  30.3 55.7 %copy-start.47 = (s32[1,6]{1,0:T(1,128)S(1)}, s32[1,6]{1,0:T(1,128)}, u32[]{:S(2)}) copy-start(s32[1,6]{1,0:T(1,128)} %param.13) | copy-start | bytes 76
  30.3 56.4 %copy-start.31 = (bf16[5504,64]{0,1:T(8,128)(2,1)S(1)}, bf16[5504,64]{0,1:T(8,128)(2,1)}, u32[]{:S(2)}) copy-start(bf16[5504,64]{0,1:T(8,128)(2,1)} %param.22) | copy-start | bytes 2113540
  86.1 28.9 %copy-start.4 = (s32[2048]{0:T(1024)}, s32[2048]{0:T(1024)S(1)}, u32[]{:S(2)}) copy-start(s32[2048]{0:T(1024)S(1)} %convert_reduce_fusion) | copy-start | bytes 24580
  89.5 25.5 %copy-start = (s32[2048,1]{1,0:T(8,128)}, s32[2048,1]{1,0:T(8,128)S(1)}, u32[]{:S(2)}) copy-start(s32[2048,1]{1,0:T(8,128)S(1)} %copy.199.sc_ref.refs_1_) | copy-start | bytes 24580
  95.1 11.1 %copy-start.45 = (f32[1,2,8,128]{3,1,2,0:T(2,128)}, f32[1,2,8,128]{3,1,2,0:T(2,128)S(1)}, u32[]{:S(2)}) copy-start(f32[1,2,8,128]{3,1,2,0:T(2,128)S(1)} %copy.230) | copy-start | bytes 24580
  95.9 19.1 %copy-start.3 = (f32[2048,1]{1,0:T(8,128)}, f32[2048,1]{1,0:T(8,128)S(1)}, u32[]{:S(2)}) copy-start(f32[2048,1]{1,0:T(8,128)S(1)} %compare_convert_fusion.edge_ref.refs_3_) | copy-start | bytes 24580
  98.6 38.6 %all-to-all-start.1 = ((bf16[8,256,256]{2,1,0:T(8,128)(2,1)}), bf16[8,256,256]{2,1,0:T(8,128)(2,1)S(1)}, u32[]{:S(2)}, u32[]{:S(2)}) async-start(bf16[8,256,256]{2,1,0:T(8,128)(2,1)} %bitcast.119), calls=%async_computation.1 | async-start | bytes 2097152 | tf_op jit(solution)/shard_map/all_to_all | solution.py:653
  104.6 10.3 %copy-start.36 = (f32[2048]{0:T(1024)}, f32[2048]{0:T(1024)S(1)}, u32[]{:S(2)}) copy-start(f32[2048]{0:T(1024)S(1)} %get-tuple-element.110) | copy-start | bytes 24580
  104.6 87.1 %copy-start.33 = (f32[2048]{0:T(1024)}, f32[2048]{0:T(1024)S(1)}, u32[]{:S(2)}) copy-start(f32[2048]{0:T(1024)S(1)} %get-tuple-element.109) | copy-start | bytes 24580
  106.2 8.7 %copy-start.24 = (bf16[2048,384]{1,0:T(8,128)(2,1)}, bf16[2048,384]{1,0:T(8,128)(2,1)S(1)}, u32[]{:S(2)}) copy-start(bf16[2048,384]{1,0:T(8,128)(2,1)S(1)} %slice_select_fusion.r_ref) | copy-start | bytes 4718596
  114.9 17.9 %copy-start.5 = (bf16[2048,384]{1,0:T(8,128)(2,1)}, bf16[2048,384]{1,0:T(8,128)(2,1)S(1)}, u32[]{:S(2)}) copy-start(bf16[2048,384]{1,0:T(8,128)(2,1)S(1)} %convolution_convert_fusion.4.qkv_ref.refs_0_) | copy-start | bytes 4718596
  132.9 1.0 copy-start.1
  133.8 2.0 copy-start.6
  137.3 95.3 %all-to-all-start.2 = ((bf16[8,64,688]{2,1,0:T(8,128)(2,1)}), bf16[8,64,688]{2,1,0:T(8,128)(2,1)S(1)}, u32[]{:S(2)}, u32[]{:S(2)}) async-start(bf16[8,64,688]{2,1,0:T(8,128)(2,1)} %bitcast.105), calls=%async_computation.2 | async-start | bytes 1572864 | tf_op jit(solution)/shard_map/all_to_all | solution.py:647
  141.5 163.5 %all-gather.8.cloned.1.call-start = ((), (), s32[]{:S(2)}) async-start(), calls=%async_computation.14 | async-start | bytes 3932160 | tf_op jit(solution)/shard_map/all_gather | solution.py:596
  142.8 46.8 %copy-start.10 = (bf16[1,256,2048]{2,1,0:T(8,128)(2,1)S(1)}, bf16[1,256,2048]{2,1,0:T(8,128)(2,1)}, u32[]{:S(2)}) copy-start(bf16[1,256,2048]{2,1,0:T(8,128)(2,1)} %param.12) | copy-start | bytes 3145732
  189.6 2.2 copy-start.7
  191.7 40.9 %copy-start.38 = (f32[256]{0:T(256)}, f32[256]{0:T(256)S(1)}, u32[]{:S(2)}) copy-start(f32[256]{0:T(256)S(1)} %add_rsqrt_fusion.1) | copy-start | bytes 3076
  232.6 0.9 copy-start.21
  233.6 126.6 %reduce-scatter.5.cloned.1.call-start = ((), (), s32[]{:S(2)}) async-start(), calls=%async_computation.15 | async-start | bytes 3522560 | tf_op jit(solution)/shard_map/reduce_scatter | solution.py:600
  250.8 4.3 copy-start.15
  255.1 39.9 %copy-start.22 = (bf16[2048,688]{1,0:T(8,128)(2,1)}, bf16[2048,688]{1,0:T(8,128)(2,1)S(1)}, u32[]{:S(2)}) copy-start(bf16[2048,688]{1,0:T(8,128)(2,1)S(1)} %multiply_convert_fusion.3) | copy-start | bytes 8454148
  304.6 187.3 %reduce-scatter.7.cloned.1.call-start = ((), (), s32[]{:S(2)}) async-start(), calls=%async_computation.16 | async-start | bytes 7208960 | tf_op jit(solution)/shard_map/reduce_scatter | solution.py:600
  321.2 2.5 copy-start.17
  360.2 53.7 %copy-start.8 = (f32[256,2048]{1,0:T(8,128)S(1)}, f32[256,2048]{1,0:T(8,128)}, u32[]{:S(2)}) copy-start(f32[256,2048]{1,0:T(8,128)} %product_sum.3) | copy-start | bytes 6291460
  360.2 53.7 %copy-start.11 = (bf16[1,256,2048]{2,1,0:T(8,128)(2,1)S(1)}, bf16[1,256,2048]{2,1,0:T(8,128)(2,1)}, u32[]{:S(2)}) copy-start(bf16[1,256,2048]{2,1,0:T(8,128)(2,1)} %param.12) | copy-start | bytes 3145732
  360.2 53.7 %copy-start.34 = (f32[2048]{0:T(1024)S(1)}, f32[2048]{0:T(1024)}, u32[]{:S(2)}) copy-start(f32[2048]{0:T(1024)} %copy-done.33) | copy-start | bytes 24580
  360.3 53.7 %copy-start.39 = (f32[256]{0:T(256)S(1)}, f32[256]{0:T(256)}, u32[]{:S(2)}) copy-start(f32[256]{0:T(256)} %copy-done.38) | copy-start | bytes 3076
  413.9 3.0 copy-start.13
  414.0 3.0 copy-start.18
  416.4 0.6 copy-start.41
  418.7 39.3 %copy-start.2 = (bf16[2048,256]{1,0:T(8,128)(2,1)S(1)}, bf16[2048,256]{1,0:T(8,128)(2,1)}, u32[]{:S(2)}) copy-start(bf16[2048,256]{1,0:T(8,128)(2,1)} %copy-done.1) | copy-start | bytes 3145732
  464.7 23.0 %all-to-all-start.3 = ((bf16[256,8,256]{2,0,1:T(8,128)(2,1)}), bf16[256,8,256]{2,0,1:T(8,128)(2,1)S(1)}, u32[]{:S(2)}, u32[]{:S(2)}) async-start(bf16[256,8,256]{2,0,1:T(8,128)(2,1)} %bitcast.104), calls=%async_computation.5 | async-start | bytes 2097152 | tf_op jit(solution)/shard_map/all_to_all | solution.py:694
  468.3 11.6 %copy-start.32 = (bf16[512,688]{0,1:T(8,128)(2,1)S(1)}, bf16[512,688]{0,1:T(8,128)(2,1)}, u32[]{:S(2)}) copy-start(bf16[512,688]{0,1:T(8,128)(2,1)} %reduce-scatter.5.cloned.1.call-done) | copy-start | bytes 2113540
  468.3 12.7 %copy-start.28 = (bf16[8,32,8,256]{3,2,0,1:T(8,128)(2,1)S(1)}, bf16[8,32,8,256]{3,2,0,1:T(8,128)(2,1)}, u32[]{:S(2)}) copy-start(bf16[8,32,8,256]{3,2,0,1:T(8,128)(2,1)} %copy.227) | copy-start | bytes 3145732
  487.7 4.2 copy-start.20
  487.7 66.7 %all-to-all-start.7 = ((bf16[8,64,688]{2,1,0:T(8,128)(2,1)}), bf16[8,64,688]{2,1,0:T(8,128)(2,1)S(1)}, u32[]{:S(2)}, u32[]{:S(2)}) async-start(bf16[8,64,688]{2,1,0:T(8,128)(2,1)} %bitcast.34), calls=%async_computation.11 | async-start | bytes 1572864 | tf_op jit(solution)/shard_map/all_to_all | solution.py:605
  491.9 69.7 %reduce-scatter.9.cloned.1.call-start = ((), (), s32[]{:S(2)}) async-start(), calls=%async_computation.17 | async-start | bytes 1310720 | tf_op jit(solution)/shard_map/reduce_scatter | solution.py:600
  492.4 52.0 %copy-start.37 = (f32[2048]{0:T(1024)S(1)}, f32[2048]{0:T(1024)}, u32[]{:S(2)}) copy-start(f32[2048]{0:T(1024)} %copy-done.36) | copy-start | bytes 24580
  492.4 52.0 %copy-start.46 = (f32[1,2,8,128]{3,1,2,0:T(2,128)S(1)}, f32[1,2,8,128]{3,1,2,0:T(2,128)}, u32[]{:S(2)}) copy-start(f32[1,2,8,128]{3,1,2,0:T(2,128)} %copy-done.45) | copy-start | bytes 24580
  557.2 68.1 %all-to-all-start.6 = ((bf16[8,64,1376]{2,1,0:T(8,128)(2,1)}), bf16[8,64,1376]{2,1,0:T(8,128)(2,1)}, u32[]{:S(2)}, u32[]{:S(2)}) async-start(bf16[8,64,1376]{2,1,0:T(8,128)(2,1)} %bitcast.32), calls=%async_computation.10 | async-start | bytes 2883584 | tf_op jit(solution)/shard_map/all_to_all | solution.py:605
  561.5 68.8 %reduce-scatter.11.cloned.1.call-start = ((), (), s32[]{:S(2)}) async-start(), calls=%async_computation.18 | async-start | bytes 1966080 | tf_op jit(solution)/shard_map/reduce_scatter | solution.py:600
  562.3 55.9 %copy-start.44 = (f32[512]{0:T(512)S(1)}, f32[512]{0:T(512)}, u32[]{:S(2)}) copy-start(f32[512]{0:T(512)} %dynamic-slice_reduce_fusion) | copy-start | bytes 6148
  562.3 56.1 %copy-start.12 = (bf16[1,256,2048]{2,1,0:T(8,128)(2,1)S(1)}, bf16[1,256,2048]{2,1,0:T(8,128)(2,1)}, u32[]{:S(2)}) copy-start(bf16[1,256,2048]{2,1,0:T(8,128)(2,1)} %param.12) | copy-start | bytes 3145732
  562.3 58.1 %copy-start.25 = (f32[256,2048]{1,0:T(8,128)S(1)}, f32[256,2048]{1,0:T(8,128)}, u32[]{:S(2)}) copy-start(f32[256,2048]{1,0:T(8,128)} %get-tuple-element.37) | copy-start | bytes 6291460
  615.7 4.7 copy-start.9
  615.7 4.7 copy-start.14
  615.7 4.7 copy-start.19
  615.7 4.7 copy-start.35
  615.8 4.7 copy-start.40
  615.8 4.7 copy-start.42
  625.3 6.4 copy-start.43
  626.9 10.3 %all-to-all-start.5 = ((bf16[8,64,256]{2,1,0:T(8,128)(2,1)}), bf16[8,64,256]{2,1,0:T(8,128)(2,1)S(1)}, u32[]{:S(2)}, u32[]{:S(2)}) async-start(bf16[8,64,256]{2,1,0:T(8,128)(2,1)} %bitcast.30), calls=%async_computation.9 | async-start | bytes 524288 | tf_op jit(solution)/shard_map/all_to_all | solution.py:605
  637.2 5.2 copy-start.26
  637.2 11.7 %all-to-all-start.4 = ((bf16[8,64,322]{2,1,0:T(8,128)(2,1)}), bf16[8,64,322]{2,1,0:T(8,128)(2,1)S(1)}, u32[]{:S(2)}, u32[]{:S(2)}) async-start(bf16[8,64,322]{2,1,0:T(8,128)(2,1)} %bitcast.26), calls=%async_computation.8 | async-start | bytes 786432 | tf_op jit(solution)/shard_map/all_to_all | solution.py:605
  642.4 2.6 copy-start.16
  645.9 1.7 copy-start.27
Sparse Core Ops, SparseCore 0:
  30.4 54.1 all-gather.3
  86.1 106.9 all-gather.5
  233.7 63.7 all-gather.7
  304.8 55.3 reduce-scatter.4
  362.4 102.0 reduce-scatter.6
  495.4 27.4 reduce-scatter.8
  564.7 35.4 reduce-scatter.10

commit v3 on v2

--- a/solution.py
+++ b/solution.py
@@ -129,12 +129,12 @@
         self.whole.wait_recv()
         for copy in self.core:
             copy.wait_recv()
-        self.close()
-
-    def close(self):
+        self.sent()
+        self.keep.wait()
+
+    def sent(self):
         for copy in [self.x_hi, self.y_lo, self.x_lo, self.y_hi, self.whole, self.over_x, self.over_y] + self.core:
             copy.wait_send()
-        self.keep.wait()
 
 
 def gather_scratch():
@@ -376,7 +376,34 @@
             vx[h, here, wide:] = (first * edge).astype(BF16)
 
 
-def attend_kernel(heads, wide, blocks, qkv_ref, sc_ref, sr_ref, edge_ref, att_ref, full_ref, den_ref, qz, vx):
+def attend_kernel(
+    heads, wide, blocks, x_ref, gain_ref, w_ref, sc_ref, sr_ref, edge_ref,
+    qkv_ref, att_ref, full_ref, den_ref, xs, act, load, qz, vx,
+):
+    width = x_ref.shape[1]
+
+    def fetch(b):
+        return pltpu.make_async_copy(x_ref.at[moving(b)], xs.at[lax.rem(b, 2)], load.at[lax.rem(b, 2)])
+
+    fetch(0).start()
+
+    @pl.loop(0, blocks)
+    def _(b):
+        @pl.when(b < blocks - 1)
+        def _():
+            fetch(b + 1).start()
+
+        fetch(b).wait()
+
+        @pl.loop(0, BLK // 64)
+        def _(n):
+            some = pl.ds(pl.multiple_of(n * 64, 64), 64)
+            x = xs[lax.rem(b, 2), some, :].astype(F32)
+            factor = lax.rsqrt(jnp.sum(x * x, 1, keepdims=True) * (1.0 / width) + EPS)
+            act[some, :] = (x * factor * gain_ref[...]).astype(BF16)
+
+        qkv_ref[moving(b), :] = dot(act[...], w_ref[...]).astype(BF16)
+
     lay_out(heads, wide, blocks, qkv_ref, edge_ref, qz, vx)
     one = (lax.broadcasted_iota(jnp.int32, (BLK, wide), 1) == 0).astype(BF16)
     for b in range(blocks):
@@ -522,24 +549,26 @@
     return seg[:, None], seg.reshape(length // BLK, 1, BLK), edge[:, None]
 
 
-def attend(qkv, seg, heads, wide):
-    length = qkv.shape[0]
+def attend(x_all, gain, w_qkv, seg, heads, wide):
+    length, columns = x_all.shape[0], w_qkv.shape[1]
     blocks = length // BLK
     width = heads * wide
     return pl.pallas_call(
         functools.partial(attend_kernel, heads, wide, blocks),
         out_shape=(
+            jax.ShapeDtypeStruct((length, columns), BF16),
             jax.ShapeDtypeStruct((length, width), BF16),
             jax.ShapeDtypeStruct((length, width), F32),
             jax.ShapeDtypeStruct((length, heads), F32),
         ),
-        in_specs=[WHOLE] * 4,
-        out_specs=(WHOLE,) * 3,
-        scratch_shapes=[VMEM((blocks, heads * BLK, 128), BF16), VMEM((heads, length, 2 * wide), BF16)],
+        in_specs=[ANY] + [WHOLE] * 5,
+        out_specs=(WHOLE,) * 4,
+        scratch_shapes=[VMEM((2, BLK, x_all.shape[1]), BF16), VMEM((BLK, x_all.shape[1]), BF16),
+                        pltpu.SemaphoreType.DMA((2,)), VMEM((blocks, heads * BLK, 128), BF16), VMEM((heads, length, 2 * wide), BF16)],
         compiler_params=pltpu.CompilerParams(vmem_limit_bytes=48 << 20),
         cost_estimate=pl.CostEstimate(flops=2 * 10**10, bytes_accessed=4 * 10**7, transcendentals=0),
         name="attend",
-    )(qkv, *marks(seg))
+    )(x_all, gain[None, :], w_qkv, *marks(seg))
 
 
 def attend_back(qkv, seg, heads, wide, da, full, den, part, cid):
@@ -581,6 +610,349 @@
     return got[0], lax.psum_scatter(part, "fsdp", scatter_dimension=0, tiled=True).astype(F32)
 
 
+def tiles(cols):
+    return [pl.ds(at, min(256, cols - at)) for at in range(0, cols, 256)]
+
+
+def gated(gate, up):
+    return gate * jax.nn.sigmoid(gate) * up
+
+
+def gated_back(grad, gate, up):
+    sigma = jax.nn.sigmoid(gate)
+    return grad * up * sigma * (1.0 + gate * (1.0 - sigma)), grad * gate * sigma
+
+
+def lane_index(rows):
+    return lax.broadcasted_iota(jnp.int32, (rows, 128), 1)
+
+
+def feed_kernel(
+    ff, cot_ref, act_ref, w_ref, cot_all_ref, gu_ref, hid_ref, grad_ref,
+    acts, gus, hid, cots, acc, load, save_gu, save_hid, save_cot, send, recv, local,
+):
+    me, sib, xn, yn, dg, flip = neighbours()
+    rows = cot_ref.shape[0]
+    main = ff // 128 * 128
+    tail = ff - main
+    greet([sib, xn, yn])
+    g = Gather(cot_ref, cots, send, recv, local)
+    g.start()
+
+    def at(b):
+        return pl.ds(pl.multiple_of(b * rows, rows), rows)
+
+    def fetch(b):
+        return pltpu.make_async_copy(act_ref.at[at(b)], acts.at[lax.rem(b, 2)], load.at[lax.rem(b, 2)])
+
+    def keep_gu(b):
+        return pltpu.make_async_copy(gus.at[lax.rem(b, 2)], gu_ref.at[at(b)], save_gu.at[lax.rem(b, 2)])
+
+    fetch(0).start()
+
+    def work(lo, hi):
+        @pl.loop(lo, hi)
+        def _(b):
+            slot = lax.rem(b, 2)
+
+            @pl.when(b < 7)
+            def _():
+                fetch(b + 1).start()
+
+            fetch(b).wait()
+
+            @pl.when(b >= 2)
+            def _():
+                keep_gu(b - 2).wait()
+
+            gu = gus.at[slot]
+            for tile in tiles(w_ref.shape[1]):
+                gu[:, tile] = dot(acts[slot], w_ref[:, tile])
+            hid[b, :, :main] = gated(gu[:, :main], gu[:, main : 2 * main]).astype(BF16)
+            last = gu[:, 2 * main :]
+            value = gated(last, pltpu.roll(last, 128 - tail, 1))
+            hid[b, :, main:] = jnp.where(lane_index(rows) < tail, value, 0.0).astype(BF16)
+            keep_gu(b).start()
+
+    work(0, 5)
+    g.turn()
+    work(5, 8)
+    keep_gu(6).wait()
+    keep_gu(7).wait()
+    store = pltpu.make_async_copy(hid, hid_ref, save_hid)
+    store.start()
+
+    def add(first, second, start):
+        @pl.loop(0, acc.shape[0] // 256)
+        def _(n):
+            here = pl.ds(pl.multiple_of(n * 256, 256), 256)
+            value = dot_tn(cots[first, :, here], hid[first]) + dot_tn(cots[second, :, here], hid[second])
+            acc[here, :] = value if start else acc[here, :] + value
+
+    g.whole.wait_recv()
+    g.keep.wait()
+    g.rest()
+    add(me, sib, True)
+    g.across()
+    for k in range(4):
+        g.core[k].wait_recv()
+    add(xn, xn + flip, False)
+    add(yn, yn + flip, False)
+    g.core[4].wait_recv()
+    g.core[5].wait_recv()
+    store_cot = pltpu.make_async_copy(cots, cot_all_ref, save_cot)
+    store_cot.start()
+
+    @pl.loop(0, acc.shape[0] // 256)
+    def _(n):
+        here = pl.ds(pl.multiple_of(n * 256, 256), 256)
+        value = dot_tn(cots[dg, :, here], hid[dg]) + dot_tn(cots[dg + flip, :, here], hid[dg + flip])
+        grad_ref[here, :] = (acc[here, :] + value).astype(BF16)
+
+    g.sent()
+    store.wait()
+    store_cot.wait()
+
+
+def feed(cot, act, w_gu, ff, cid):
+    main = ff // 128 * 128
+    tail = ff - main
+    hid_cols = main + -(-tail // 128) * 128
+    if lax.axis_size("fsdp") != 8:
+        cot_all = lax.all_gather(cot, "fsdp", axis=0, tiled=True)
+        gu = dot(act, w_gu)
+        gate = jnp.concatenate([gu[:, :main], gu[:, 2 * main : 2 * main + tail]], 1)
+        up = jnp.concatenate([gu[:, main : 2 * main], gu[:, 2 * main + tail : 2 * ff]], 1)
+        hidden = jnp.pad(gated(gate, up), ((0, 0), (0, hid_cols - ff))).astype(BF16)
+        return cot_all, gu, hidden, dot_tn(cot_all, hidden).astype(BF16)
+    rows, width = cot.shape
+    gu_cols = w_gu.shape[1]
+    dma = pltpu.SemaphoreType.DMA
+    cot_all, gu, hidden, grad = pl.pallas_call(
+        functools.partial(feed_kernel, ff),
+        out_shape=(
+            jax.ShapeDtypeStruct((8, rows, width), BF16),
+            jax.ShapeDtypeStruct((8 * rows, gu_cols), F32),
+            jax.ShapeDtypeStruct((8, rows, hid_cols), BF16),
+            jax.ShapeDtypeStruct((width, hid_cols), BF16),
+        ),
+        in_specs=[ANY, ANY, WHOLE],
+        out_specs=(ANY, ANY, ANY, WHOLE),
+        scratch_shapes=[
+            VMEM((2, rows, width), BF16), VMEM((2, rows, gu_cols), F32), VMEM((8, rows, hid_cols), BF16),
+            VMEM((8, rows, width), BF16), VMEM((width, hid_cols), F32),
+            dma((2,)), dma((2,)), dma(()), dma(()),
+        ] + gather_scratch(),
+        compiler_params=pltpu.CompilerParams(
+            collective_id=cid, has_side_effects=True, vmem_limit_bytes=56 << 20
+        ),
+        cost_estimate=LINKED,
+        name="feed",
+    )(cot, act, w_gu)
+    return cot_all.reshape(-1, width), gu, hidden.reshape(-1, hid_cols), grad
+
+
+def feed_back_kernel(
+    ff, cot_ref, gu_ref, act_ref, w_ref, d_ref, o_ref, grad_ref,
+    acts, cots, gus, dh, dgu, out, load_act, load_cot, load_gu, mine, got, ex, ey, fx, fy, send, recv,
+):
+    me, sib, xn, yn, dg, flip = neighbours()
+    rows, cols = o_ref.shape
+    main = ff // 128 * 128
+    tail = ff - main
+    order = [dg + flip, dg, xn + flip, xn, yn + flip, yn, me + flip, me]
+
+    def fetch(k):
+        q, slot = order[k], k % 2
+        return [
+            pltpu.make_async_copy(cot_ref.at[q], cots.at[slot], load_cot.at[slot]),
+            pltpu.make_async_copy(gu_ref.at[q], gus.at[slot], load_gu.at[slot]),
+        ]
+
+    for copy in fetch(0):
+        copy.start()
+    whole = pltpu.make_async_copy(act_ref, acts, load_act)
+    whole.start()
+    greet([sib, xn, yn])
+    s = Sum(mine, got, out.at.__getitem__, ex, ey, fx, fy, o_ref, send, recv)
+
+    def block(k, to):
+        if k < 7:
+            for copy in fetch(k + 1):
+                copy.start()
+        for copy in fetch(k):
+            copy.wait()
+        slot, q = k % 2, order[k]
+        gu = gus.at[slot]
+        for tile in tiles(d_ref.shape[1]):
+            dh[:, tile] = dot(cots[slot], d_ref[:, tile])
+        here = pl.ds(pl.multiple_of(q * rows, rows), rows)
+        d_gate, d_up = gated_back(dh[:, :main], gu[:, :main], gu[:, main : 2 * main])
+        dgu[here, :main] = d_gate.astype(BF16)
+        dgu[here, main : 2 * main] = d_up.astype(BF16)
+        last = gu[:, 2 * main :]
+        d_gate, d_up = gated_back(dh[:, main:], last, pltpu.roll(last, 128 - tail, 1))
+        lane = lane_index(rows)
+        both = jnp.where(lane < tail, d_gate, jnp.where(lane < 2 * tail, pltpu.roll(d_up, tail, 1), 0.0))
+        dgu[here, 2 * main :] = both.astype(BF16)
+
+        @pl.loop(0, cols // 256)
+        def _(n):
+            part = pl.ds(pl.multiple_of(n * 256, 256), 256)
+            to[:, part] = dot_nt(dgu[here, :], w_ref[part, :]).astype(BF16)
+
+    def away(k):
+        block(2 * k, out.at[k])
+        s.swaps[k].start()
+
+    def home(k):
+        block(2 * k + 1, mine.at[k])
+
+    away(0)
+    home(0)
+    s.over()
+    away(1)
+    home(1)
+    s.along_x()
+    away(2)
+    home(2)
+    s.along_y()
+    s.second()
+    away(3)
+    home(3)
+    s.own()
+    whole.wait()
+
+    @pl.loop(0, cols // 256)
+    def _(n):
+        part = pl.ds(pl.multiple_of(n * 256, 256), 256)
+        grad_ref[part, :] = dot_tn(acts[:, part], dgu[...]).astype(BF16)
+
+    s.finish()
+
+
+def feed_back(cot_all, gu, act, w_gu, w_dt, ff, cid):
+    main = ff // 128 * 128
+    tail = ff - main
+    if lax.axis_size("fsdp") != 8:
+        gate = jnp.concatenate([gu[:, :main], gu[:, 2 * main : 2 * main + tail]], 1)
+        up = jnp.concatenate([gu[:, main : 2 * main], gu[:, 2 * main + tail : 2 * ff]], 1)
+        d_gate, d_up = gated_back(dot(cot_all, w_dt)[:, :ff], gate, up)
+        d_gu = jnp.concatenate(
+            [d_gate[:, :main], d_up[:, :main], d_gate[:, main:], d_up[:, main:],
+             jnp.zeros((gu.shape[0], gu.shape[1] - 2 * ff), F32)], 1
+        ).astype(BF16)
+        part = lax.psum_scatter(
+            dot_nt(d_gu, w_gu).astype(BF16), "fsdp", scatter_dimension=0, tiled=True
+        )
+        return part.astype(F32), dot_tn(act, d_gu).astype(BF16)
+    length, width = act.shape
+    rows, gu_cols, hid_cols = length // 8, gu.shape[1], w_dt.shape[1]
+    dma = pltpu.SemaphoreType.DMA
+    return pl.pallas_call(
+        functools.partial(feed_back_kernel, ff),
+        out_shape=(
+            jax.ShapeDtypeStruct((rows, width), F32),
+            jax.ShapeDtypeStruct((width, gu_cols), BF16),
+        ),
+        in_specs=[ANY, ANY, ANY, WHOLE, WHOLE],
+        out_specs=(WHOLE, WHOLE),
+        scratch_shapes=[
+            VMEM((length, width), BF16), VMEM((2, rows, width), BF16), VMEM((2, rows, gu_cols), F32),
+            VMEM((rows, hid_cols), F32), VMEM((length, gu_cols), BF16), VMEM((4, rows, width), BF16),
+            dma(()), dma((2,)), dma((2,)),
+        ] + sum_scratch(rows, width),
+        compiler_params=pltpu.CompilerParams(
+            collective_id=cid, has_side_effects=True, vmem_limit_bytes=61 << 20
+        ),
+        cost_estimate=LINKED,
+        name="feed_back",
+    )(cot_all.reshape(8, rows, width), gu.reshape(8, rows, gu_cols), act, w_gu, w_dt)
+
+
+def project_back_kernel(
+    p_ref, hid_ref, d_ref, w_ref, mix_ref, att_ref, part_ref, grad_ref,
+    rowed, parts, acc, save, send, recv, local,
+):
+    me, sib, xn, yn, dg, flip = neighbours()
+    rows, cols = p_ref.shape
+    greet([sib, xn, yn])
+    g = Gather(p_ref, rowed, send, recv, local)
+    g.start()
+
+    def side(lo, hi):
+        @pl.loop(lo, hi)
+        def _(b):
+            left = hid_ref[pl.ds(pl.multiple_of(b * rows, rows), rows), :]
+            for tile in tiles(cols):
+                parts[b, :, tile] = dot_nt(left, d_ref[tile, :]).astype(BF16)
+
+    def use(q, start):
+        at = pl.ds(pl.multiple_of(q * rows, rows), rows)
+        att_ref[at, :] = dot_nt(rowed[q], w_ref[...]).astype(BF16)
+        left = mix_ref[at, :]
+        for tile in tiles(cols):
+            value = dot_tn(left, rowed[q, :, tile])
+            acc[:, tile] = value if start else acc[:, tile] + value
+
+    side(0, 5)
+    g.turn()
+    side(5, 8)
+    store = pltpu.make_async_copy(parts, part_ref, save)
+    store.start()
+    g.keep.wait()
+    use(me, True)
+    g.whole.wait_recv()
+    use(sib, False)
+    g.rest()
+    use(xn, False)
+    use(yn, False)
+    g.across()
+    use(dg, False)
+    for k in range(4):
+        g.core[k].wait_recv()
+    use(xn + flip, False)
+    use(yn + flip, False)
+    g.core[4].wait_recv()
+    g.core[5].wait_recv()
+    use(dg + flip, False)
+    grad_ref[...] = acc[...].astype(BF16)
+    g.sent()
+    store.wait()
+
+
+def project_back(d_proj, hidden, w_dt, w_o, mixed, cid):
+    if lax.axis_size("fsdp") != 8:
+        d_proj = lax.all_gather(d_proj, "fsdp", axis=0, tiled=True)
+        return (
+            dot_nt(d_proj, w_o).astype(BF16),
+            dot_nt(hidden, w_dt).astype(BF16),
+            dot_tn(mixed, d_proj).astype(BF16),
+        )
+    rows, width = d_proj.shape
+    own = w_o.shape[0]
+    att, part, grad = pl.pallas_call(
+        project_back_kernel,
+        out_shape=(
+            jax.ShapeDtypeStruct((8 * rows, own), BF16),
+            jax.ShapeDtypeStruct((8, rows, width), BF16),
+            jax.ShapeDtypeStruct((own, width), BF16),
+        ),
+        in_specs=[ANY] + [WHOLE] * 4,
+        out_specs=(WHOLE, ANY, WHOLE),
+        scratch_shapes=[
+            VMEM((8, rows, width), BF16), VMEM((8, rows, width), BF16), VMEM((own, width), F32),
+            pltpu.SemaphoreType.DMA(()),
+        ] + gather_scratch(),
+        compiler_params=pltpu.CompilerParams(
+            collective_id=cid, has_side_effects=True, vmem_limit_bytes=50 << 20
+        ),
+        cost_estimate=LINKED,
+        name="project_back",
+    )(d_proj, hidden, w_dt, w_o, mixed)
+    return att, part.reshape(8 * rows, width), grad
+
+
 def row_all(part, cid):
     if lax.axis_size("fsdp") == 8:
         return row_gather(part, cid)
@@ -642,10 +1014,21 @@
         n_f,
     )
     attn = over_rows(lax.all_to_all(attn, "fsdp", 0, 0, tiled=True))
-    x_all, gu_part = start_exchange(x, group([w_gate, w_up], n_f), 0)
+    main = ff_own // 128 * 128
+
+    def halves(a):
+        a = a.reshape(rows, n_f, ff_own)
+        return a[:, :, :main], a[:, :, main:]
+
+    (gate_main, gate_tail), (up_main, up_tail) = halves(w_gate), halves(w_up)
+    empty = jnp.zeros((rows, n_f, 128), BF16)
+    gu = group(
+        [gate_main, up_main, gate_tail, up_tail, empty[:, :, : -(2 * ff_own) % 128]], n_f
+    )
+    x_all, gu_part = start_exchange(x, gu, 0)
     w_gu = over_rows(gu_part)
-    dt_part = lax.all_to_all(after(group([w_down.T], n_f), x_all), "fsdp", 0, 0, tiled=True)
-    w_dt = over_rows(after(dt_part, w_gu))
+    dt = group([w_down.T, empty[:, :, : -ff_own % 128]], n_f)
+    w_dt = over_rows(lax.all_to_all(after(dt, x_all), "fsdp", 0, 0, tiled=True))
     gain_one = attn[:, gain_at].astype(F32)
     gain_two = attn[:, gain_at + 1].astype(F32)
     keep = (jnp.arange(qkv_cols) < used)[None, :]
@@ -657,41 +1040,25 @@
 
     normed_one, _ = rms_apply(x_all.astype(F32), gain_one)
     act_one = normed_one.astype(BF16)
-    qkv = dot(act_one, w_qkv).astype(BF16)
-    mixed, full, den = attend(qkv, seg, heads, wide)
+    qkv, mixed, full, den = attend(x_all, gain_one, w_qkv, seg, heads, wide)
     x_f = x.astype(F32)
     resid = x_f + product_sum(mixed, w_o, False, 2)
     normed_two, factor_two = rms_apply(resid, gain_two)
     act_two = row_all(normed_two.astype(BF16), 3)
 
-    gate_up = dot(act_two, w_gu)
-    gate, up = gate_up[:, :ff_own], gate_up[:, ff_own:]
-    sigma = jax.nn.sigmoid(gate)
-    swish = gate * sigma
-    hidden = (swish * up).astype(BF16)
-    cot_all = row_all(after(cot, hidden), 1)
-    g_dt = dot_tn(cot_all, hidden).astype(BF16)
-    d_hidden = dot(cot_all, w_dt)
-    d_gate = (d_hidden * up * sigma * (1.0 + gate * (1.0 - sigma))).astype(BF16)
-    d_up = (d_hidden * swish).astype(BF16)
-    d_gu = jnp.concatenate([d_gate, d_up], 1)
-    g_gu = dot_tn(act_two, d_gu).astype(BF16)
-    d_act_two = product_sum(after(d_gu, g_gu, g_dt), w_gu, True, 4)
+    cot_all, gate_up, hidden, g_dt = feed(cot, act_two, w_gu, ff_own, 1)
+    d_act_two, g_gu = feed_back(cot_all, gate_up, act_two, w_gu, w_dt, ff_own, 4)
     g_dt = sum_rows(g_dt)
     g_gu = sum_rows(after(g_gu, g_dt))
-    d_act_two = after(d_act_two, g_dt)
-    out_part = dot_nt(hidden, w_dt).astype(BF16)
 
     d_norm, _ = rms_back(d_act_two, resid, factor_two, gain_two)
     d_resid = cot.astype(F32) + d_norm
-    d_proj = row_all(d_resid.astype(BF16), 5)
-    d_att = dot_nt(d_proj, w_o).astype(BF16)
-    g_out = dot_tn(mixed, d_proj).astype(BF16)
+    d_att, out_part, g_out = project_back(d_resid.astype(BF16), hidden, w_dt, w_o, mixed, 5)
     d_qkv, out_sum = attend_back(qkv, seg, heads, wide, d_att, full, den, out_part, 7)
     g_qkv = dot_tn(act_one, d_qkv).astype(BF16)
     d_act_one = product_sum(after(d_qkv, g_qkv, g_gu), w_qkv, True, 6)
 
-    g_out = sum_rows(after(lax.all_to_all(g_out, "fsdp", 1, 0, tiled=True), g_gu))
+    g_out = sum_rows(after(lax.all_to_all(g_out, "fsdp", 1, 0, tiled=True), g_gu, d_qkv))
     g_qkv = sum_rows(after(g_qkv, g_out))
     own_rows = lax.axis_index("dp") * (width // lax.axis_size("dp"))
 
@@ -701,11 +1068,16 @@
         return inner / lax.dynamic_slice_in_dim(gain, own_rows, grads.shape[0], 0)
 
     gains = jnp.stack([gain_grad(w_qkv, g_qkv, gain_one), gain_grad(w_gu, g_gu, gain_two)], 1)
-    g_qkv = jnp.concatenate([g_qkv[:, :used], gains.astype(BF16)], 1)
+    filler = jnp.zeros((g_qkv.shape[0], qkv_cols - used - 2), BF16)
+    g_attn = jnp.concatenate([g_qkv[:, :used], gains.astype(BF16), filler, g_out], 1)
     g_dt = to_owners(g_dt, n_f)
     g_gu = to_owners(g_gu, n_f)
-    g_out = to_owners(g_out, n_f)
-    g_qkv = to_owners(g_qkv, n_f)
+    g_attn = to_owners(g_attn, n_f)
+
+    def from_halves(at, tail):
+        both = [g_gu[:, :, at : at + main], g_gu[:, :, tail : tail + ff_own - main]]
+        return jnp.concatenate(both, 2).reshape(rows, ff)
+
     output = (resid + out_sum).astype(BF16)[None]
     factor_one = lax.rsqrt(jnp.mean(x_f * x_f, -1, keepdims=True) + EPS)
     d_norm, _ = rms_back(d_act_one, x_f, factor_one, gain_one)
@@ -713,14 +1085,14 @@
     return (
         output,
         grad_input,
-        jnp.sum(g_qkv[:, :, gain_at], 1),
-        columns(g_qkv, v_own, v_own + qk_own),
-        columns(g_qkv, v_own + qk_own, used),
-        columns(g_qkv, 0, v_own),
-        columns(g_out, 0, v_own),
-        jnp.sum(g_qkv[:, :, gain_at + 1], 1),
-        columns(g_gu, 0, ff_own),
-        columns(g_gu, ff_own, 2 * ff_own),
+        jnp.sum(g_attn[:, :, gain_at], 1),
+        columns(g_attn, v_own, v_own + qk_own),
+        columns(g_attn, v_own + qk_own, used),
+        columns(g_attn, 0, v_own),
+        columns(g_attn, qkv_cols, att_cols),
+        jnp.sum(g_attn[:, :, gain_at + 1], 1),
+        from_halves(0, 2 * main),
+        from_halves(main, main + ff_own),
         columns(g_dt, 0, ff_own).T,
     )
 

time: 667 us -> 591 us (0.89)
  matrix products: 101 us -> 9.95 us
  Pallas kernels: 398 us -> 432 us
  other arithmetic: 40.7 us -> 33.9 us
  waiting for transfers between devices: 30.9 us -> 24.1 us
    pallas_call x0 -> x3, Pallas kernels: none -> 156 us  [the longest x1 60.5 us: feed_back(): pl.pallas_call(functools.partial(feed_back_kernel, ff), out_shape=(jax.Sh...]
    pallas_call x3 -> x1, Pallas kernels: 119 us -> 38.6 us  [row_gather(): pl.pallas_call(gather_kernel, out_shape=jax.ShapeDtypeStruct((8, rows, co...]
    dot_general x5 -> x0, matrix products: 58.6 us -> none  [the longest x3 40.3 us: dot(): return jnp.dot(a, b, preferred_element_type=F32)]
    pallas_call x3 -> x2, Pallas kernels: 154 us -> 98.3 us  [product_sum(): pl.pallas_call(functools.partial(product_sum_kernel, turned), out_shape=j...]
    dot_general x4 -> x1, matrix products: 42.6 us -> 9.95 us  [dot_tn(): return lax.dot_general(a, b, TN, preferred_element_type=F32)]
    reduce_scatter x4, waiting for transfers between devices: 19.2 us -> 2.16 us  [sum_rows(): return lax.psum_scatter(array, 'dp', scatter_dimension=0, tiled=True)]
    pallas_call x1, Pallas kernels: 17.9 us -> 31.5 us  [attend(): pl.pallas_call(functools.partial(attend_kernel, heads, wide, blocks), out...]
    all_to_all x1, waiting for transfers between devices: 0.01 us -> 10.6 us  [on_device(): w_dt = over_rows(lax.all_to_all(after(dt, x_all), 'fsdp', 0, 0, tiled=True))]
  transfers between devices with their start and end apart: 15 -> 14, of which waited for: 4 -> 6; matrix products, arithmetic and copies ran while one was open for 25% -> 11% of each run, Pallas kernels for 60% -> 74%
where the time goes in v3:
time: 591 us; the launch traced here: 584 us
  Pallas kernels  432 us (73%)
  local copies, waits for them, and re-layouts  41.6 us (7%)
  other arithmetic  33.9 us (6%)
  starting transfers between devices  27.8 us (5%)
  waiting for transfers between devices  24.1 us (4%)
  between operations  15.2 us (3%)
  matrix products  9.95 us (2%)
    pallas_call x2, Pallas kernels, product_sum(): pl.pallas_call(functools.partial(product_sum_kernel, turned), out_shape=j...  98.3 us
    pallas_call x1, Pallas kernels, feed_back(): pl.pallas_call(functools.partial(feed_back_kernel, ff), out_shape=(jax.Sh...  60.5 us
    pallas_call x1, Pallas kernels, start_exchange(): pl.pallas_call(start_kernel, out_shape=(jax.ShapeDtypeStruct((8,) + x.sha...  55.6 us
    pallas_call x1, Pallas kernels, attend_back(): pl.pallas_call(functools.partial(attend_back_kernel, heads, wide, blocks,...  52 us
    pallas_call x1, Pallas kernels, feed(): pl.pallas_call(functools.partial(feed_kernel, ff), out_shape=(jax.ShapeDt...  51.4 us
    pallas_call x1, Pallas kernels, project_back(): pl.pallas_call(project_back_kernel, out_shape=(jax.ShapeDtypeStruct((8 *...  43.8 us
    pallas_call x1, Pallas kernels, row_gather(): pl.pallas_call(gather_kernel, out_shape=jax.ShapeDtypeStruct((8, rows, co...  38.6 us
    pallas_call x1, Pallas kernels, attend(): pl.pallas_call(functools.partial(attend_kernel, heads, wide, blocks), out...  31.5 us
  transfers between devices with their start and end apart: 14, of which 6 were waited for; matrix products, arithmetic and copies ran while one was open for 11% of the time, Pallas kernels for 74%

profile of v3, /device:TPU:0, one launch (start us, length us, event | category | flops | bytes accessed | tf_op | source)
XLA Modules:
  0.0 584.1 jit_solution(6996570855302824112)
XLA Ops:
  7.2 0.9 copy.146
  8.2 0.9 copy.147
  9.2 1.1 copy_bitcast_fusion.1
  11.9 1.1 concatenate.20
  13.0 5.3 all-to-all-start
  18.4 1.4 reshape.188
  19.9 1.4 reshape.189
  21.6 1.9 concatenate.19
  23.5 6.0 %all-to-all-done = bf16[8,64,640]{2,1,0:T(8,128)(2,1)S(1)} async-done(((bf16[8,64,640]{2,1,0:T(8,128)(2,1)}), bf16[8,64,640]{2,1,0:T(8,128)(2,1)S(1)}, u32[]{:S(2)}, u32[]{:S(2)}) %all-to-all-start) | async-done | bytes 655392 | tf_op jit(solution)/shard_map/all_to_all | solution.py:1016
  29.5 0.8 copy-done.21
  30.4 55.6 %start_exchange.1 = (bf16[8,256,2048]{2,1,0:T(8,128)(2,1)}, bf16[8,64,1408]{2,1,0:T(8,128)(2,1)}) custom-call(bf16[256,2048]{1,0:T(8,128)(2,1)} %bitcast.92, bf16[8,64,1408]{2,1,0:T(8,128)(2,1)} %bitcast.104), custom_call_target="tpu_custom_call" | custom-call | flops 44999999488 | bytes 100000000 | tf_op jit(solution)/shard_map/start_exchange/pallas_call | solution.py:328
  86.1 1.4 reshape.200
  87.6 0.9 pad_bitcast_fusion
  88.6 3.5 all-to-all-start.2
  94.1 10.6 %all-to-all-done.2 = bf16[8,64,768]{2,1,0:T(8,128)(2,1)S(1)} async-done(((bf16[8,64,768]{2,1,0:T(8,128)(2,1)}), bf16[8,64,768]{2,1,0:T(8,128)(2,1)S(1)}, u32[]{:S(2)}, u32[]{:S(2)}) %all-to-all-start.2) | async-done | bytes 786464 | tf_op jit(solution)/shard_map/all_to_all | solution.py:1031
  104.7 0.9 copy-done.20
  105.6 2.3 slice.98
  107.8 3.6 all-to-all-start.1
  111.6 2.0 fusion.14
  113.6 2.7 slice_select_fusion.w_ref.r_ref
  116.4 31.5 %attend.1 = (bf16[2048,384]{1,0:T(8,128)(2,1)S(1)}, bf16[2048,256]{1,0:T(8,128)(2,1)S(1)}, f32[2048,256]{1,0:T(8,128)}, f32[2048,2]{1,0:T(8,128)S(1)}) custom-call(bf16[2048,2048]{1,0:T(8,128)(2,1)} %bitcast.93, f32[1,2048]{1,0:T(1,128)S(1)} %bitcast.88, bf16[2048,384]{1,0:T(8,128)(2,1)} %slice_select_fusion.w_ref.r_ref, ...), custom_call_target="tpu_custom_call" | custom-call | flops 20000000000 | bytes 40000000 | tf_op jit(solution)/shard_map/attend/pallas_call | solution.py:556
  147.9 1.1 copy-done.5
  149.0 1.0 copy-done.6
  150.0 1.0 copy-done.7
  151.0 1.1 copy.177
  152.1 46.1 %product_sum.2 = f32[256,2048]{1,0:T(8,128)} custom-call(bf16[2048,256]{1,0:T(8,128)(2,1)} %copy-done.7, bf16[256,2048]{1,0:T(8,128)(2,1)} %bitcast.106), custom_call_target="tpu_custom_call" | custom-call | flops 44999999488 | bytes 100000000 | tf_op jit(solution)/shard_map/product_sum/pallas_call | solution.py:287
  198.2 2.2 multiply_reduce_fusion.3
  200.7 1.4 multiply_convert_fusion.4.x_ref
  202.1 38.6 %row_gather.1 = bf16[8,256,2048]{2,1,0:T(8,128)(2,1)} custom-call(bf16[256,2048]{1,0:T(8,128)(2,1)} %multiply_convert_fusion.4.x_ref), custom_call_target="tpu_custom_call" | custom-call | flops 44999999488 | bytes 100000000 | tf_op jit(solution)/shard_map/row_gather/pallas_call | solution.py:163
  240.7 51.4 %feed.1 = (bf16[8,256,2048]{2,1,0:T(8,128)(2,1)}, f32[2048,1408]{1,0:T(8,128)}, bf16[8,256,768]{2,1,0:T(8,128)(2,1)}, bf16[2048,768]{1,0:T(8,128)(2,1)}) custom-call(bf16[256,2048]{1,0:T(8,128)(2,1)} %bitcast.95, bf16[2048,2048]{1,0:T(8,128)(2,1)} %bitcast.120, bf16[2048,1408]{1,0:T(8,128)(2,1)} %all-gather.6.cloned.1.call-done.w_ref), custom_call_target="tpu_custom_call" | custom-call | flops 44999999488 | bytes 100000000 | tf_op jit(solution)/shard_map/feed/pallas_call | solution.py:731
  292.1 60.5 %feed_back.1 = (f32[256,2048]{1,0:T(8,128)}, bf16[2048,1408]{1,0:T(8,128)(2,1)}) custom-call(bf16[8,256,2048]{2,1,0:T(8,128)(2,1)} %get-tuple-element.37.cot_ref, f32[8,256,1408]{2,1,0:T(8,128)} %bitcast.119, bf16[2048,2048]{1,0:T(8,128)(2,1)} %bitcast.121, bf16[2048,1408]{1,0:T(8,128)(2,1)} %all-gather.6.cloned.1.call-done.w_ref, ...), custom_call_target="tpu_custom_call" | custom-call | flops 44999999488 | bytes 100000000 | tf_op jit(solution)/shard_map/feed_back/pallas_call | solution.py:852
  352.9 5.1 multiply_reduce_fusion
  358.1 2.7 fusion.11
  362.1 43.8 %project_back.1 = (bf16[2048,256]{1,0:T(8,128)(2,1)S(1)}, bf16[8,256,2048]{2,1,0:T(8,128)(2,1)}, bf16[256,2048]{1,0:T(8,128)(2,1)S(1)}) custom-call(bf16[256,2048]{1,0:T(8,128)(2,1)S(1)} %fusion.15.p_ref, bf16[2048,768]{1,0:T(8,128)(2,1)} %bitcast.122, bf16[2048,768]{1,0:T(8,128)(2,1)} %all-gather.8.cloned.1.call-done.d_ref, bf16[256,2048]{1,0:T(8,128)(2,1)} %bitcast.107, ...), custom_call_target="tpu_custom_call" | custom-call | flops 44999999488 | bytes 100000000 | tf_op jit(solution)/shard_map/project_back/pallas_call | solution.py:934
  406.0 1.1 copy.184
  407.3 3.6 all-to-all-start.3
  410.9 52.0 %attend_back.1 = (bf16[2048,384]{1,0:T(8,128)(2,1)}, f32[256,2048]{1,0:T(8,128)}) custom-call(bf16[2048,384]{1,0:T(8,128)(2,1)} %copy-done.5, s32[2048,1]{1,0:T(8,128)} %copy-done, s32[8,1,256]{2,1,0:T(1,128)} %bitcast.91, f32[2048,1]{1,0:T(8,128)} %copy-done.1, bf16[2048,256]{1,0:T(8,128)(2,1)} %copy-done.8, f32[2048,256]{1,0:T(8,128)} %get-tuple-element.43.refs_5_, ...), custom_call_target="tpu_custom_call" | custom-call | flops 44999999488 | bytes 100000000 | tf_op jit(solution)/shard_map/attend_back/pallas_call | solution.py:598
  462.9 0.9 copy-done.19
  463.9 1.6 slice_convert_fusion.1
  465.8 3.6 all-to-all-start.6
  469.3 10.0 %fusion.3 = bf16[2048,384]{1,0:T(8,128)(2,1)} fusion(bf16[2048,384]{1,0:T(8,128)(2,1)} %get-tuple-element.51.l_ref, bf16[2048,2048]{1,0:T(8,128)(2,1)} %bitcast.94, f32[2048]{0:T(1024)S(1)} %copy-done.3, f32[2048]{0:T(1024)S(1)} %bitcast.117), kind=kOutput, calls=%fused_computation.10 | convolution fusion | flops 3238789120 | bytes 11550720 | tf_op jit(solution)/shard_map/dot_general | solution.py:31
  479.3 2.6 all-to-all-done.6
  482.0 0.9 copy.167
  482.9 1.7 reshape.214
  484.6 4.3 all-to-all-start.5
  488.9 1.8 reduce-scatter.9.cloned.1.call-done
  490.8 52.2 %product_sum.3 = f32[256,2048]{1,0:T(8,128)} custom-call(bf16[2048,384]{1,0:T(8,128)(2,1)} %get-tuple-element.51.l_ref, bf16[2048,384]{1,0:T(8,128)(2,1)} %slice_select_fusion.w_ref.r_ref), custom_call_target="tpu_custom_call" | custom-call | flops 44999999488 | bytes 100000000 | tf_op jit(solution)/shard_map/product_sum/pallas_call | solution.py:287
  543.1 2.4 multiply_reduce_fusion.1
  545.7 2.2 fusion.6
  548.0 4.8 fusion.10
  552.8 1.6 convert_bitcast_fusion
  554.5 1.3 multiply_reduce_fusion.4
  556.0 1.9 concatenate.22
  557.9 3.5 all-to-all-start.4
  561.5 1.2 fusion.16
  563.6 0.9 copy.166
  564.5 1.7 reshape.210
  566.3 1.1 pad_maximum_fusion
  567.3 0.9 copy.165
  568.3 1.7 reshape.209
  570.0 2.6 all-to-all-done.4
  572.6 0.8 slice_reduce_fusion
  573.7 0.8 copy.179
  576.2 0.8 copy.178
  (129 shorter events, 10.6 us)
Async XLA Ops:
  9.2 9.2 %copy-start.23 = (bf16[64,5504]{1,0:T(8,128)(2,1)S(1)}, bf16[64,5504]{1,0:T(8,128)(2,1)}, u32[]{:S(2)}) copy-start(bf16[64,5504]{1,0:T(8,128)(2,1)} %param.20) | copy-start | bytes 2113540
  13.0 6.8 %copy-start.24 = (bf16[64,5504]{1,0:T(8,128)(2,1)S(1)}, bf16[64,5504]{1,0:T(8,128)(2,1)}, u32[]{:S(2)}) copy-start(bf16[64,5504]{1,0:T(8,128)(2,1)} %param.21) | copy-start | bytes 2113540
  13.0 16.5 %all-to-all-start = ((bf16[8,64,640]{2,1,0:T(8,128)(2,1)}), bf16[8,64,640]{2,1,0:T(8,128)(2,1)S(1)}, u32[]{:S(2)}, u32[]{:S(2)}) async-start(bf16[8,64,640]{2,1,0:T(8,128)(2,1)} %bitcast.5), calls=%async_computation | async-start | bytes 1310720 | tf_op jit(solution)/shard_map/all_to_all | solution.py:1016
  18.3 87.2 %all-gather.4.cloned.1.call-start = ((), (), s32[]{:S(2)}) async-start(), calls=%async_computation.11 | async-start | bytes 3276800 | tf_op jit(solution)/shard_map/all_gather | solution.py:968
  29.5 0.8 copy-start.21
  30.4 210.3 %all-gather.6.cloned.1.call-start = ((), (), s32[]{:S(2)}) async-start(), calls=%async_computation.12 | async-start | bytes 7208960 | tf_op jit(solution)/shard_map/all_gather | solution.py:968
  30.4 55.7 %copy-start.25 = (bf16[5504,64]{0,1:T(8,128)(2,1)S(1)}, bf16[5504,64]{0,1:T(8,128)(2,1)}, u32[]{:S(2)}) copy-start(bf16[5504,64]{0,1:T(8,128)(2,1)} %param.22) | copy-start | bytes 2113540
  87.5 4.7 copy-start.33
  88.6 16.1 %all-to-all-start.2 = ((bf16[8,64,768]{2,1,0:T(8,128)(2,1)}), bf16[8,64,768]{2,1,0:T(8,128)(2,1)S(1)}, u32[]{:S(2)}, u32[]{:S(2)}) async-start(bf16[8,64,768]{2,1,0:T(8,128)(2,1)} %pad_bitcast_fusion), calls=%async_computation.2 | async-start | bytes 1572864 | tf_op jit(solution)/shard_map/all_to_all | solution.py:1031
  92.1 200.0 %all-gather.8.cloned.1.call-start = ((), (), s32[]{:S(2)}) async-start(), calls=%async_computation.13 | async-start | bytes 3932160 | tf_op jit(solution)/shard_map/all_gather | solution.py:968
  92.3 24.1 %copy-start.4 = (s32[2048]{0:T(1024)}, s32[2048]{0:T(1024)S(1)}, u32[]{:S(2)}) copy-start(s32[2048]{0:T(1024)S(1)} %convert_reduce_fusion) | copy-start | bytes 24580
  93.2 23.1 %copy-start = (s32[2048,1]{1,0:T(8,128)}, s32[2048,1]{1,0:T(8,128)S(1)}, u32[]{:S(2)}) copy-start(s32[2048,1]{1,0:T(8,128)S(1)} %copy.154.sc_ref.refs_1_) | copy-start | bytes 24580
  94.0 22.3 %copy-start.1 = (f32[2048,1]{1,0:T(8,128)}, f32[2048,1]{1,0:T(8,128)S(1)}, u32[]{:S(2)}) copy-start(f32[2048,1]{1,0:T(8,128)S(1)} %compare_convert_fusion.edge_ref.refs_3_) | copy-start | bytes 24580
  104.7 0.9 copy-start.20
  107.8 43.2 %all-to-all-start.1 = ((bf16[8,256,256]{2,1,0:T(8,128)(2,1)}), bf16[8,256,256]{2,1,0:T(8,128)(2,1)S(1)}, u32[]{:S(2)}, u32[]{:S(2)}) async-start(bf16[8,256,256]{2,1,0:T(8,128)(2,1)} %bitcast.98), calls=%async_computation.1 | async-start | bytes 2097152 | tf_op jit(solution)/shard_map/all_to_all | solution.py:1036
  111.4 241.5 %reduce-scatter.5.cloned.1.call-start = ((), (), s32[]{:S(2)}) async-start(), calls=%async_computation.14 | async-start | bytes 3932160 | tf_op jit(solution)/shard_map/reduce_scatter | solution.py:972
  113.6 2.8 copy-start.2
  113.6 247.2 %copy-start.27 = (f32[2048]{0:T(1024)}, f32[2048]{0:T(1024)S(1)}, u32[]{:S(2)}) copy-start(f32[2048]{0:T(1024)S(1)} %get-tuple-element.110) | copy-start | bytes 24580
  147.9 1.2 copy-start.5
  149.0 1.0 copy-start.6
  150.0 1.0 copy-start.7
  152.1 46.1 %copy-start.11 = (bf16[1,256,2048]{2,1,0:T(8,128)(2,1)S(1)}, bf16[1,256,2048]{2,1,0:T(8,128)(2,1)}, u32[]{:S(2)}) copy-start(bf16[1,256,2048]{2,1,0:T(8,128)(2,1)} %param.12) | copy-start | bytes 3145732
  198.2 2.5 copy-start.9
  200.5 160.3 %copy-start.29 = (f32[256]{0:T(256)}, f32[256]{0:T(256)S(1)}, u32[]{:S(2)}) copy-start(f32[256]{0:T(256)S(1)} %add_rsqrt_fusion.1) | copy-start | bytes 3076
  292.0 170.9 %reduce-scatter.7.cloned.1.call-start = ((), (), s32[]{:S(2)}) async-start(), calls=%async_computation.15 | async-start | bytes 7208960 | tf_op jit(solution)/shard_map/reduce_scatter | solution.py:972
  358.0 2.8 copy-start.12
  358.0 2.9 copy-start.14
  358.1 3.3 copy-start.17
  361.3 0.8 copy-start.31
  405.9 1.3 copy-start.8
  407.3 55.6 %all-to-all-start.3 = ((bf16[256,8,256]{2,0,1:T(8,128)(2,1)}), bf16[256,8,256]{2,0,1:T(8,128)(2,1)S(1)}, u32[]{:S(2)}, u32[]{:S(2)}) async-start(bf16[256,8,256]{2,0,1:T(8,128)(2,1)} %bitcast.85), calls=%async_computation.5 | async-start | bytes 2097152 | tf_op jit(solution)/shard_map/all_to_all | solution.py:1061
  410.8 80.0 %reduce-scatter.9.cloned.1.call-start = ((), (), s32[]{:S(2)}) async-start(), calls=%async_computation.16 | async-start | bytes 1310720 | tf_op jit(solution)/shard_map/reduce_scatter | solution.py:972
  462.9 1.0 copy-start.19
  463.9 5.5 copy-start.3
  465.8 16.1 %all-to-all-start.6 = ((bf16[8,64,768]{2,1,0:T(8,128)(2,1)}), bf16[8,64,768]{2,1,0:T(8,128)(2,1)S(1)}, u32[]{:S(2)}, u32[]{:S(2)}) async-start(bf16[8,64,768]{2,1,0:T(8,128)(2,1)} %bitcast.31), calls=%async_computation.10 | async-start | bytes 1572864 | tf_op jit(solution)/shard_map/all_to_all | solution.py:977
  484.6 68.2 %all-to-all-start.5 = ((bf16[8,64,1408]{2,1,0:T(8,128)(2,1)}), bf16[8,64,1408]{2,1,0:T(8,128)(2,1)}, u32[]{:S(2)}, u32[]{:S(2)}) async-start(bf16[8,64,1408]{2,1,0:T(8,128)(2,1)} %bitcast.29), calls=%async_computation.9 | async-start | bytes 2883584 | tf_op jit(solution)/shard_map/all_to_all | solution.py:977
  488.9 65.6 %reduce-scatter.11.cloned.1.call-start = ((), (), s32[]{:S(2)}) async-start(), calls=%async_computation.17 | async-start | bytes 1966080 | tf_op jit(solution)/shard_map/reduce_scatter | solution.py:972
  490.8 57.1 %copy-start.18 = (bf16[1,256,2048]{2,1,0:T(8,128)(2,1)S(1)}, bf16[1,256,2048]{2,1,0:T(8,128)(2,1)}, u32[]{:S(2)}) copy-start(bf16[1,256,2048]{2,1,0:T(8,128)(2,1)} %param.23) | copy-start | bytes 3145732
  490.8 57.1 %copy-start.22 = (f32[256,2048]{1,0:T(8,128)S(1)}, f32[256,2048]{1,0:T(8,128)}, u32[]{:S(2)}) copy-start(f32[256,2048]{1,0:T(8,128)} %get-tuple-element.46) | copy-start | bytes 6291460
  543.1 2.6 copy-start.13
  543.1 4.9 copy-start.15
  545.5 2.5 copy-start.10
  545.5 2.5 copy-start.28
  545.5 2.5 copy-start.30
  545.5 2.5 copy-start.32
  552.8 3.2 copy-start.26
  557.9 14.6 %all-to-all-start.4 = ((bf16[8,64,640]{2,1,0:T(8,128)(2,1)}), bf16[8,64,640]{2,1,0:T(8,128)(2,1)S(1)}, u32[]{:S(2)}, u32[]{:S(2)}) async-start(bf16[8,64,640]{2,1,0:T(8,128)(2,1)} %bitcast.25), calls=%async_computation.8 | async-start | bytes 1310720 | tf_op jit(solution)/shard_map/all_to_all | solution.py:977
  564.5 1.7 copy-start.16
Sparse Core Ops, SparseCore 0:
  30.5 54.1 all-gather.3
  86.3 106.9 all-gather.5
  194.8 61.7 all-gather.7
  292.2 60.6 reduce-scatter.4
  355.0 102.2 reduce-scatter.6
  464.0 26.7 reduce-scatter.8
  493.2 35.2 reduce-scatter.10

commit v4 on v3

--- a/solution.py
+++ b/solution.py
@@ -142,34 +142,9 @@
     return [dma((Gather.COPIES,)), dma((Gather.COPIES,)), dma(())]
 
 
-def gather_kernel(x_ref, o_ref, send, recv, local):
-    _, sib, xn, yn, _, _ = neighbours()
-    greet([sib, xn, yn])
-    g = Gather(x_ref, o_ref, send, recv, local)
-    g.start()
-    g.turn()
-    g.rest()
-    g.across()
-    g.finish()
-
-
 ANY = pl.BlockSpec(memory_space=pl.ANY)
 LINKED = pl.CostEstimate(flops=45 * 10**9, bytes_accessed=10**8, transcendentals=0)
 WHOLE = pl.BlockSpec(memory_space=VMEM)
-
-
-def row_gather(x, cid):
-    rows, cols = x.shape
-    return pl.pallas_call(
-        gather_kernel,
-        out_shape=jax.ShapeDtypeStruct((8, rows, cols), x.dtype),
-        in_specs=[ANY],
-        out_specs=ANY,
-        scratch_shapes=gather_scratch(),
-        compiler_params=pltpu.CompilerParams(collective_id=cid, has_side_effects=True),
-        cost_estimate=LINKED,
-        name="row_gather",
-    )(x).reshape(8 * rows, cols)
 
 
 class Sum:
@@ -241,10 +216,19 @@
     ]
 
 
-def product_sum_kernel(turned, l_ref, r_ref, o_ref, out, mine, got, ex, ey, fx, fy, send, recv):
-    _, sib, xn, yn, _, _ = neighbours()
+def product_sum_kernel(turned, normed, l_ref, r_ref, *refs):
+    if normed:
+        x_ref, gain_ref, o_ref, act, out, mine, got, ex, ey, fx, fy, send, recv = refs
+        _, sib, xn, yn, _, _ = neighbours()
+        greet([sib, xn, yn])
+    else:
+        x_ref, gain_ref, base_ref, e_ref, o_ref, e_out_ref = refs[:6]
+        out, mine, got, ex, ey, fx, fy, send, recv = refs[6:15]
+        greet(everyone())
+        moved = Exchange(e_ref, e_out_ref, *refs[15:])
+        moved.start()
     rows, cols = o_ref.shape
-    greet([sib, xn, yn])
+    depth = l_ref.shape[1]
     s = Sum(mine, got, out.at.__getitem__, ex, ey, fx, fy, o_ref, send, recv)
 
     def block(q, to):
@@ -253,7 +237,7 @@
         @pl.loop(0, cols // 256)
         def _(n):
             here = pl.ds(pl.multiple_of(n * 256, 256), 256)
-            part = dot_nt(left, r_ref[here, :]) if turned else dot(left, r_ref[:, here])
+            part = dot_nt(left, r_ref[here, :depth]) if turned else dot(left, r_ref[:, here])
             to[:, here] = part.astype(BF16)
 
     def away(k):
@@ -277,25 +261,66 @@
     home(3)
     s.own()
     s.finish()
-
-
-def product_sum(left, right, turned, cid):
+    if not normed:
+        @pl.loop(0, rows // 64)
+        def _(n):
+            some = pl.ds(pl.multiple_of(n * 64, 64), 64)
+            value = x_ref[some, :].astype(F32)
+            factor = lax.rsqrt(jnp.sum(value * value, 1, keepdims=True) * (1.0 / cols) + EPS)
+            value = value * factor
+            inner = o_ref[some, :] * gain_ref[...]
+            along = jnp.sum(inner * value, 1, keepdims=True) * (1.0 / cols)
+            o_ref[some, :] = base_ref[some, :] + factor * (inner - value * along)
+
+        moved.finish()
+    else:
+        @pl.loop(0, rows // 64)
+        def _(n):
+            some = pl.ds(pl.multiple_of(n * 64, 64), 64)
+            value = x_ref[some, :].astype(F32) + o_ref[some, :]
+            factor = lax.rsqrt(jnp.sum(value * value, 1, keepdims=True) * (1.0 / cols) + EPS)
+            o_ref[some, :] = value
+            act[some, :] = (value * factor * gain_ref[...]).astype(BF16)
+
+
+def product_sum(left, right, turned, cid, x, gain, base=None, moved=None):
+    depth = left.shape[1]
     if lax.axis_size("fsdp") != 8:
-        part = (dot_nt(left, right) if turned else dot(left, right)).astype(BF16)
-        return lax.psum_scatter(part, "fsdp", scatter_dimension=0, tiled=True).astype(F32)
+        part = (dot_nt(left, right[:, :depth]) if turned else dot(left, right)).astype(BF16)
+        part = lax.psum_scatter(part, "fsdp", scatter_dimension=0, tiled=True).astype(F32)
+        if base is not None:
+            x = x.astype(F32)
+            part, _ = rms_back(part, x, rms_apply(x, gain)[1], gain)
+            return base + part, lax.all_to_all(moved, "fsdp", 0, 0, tiled=True)
+        part = part + x.astype(F32)
+        act = rms_apply(part, gain)[0].astype(BF16)
+        return part, act
     rows, cols = left.shape[0] // 8, right.shape[0 if turned else 1]
-    return pl.pallas_call(
-        functools.partial(product_sum_kernel, turned),
-        out_shape=jax.ShapeDtypeStruct((rows, cols), F32),
-        in_specs=[WHOLE, WHOLE],
-        out_specs=WHOLE,
-        scratch_shapes=[VMEM((4, rows, cols), BF16)] + sum_scratch(rows, cols),
+    args, specs = [left, right, x, gain[None, :]], [WHOLE] * 4
+    outs, out_specs = [jax.ShapeDtypeStruct((rows, cols), F32)], [WHOLE]
+    scratch = [VMEM((4, rows, cols), BF16)] + sum_scratch(rows, cols)
+    if base is None:
+        outs.append(jax.ShapeDtypeStruct((rows, cols), BF16))
+        out_specs.append(WHOLE)
+    else:
+        args += [base, moved]
+        specs += [WHOLE, ANY]
+        outs.append(jax.ShapeDtypeStruct(moved.shape, moved.dtype))
+        out_specs.append(ANY)
+        scratch += exchange_scratch()
+    got = pl.pallas_call(
+        functools.partial(product_sum_kernel, turned, base is None),
+        out_shape=outs,
+        in_specs=specs,
+        out_specs=out_specs,
+        scratch_shapes=scratch,
         compiler_params=pltpu.CompilerParams(
             collective_id=cid, has_side_effects=True, vmem_limit_bytes=56 << 20
         ),
         cost_estimate=LINKED,
         name="product_sum",
-    )(left, right)
+    )(*args)
+    return got
 
 
 def start_kernel(x_ref, a_ref, ox_ref, oa_ref, send, recv, local, a_send, a_recv, keep):
@@ -347,6 +372,12 @@
     return (seg_rows == seg_cols) & (cols <= rows)
 
 
+def later_or_same(seg_keys, seg_queries):
+    keys = lax.broadcasted_iota(jnp.int32, (BLK, BLK), 0)
+    queries = lax.broadcasted_iota(jnp.int32, (BLK, BLK), 1)
+    return (seg_keys == seg_queries) & (keys <= queries)
+
+
 def spot(b):
     return pl.ds(b * BLK, BLK)
 
@@ -376,35 +407,79 @@
             vx[h, here, wide:] = (first * edge).astype(BF16)
 
 
-def attend_kernel(
-    heads, wide, blocks, x_ref, gain_ref, w_ref, sc_ref, sr_ref, edge_ref,
-    qkv_ref, att_ref, full_ref, den_ref, xs, act, load, qz, vx,
-):
+def attend_kernel(heads, wide, blocks, linked, *refs):
+    x_ref, gain_ref, mats_ref, sc_ref, sr_ref, edge_ref = refs[:6]
+    refs = refs[6:]
+    if linked:
+        dt_ref, cot_ref = refs[:2]
+        qkv_ref, att_ref, full_ref, den_ref, act_ref, own_dt_ref, own_out_ref, cot_all_ref = refs[2:10]
+        xs, act, w, load, save, load_w, qz, vx, dt_send, dt_recv, out_send, out_recv, stay = refs[10:23]
+        me = lax.axis_index("fsdp")
+        part = heads * wide
+
+        def rows_for(to):
+            return mats_ref.at[pl.ds(pl.multiple_of(to * part, part), part), qkv_ref.shape[1] :]
+
+        here = own_out_ref.at[:, pl.ds(pl.multiple_of(me * part, part), part)]
+        others = everyone()
+        greet(others)
+        gather = Gather(cot_ref, cot_all_ref, *refs[23:])
+        gather.start()
+        turns = {blocks - 3: gather.rest, blocks - 1: gather.across}
+        moves = []
+        for r, to in enumerate(others):
+            moves.append(push(rows_for(to), here, out_send.at[r], out_recv.at[r], to))
+            moves.append(push(dt_ref.at[to], own_dt_ref.at[me], dt_send.at[r], dt_recv.at[r], to))
+        moves.append(pltpu.make_async_copy(rows_for(me), here, stay.at[0]))
+        moves.append(pltpu.make_async_copy(dt_ref.at[me], own_dt_ref.at[me], stay.at[1]))
+        for copy in moves:
+            copy.start()
+    else:
+        qkv_ref, att_ref, full_ref, den_ref, act_ref, xs, act, w, load, save, load_w, qz, vx = refs
+        moves, turns = [], {}
     width = x_ref.shape[1]
+    weights = pltpu.make_async_copy(mats_ref.at[:, : qkv_ref.shape[1]], w, load_w)
+    weights.start()
 
     def fetch(b):
         return pltpu.make_async_copy(x_ref.at[moving(b)], xs.at[lax.rem(b, 2)], load.at[lax.rem(b, 2)])
 
+    def keep(b):
+        return pltpu.make_async_copy(act.at[lax.rem(b, 2)], act_ref.at[moving(b)], save.at[lax.rem(b, 2)])
+
     fetch(0).start()
+    weights.wait()
 
     @pl.loop(0, blocks)
     def _(b):
+        slot = lax.rem(b, 2)
+
         @pl.when(b < blocks - 1)
         def _():
             fetch(b + 1).start()
 
         fetch(b).wait()
 
+        @pl.when(b >= 2)
+        def _():
+            keep(b - 2).wait()
+
         @pl.loop(0, BLK // 64)
         def _(n):
             some = pl.ds(pl.multiple_of(n * 64, 64), 64)
-            x = xs[lax.rem(b, 2), some, :].astype(F32)
+            x = xs[slot, some, :].astype(F32)
             factor = lax.rsqrt(jnp.sum(x * x, 1, keepdims=True) * (1.0 / width) + EPS)
-            act[some, :] = (x * factor * gain_ref[...]).astype(BF16)
-
-        qkv_ref[moving(b), :] = dot(act[...], w_ref[...]).astype(BF16)
+            act[slot, some, :] = (x * factor * gain_ref[...]).astype(BF16)
+
+        keep(b).start()
+        qkv_ref[moving(b), :] = dot(act[slot], w[...]).astype(BF16)
+
+    keep(blocks - 2).wait()
+    keep(blocks - 1).wait()
 
     lay_out(heads, wide, blocks, qkv_ref, edge_ref, qz, vx)
+    if linked:
+        gather.turn()
     one = (lax.broadcasted_iota(jnp.int32, (BLK, wide), 1) == 0).astype(BF16)
     for b in range(blocks):
         here = spot(b)
@@ -435,16 +510,23 @@
             att_ref[here, entry] = att.astype(BF16)
             full_ref[here, entry] = att
             den_ref[here, h : h + 1] = den
+        if b in turns:
+            turns[b]()
+    for copy in moves:
+        copy.wait()
+    if linked:
+        gather.finish()
 
 
 def attend_back_kernel(heads, wide, blocks, with_sum, *refs):
     qkv_ref, sc_ref, sr_ref, edge_ref, da_ref, full_ref, den_ref = refs[:7]
     refs = refs[7:]
     if with_sum:
-        part_ref, d_ref, o_ref, qz, vx, near_dn, far_dn, qk_acc, v_acc = refs[:9]
-        mine, got, ex, ey, fx, fy, send, recv, local = refs[9:]
-        _, sib, xn, yn, _, flip = neighbours()
-        greet([sib, xn, yn])
+        part_ref, e_ref, c_ref, d_ref, o_ref, e_out_ref, c_out_ref = refs[:7]
+        qz, vx, kt, near_dn, far_dn, qk_acc, v_acc = refs[7:14]
+        mine, got, ex, ey, fx, fy, send, recv, local = refs[14:23]
+        flip = neighbours()[5]
+        greet(everyone())
         s = Sum(
             mine, got, lambda k: part_ref.at[neighbours()[(4, 2, 3, 0)[k]] + flip], ex, ey, fx, fy, o_ref, send, recv
         )
@@ -452,6 +534,9 @@
         for k in range(4):
             s.swaps[k].start()
             loads[k].start()
+        moved = [Exchange(c_ref, c_out_ref, *refs[26:]), Exchange(e_ref, e_out_ref, *refs[23:26])]
+        for one_move in moved:
+            one_move.start()
 
         def first():
             loads[0].wait()
@@ -469,9 +554,14 @@
 
         turns = {blocks - 1: first, blocks - 2: second, blocks - 3: s.second, blocks - 4: fourth}
     else:
-        d_ref, qz, vx, near_dn, far_dn, qk_acc, v_acc = refs
+        d_ref, qz, vx, kt, near_dn, far_dn, qk_acc, v_acc = refs
         turns = {}
     lay_out(heads, wide, blocks, qkv_ref, edge_ref, qz, vx)
+
+    @pl.loop(0, blocks)
+    def _(b):
+        kt[b] = qkv_ref[moving(b), heads * wide :].astype(F32).T.astype(BF16)
+
     qk_acc[...] = jnp.zeros_like(qk_acc)
     v_acc[...] = jnp.zeros_like(v_acc)
     one = (lax.broadcasted_iota(jnp.int32, (BLK, wide), 1) == 0).astype(F32)
@@ -494,42 +584,42 @@
 
         far = far_dn if b == blocks - 1 else near_dn
 
-        def pair(c, grads, values, mask):
-            keys = qkv_ref[c, heads * wide :]
-            t = dot_nt(qz[b], keys) + 1.0
-            out, parts = [], []
+        def pair(c, keys_t, grads, values, mask):
+            t = dot_nt(qkv_ref[c, heads * wide :], qz[b]) + 1.0
+            parts = []
             for h in range(heads):
                 rows = slice(h * BLK, (h + 1) * BLK)
-                t_h = t[rows]
+                t_h = t[:, rows]
                 w = t_h * t_h + 1.0
-                ds = dot_nt(grads[rows, :], values(h)) * t_h
+                ds = dot_nt(values(h), grads[rows, :]) * t_h
                 if mask is not None:
                     w = jnp.where(mask, w, 0.0)
                     ds = jnp.where(mask, ds, 0.0)
-                ds = ds.astype(BF16)
-                parts.append(ds)
-                v_acc[c, h * wide : (h + 1) * wide] += dot_tn(w.astype(BF16), grads[rows, :wide])
-                out.append(dot(ds, keys))
-            qk_acc[c, :] += dot_tn(jnp.concatenate(parts, 0), qz[b])
-            return out
+                parts.append(ds.astype(BF16))
+                v_acc[c, h * wide : (h + 1) * wide] += dot(w.astype(BF16), grads[rows, :wide])
+            ds = jnp.concatenate(parts, 1)
+            qk_acc[c, :] += dot(ds, qz[b])
+            return dot(keys_t, ds)
 
         def step(c, dq):
             at = moving(c)
-            return tuple(
-                a + g for a, g in zip(dq, pair(at, far, lambda h: vx[h, at, :], None))
-            )
-
-        dq = lax.fori_loop(0, b, step, (jnp.zeros((BLK, 128), F32),) * heads)
+            return dq + pair(at, kt[c], far, lambda h: vx[h, at, :], None)
+
+        dq = lax.fori_loop(0, b, step, jnp.zeros((128, heads * BLK), F32))
         if b == 0:
             v_acc[here, :] = v_acc[here, :] * edge_ref[here, :]
-        near = pair(
-            here, near_dn,
+        dq = dq + pair(
+            here, kt[b], near_dn,
             lambda h: jnp.concatenate([qkv_ref[here, h * wide : (h + 1) * wide], unit], 1),
-            same_or_later(sc_ref[here, :], sr_ref[b]),
+            later_or_same(sc_ref[here, :], sr_ref[b]),
         )
-        total = jnp.zeros((BLK, 128), F32)
+        row = lax.broadcasted_iota(jnp.int32, (128, BLK), 0)
+        total = jnp.zeros((128, BLK), F32)
         for h in range(heads):
-            total = jnp.where(lanes_of(h, heads), dq[h] + near[h], total)
+            at = (heads + h) * FEAT
+            own = (row >= at) & (row < at + FEAT)
+            total = jnp.where(own, dq[:, h * BLK : (h + 1) * BLK], total)
+        total = total.T
         back = pltpu.roll(total, 128 - heads * FEAT, 1) * 0.5
         d_ref[here, heads * wide :] = back.astype(BF16)
         if b in turns:
@@ -541,6 +631,8 @@
         d_ref[here, heads * wide :] = (queries + 2.0 * qk_acc[here, :]).astype(BF16)
     if with_sum:
         s.finish()
+        for one_move in moved:
+            one_move.finish()
 
 
 def marks(seg):
@@ -549,29 +641,61 @@
     return seg[:, None], seg.reshape(length // BLK, 1, BLK), edge[:, None]
 
 
-def attend(x_all, gain, w_qkv, seg, heads, wide):
-    length, columns = x_all.shape[0], w_qkv.shape[1]
+def attend(x_all, gain, mats, seg, heads, wide, dt, cot, cid):
+    length, width = x_all.shape
     blocks = length // BLK
-    width = heads * wide
-    return pl.pallas_call(
-        functools.partial(attend_kernel, heads, wide, blocks),
-        out_shape=(
-            jax.ShapeDtypeStruct((length, columns), BF16),
-            jax.ShapeDtypeStruct((length, width), BF16),
-            jax.ShapeDtypeStruct((length, width), F32),
-            jax.ShapeDtypeStruct((length, heads), F32),
-        ),
-        in_specs=[ANY] + [WHOLE] * 5,
-        out_specs=(WHOLE,) * 4,
-        scratch_shapes=[VMEM((2, BLK, x_all.shape[1]), BF16), VMEM((BLK, x_all.shape[1]), BF16),
-                        pltpu.SemaphoreType.DMA((2,)), VMEM((blocks, heads * BLK, 128), BF16), VMEM((heads, length, 2 * wide), BF16)],
-        compiler_params=pltpu.CompilerParams(vmem_limit_bytes=48 << 20),
-        cost_estimate=pl.CostEstimate(flops=2 * 10**10, bytes_accessed=4 * 10**7, transcendentals=0),
+    part = heads * wide
+    columns = mats.shape[1] - part
+    linked = lax.axis_size("fsdp") == 8
+    dma = pltpu.SemaphoreType.DMA
+    args = [x_all, gain[None, :], mats, *marks(seg)]
+    specs = [ANY, WHOLE, ANY, WHOLE, WHOLE, WHOLE]
+    outs = [
+        jax.ShapeDtypeStruct((length, columns), BF16),
+        jax.ShapeDtypeStruct((length, part), BF16),
+        jax.ShapeDtypeStruct((length, part), F32),
+        jax.ShapeDtypeStruct((length, heads), F32),
+        jax.ShapeDtypeStruct((length, width), BF16),
+    ]
+    out_specs = [WHOLE] * 4 + [ANY]
+    scratch = [
+        VMEM((2, BLK, width), BF16), VMEM((2, BLK, width), BF16), VMEM((width, columns), BF16),
+        dma((2,)), dma((2,)), dma(()),
+        VMEM((blocks, heads * BLK, 128), BF16), VMEM((heads, length, 2 * wide), BF16),
+    ]
+    params = dict(vmem_limit_bytes=48 << 20)
+    if linked:
+        args += [dt, cot]
+        specs += [ANY, ANY]
+        outs += [
+            jax.ShapeDtypeStruct(dt.shape, BF16),
+            jax.ShapeDtypeStruct((part, width), BF16),
+            jax.ShapeDtypeStruct((8,) + cot.shape, BF16),
+        ]
+        out_specs += [ANY] * 3
+        scratch += [dma((7,))] * 4 + [dma((2,))] + gather_scratch()
+        params.update(collective_id=cid, has_side_effects=True)
+    got = pl.pallas_call(
+        functools.partial(attend_kernel, heads, wide, blocks, linked),
+        out_shape=outs,
+        in_specs=specs,
+        out_specs=out_specs,
+        scratch_shapes=scratch,
+        compiler_params=pltpu.CompilerParams(**params),
+        cost_estimate=LINKED,
         name="attend",
-    )(x_all, gain[None, :], w_qkv, *marks(seg))
-
-
-def attend_back(qkv, seg, heads, wide, da, full, den, part, cid):
+    )(*args)
+    if linked:
+        return *got[:7], got[7].reshape(length, width)
+    return (
+        *got,
+        lax.all_to_all(dt, "fsdp", 0, 0, tiled=True),
+        lax.all_to_all(mats[:, columns:], "fsdp", 0, 1, tiled=True),
+        lax.all_gather(cot, "fsdp", axis=0, tiled=True),
+    )
+
+
+def attend_back(qkv, seg, heads, wide, da, full, den, part, moved, across, cid):
     length, columns = qkv.shape
     blocks = length // BLK
     width = heads * wide
@@ -581,15 +705,19 @@
     outs = [jax.ShapeDtypeStruct((length, columns), BF16)]
     scratch = [
         VMEM((blocks, heads * BLK, 128), BF16), VMEM((heads, length, 2 * wide), BF16),
-        VMEM((heads * BLK, 2 * wide), BF16), VMEM((heads * BLK, 2 * wide), BF16),
+        VMEM((blocks, 128, BLK), BF16), VMEM((heads * BLK, 2 * wide), BF16), VMEM((heads * BLK, 2 * wide), BF16),
         VMEM((length, 128), F32), VMEM((length, width), F32),
     ]
     if with_sum:
         rows, cols = length // 8, part.shape[1]
-        args.append(part.reshape(8, rows, cols))
-        specs.append(ANY)
-        outs.append(jax.ShapeDtypeStruct((rows, cols), F32))
-        scratch += sum_scratch(rows, cols) + [pltpu.SemaphoreType.DMA((4,))]
+        args += [part.reshape(8, rows, cols), moved, across]
+        specs += [ANY] * 3
+        outs += [
+            jax.ShapeDtypeStruct((rows, cols), F32),
+            jax.ShapeDtypeStruct(moved.shape, moved.dtype),
+            jax.ShapeDtypeStruct((8, across.shape[0], across.shape[1] // 8), across.dtype),
+        ]
+        scratch += sum_scratch(rows, cols) + [pltpu.SemaphoreType.DMA((4,))] + 2 * exchange_scratch()
         params = pltpu.CompilerParams(
             vmem_limit_bytes=60 << 20, collective_id=cid, has_side_effects=True
         )
@@ -599,15 +727,53 @@
         functools.partial(attend_back_kernel, heads, wide, blocks, with_sum),
         out_shape=outs,
         in_specs=specs,
-        out_specs=[WHOLE] * len(outs),
+        out_specs=[WHOLE, WHOLE, ANY, ANY][: len(outs)],
         scratch_shapes=scratch,
         compiler_params=params,
         cost_estimate=LINKED,
         name="attend_back",
     )(*args)
     if with_sum:
-        return got
-    return got[0], lax.psum_scatter(part, "fsdp", scatter_dimension=0, tiled=True).astype(F32)
+        return *got[:3], got[3].reshape(-1, got[3].shape[2])
+    return (
+        got[0],
+        lax.psum_scatter(part, "fsdp", scatter_dimension=0, tiled=True).astype(F32),
+        lax.all_to_all(moved, "fsdp", 0, 0, tiled=True),
+        lax.all_to_all(across, "fsdp", 1, 0, tiled=True),
+    )
+
+
+class Exchange:
+    def __init__(self, x_ref, o_ref, send, recv, local):
+        me = lax.axis_index("fsdp")
+        cols = o_ref.shape[2]
+
+        def block(to):
+            if len(x_ref.shape) == 3:
+                return x_ref.at[to]
+            return x_ref.at[:, pl.ds(pl.multiple_of(to * cols, cols), cols)]
+
+        self.copies = [
+            push(block(to), o_ref.at[me], send.at[r], recv.at[r], to) for r, to in enumerate(everyone())
+        ] + [pltpu.make_async_copy(block(me), o_ref.at[me], local)]
+
+    def start(self):
+        for copy in self.copies:
+            copy.start()
+
+    def finish(self):
+        for copy in self.copies:
+            copy.wait()
+
+
+def exchange_scratch():
+    dma = pltpu.SemaphoreType.DMA
+    return [dma((7,)), dma((7,)), dma(())]
+
+
+def everyone():
+    me = lax.axis_index("fsdp")
+    return [lax.rem(me + r, 8) for r in range(1, 8)]
 
 
 def tiles(cols):
@@ -628,107 +794,100 @@
 
 
 def feed_kernel(
-    ff, cot_ref, act_ref, w_ref, cot_all_ref, gu_ref, hid_ref, grad_ref,
-    acts, gus, hid, cots, acc, load, save_gu, save_hid, save_cot, send, recv, local,
+    ff, cot_ref, act_ref, w_ref, act_all_ref, gu_ref, hid_ref, grad_ref,
+    acts, gus, hid, cots, acc, load, save_gu, save_hid, save_act, send, recv, local,
 ):
     me, sib, xn, yn, dg, flip = neighbours()
-    rows = cot_ref.shape[0]
+    rows = act_ref.shape[0]
     main = ff // 128 * 128
     tail = ff - main
+    order = [me, sib, xn, yn, xn + flip, yn + flip, dg, dg + flip]
+    cot_load = pltpu.make_async_copy(cot_ref, cots, load)
+    cot_load.start()
     greet([sib, xn, yn])
-    g = Gather(cot_ref, cots, send, recv, local)
+    g = Gather(act_ref, acts, send, recv, local)
     g.start()
 
-    def at(b):
-        return pl.ds(pl.multiple_of(b * rows, rows), rows)
-
-    def fetch(b):
-        return pltpu.make_async_copy(act_ref.at[at(b)], acts.at[lax.rem(b, 2)], load.at[lax.rem(b, 2)])
-
-    def keep_gu(b):
-        return pltpu.make_async_copy(gus.at[lax.rem(b, 2)], gu_ref.at[at(b)], save_gu.at[lax.rem(b, 2)])
-
-    fetch(0).start()
-
-    def work(lo, hi):
-        @pl.loop(lo, hi)
-        def _(b):
-            slot = lax.rem(b, 2)
-
-            @pl.when(b < 7)
-            def _():
-                fetch(b + 1).start()
-
-            fetch(b).wait()
-
-            @pl.when(b >= 2)
-            def _():
-                keep_gu(b - 2).wait()
-
-            gu = gus.at[slot]
-            for tile in tiles(w_ref.shape[1]):
-                gu[:, tile] = dot(acts[slot], w_ref[:, tile])
-            hid[b, :, :main] = gated(gu[:, :main], gu[:, main : 2 * main]).astype(BF16)
-            last = gu[:, 2 * main :]
-            value = gated(last, pltpu.roll(last, 128 - tail, 1))
-            hid[b, :, main:] = jnp.where(lane_index(rows) < tail, value, 0.0).astype(BF16)
-            keep_gu(b).start()
-
-    work(0, 5)
-    g.turn()
-    work(5, 8)
-    keep_gu(6).wait()
-    keep_gu(7).wait()
-    store = pltpu.make_async_copy(hid, hid_ref, save_hid)
-    store.start()
+    def keep_gu(k):
+        at = pl.ds(pl.multiple_of(order[k] * rows, rows), rows)
+        return pltpu.make_async_copy(gus.at[k % 2], gu_ref.at[at], save_gu.at[k % 2])
+
+    def work(k):
+        q = order[k]
+        if k >= 2:
+            keep_gu(k - 2).wait()
+        gu = gus.at[k % 2]
+        for tile in tiles(w_ref.shape[1]):
+            gu[:, tile] = dot(acts[q], w_ref[:, tile])
+        hid[q, :, :main] = gated(gu[:, :main], gu[:, main : 2 * main]).astype(BF16)
+        last = gu[:, 2 * main :]
+        value = gated(last, pltpu.roll(last, 128 - tail, 1))
+        hid[q, :, main:] = jnp.where(lane_index(rows) < tail, value, 0.0).astype(BF16)
+        keep_gu(k).start()
+
+    def product(first, second, here):
+        return dot_tn(cots[first, :, here], hid[first]) + dot_tn(cots[second, :, here], hid[second])
 
     def add(first, second, start):
         @pl.loop(0, acc.shape[0] // 256)
         def _(n):
             here = pl.ds(pl.multiple_of(n * 256, 256), 256)
-            value = dot_tn(cots[first, :, here], hid[first]) + dot_tn(cots[second, :, here], hid[second])
+            value = product(first, second, here)
             acc[here, :] = value if start else acc[here, :] + value
 
+    g.keep.wait()
+    work(0)
     g.whole.wait_recv()
-    g.keep.wait()
+    work(1)
+    g.turn()
+    cot_load.wait()
+    add(me, sib, True)
     g.rest()
-    add(me, sib, True)
-    g.across()
+    work(2)
+    work(3)
     for k in range(4):
         g.core[k].wait_recv()
+    work(4)
+    g.across()
+    work(5)
     add(xn, xn + flip, False)
     add(yn, yn + flip, False)
+    work(6)
     g.core[4].wait_recv()
     g.core[5].wait_recv()
-    store_cot = pltpu.make_async_copy(cots, cot_all_ref, save_cot)
-    store_cot.start()
+    store_act = pltpu.make_async_copy(acts, act_all_ref, save_act)
+    store_act.start()
+    work(7)
+    store = pltpu.make_async_copy(hid, hid_ref, save_hid)
+    store.start()
 
     @pl.loop(0, acc.shape[0] // 256)
     def _(n):
         here = pl.ds(pl.multiple_of(n * 256, 256), 256)
-        value = dot_tn(cots[dg, :, here], hid[dg]) + dot_tn(cots[dg + flip, :, here], hid[dg + flip])
-        grad_ref[here, :] = (acc[here, :] + value).astype(BF16)
-
+        grad_ref[here, :] = (acc[here, :] + product(dg, dg + flip, here)).astype(BF16)
+
+    keep_gu(6).wait()
+    keep_gu(7).wait()
     g.sent()
     store.wait()
-    store_cot.wait()
-
-
-def feed(cot, act, w_gu, ff, cid):
+    store_act.wait()
+
+
+def feed(cot_all, act, w_gu, ff, cid):
     main = ff // 128 * 128
     tail = ff - main
     hid_cols = main + -(-tail // 128) * 128
     if lax.axis_size("fsdp") != 8:
-        cot_all = lax.all_gather(cot, "fsdp", axis=0, tiled=True)
+        act = lax.all_gather(act, "fsdp", axis=0, tiled=True)
         gu = dot(act, w_gu)
         gate = jnp.concatenate([gu[:, :main], gu[:, 2 * main : 2 * main + tail]], 1)
         up = jnp.concatenate([gu[:, main : 2 * main], gu[:, 2 * main + tail : 2 * ff]], 1)
         hidden = jnp.pad(gated(gate, up), ((0, 0), (0, hid_cols - ff))).astype(BF16)
-        return cot_all, gu, hidden, dot_tn(cot_all, hidden).astype(BF16)
-    rows, width = cot.shape
+        return act, gu, hidden, dot_tn(cot_all, hidden).astype(BF16)
+    rows, width = act.shape
     gu_cols = w_gu.shape[1]
     dma = pltpu.SemaphoreType.DMA
-    cot_all, gu, hidden, grad = pl.pallas_call(
+    act_all, gu, hidden, grad = pl.pallas_call(
         functools.partial(feed_kernel, ff),
         out_shape=(
             jax.ShapeDtypeStruct((8, rows, width), BF16),
@@ -739,17 +898,17 @@
         in_specs=[ANY, ANY, WHOLE],
         out_specs=(ANY, ANY, ANY, WHOLE),
         scratch_shapes=[
-            VMEM((2, rows, width), BF16), VMEM((2, rows, gu_cols), F32), VMEM((8, rows, hid_cols), BF16),
+            VMEM((8, rows, width), BF16), VMEM((2, rows, gu_cols), F32), VMEM((8, rows, hid_cols), BF16),
             VMEM((8, rows, width), BF16), VMEM((width, hid_cols), F32),
-            dma((2,)), dma((2,)), dma(()), dma(()),
+            dma(()), dma((2,)), dma(()), dma(()),
         ] + gather_scratch(),
         compiler_params=pltpu.CompilerParams(
             collective_id=cid, has_side_effects=True, vmem_limit_bytes=56 << 20
         ),
         cost_estimate=LINKED,
         name="feed",
-    )(cot, act, w_gu)
-    return cot_all.reshape(-1, width), gu, hidden.reshape(-1, hid_cols), grad
+    )(cot_all.reshape(8, rows, width), act, w_gu)
+    return act_all.reshape(-1, width), gu, hidden.reshape(-1, hid_cols), grad
 
 
 def feed_back_kernel(
@@ -953,12 +1112,6 @@
     return att, part.reshape(8 * rows, width), grad
 
 
-def row_all(part, cid):
-    if lax.axis_size("fsdp") == 8:
-        return row_gather(part, cid)
-    return lax.all_gather(part, "fsdp", axis=0, tiled=True)
-
-
 def group(arrays, groups):
     parts = jnp.concatenate([a.reshape(a.shape[0], groups, -1) for a in arrays], -1)
     return jnp.transpose(parts, (1, 0, 2))
@@ -1005,6 +1158,9 @@
     qkv_cols = v_own + 128
     att_cols = qkv_cols + v_own
 
+    def blocked(a):
+        return a.reshape(n_f, a.shape[0] // n_f, a.shape[1])
+
     def each(vec):
         return jnp.broadcast_to(vec[:, None, None], (rows, n_f, 1))
 
@@ -1017,8 +1173,7 @@
     main = ff_own // 128 * 128
 
     def halves(a):
-        a = a.reshape(rows, n_f, ff_own)
-        return a[:, :, :main], a[:, :, main:]
+        return a[:, : n_f * main].reshape(rows, n_f, main), a[:, n_f * main :].reshape(rows, n_f, -1)
 
     (gate_main, gate_tail), (up_main, up_tail) = halves(w_gate), halves(w_up)
     empty = jnp.zeros((rows, n_f, 128), BF16)
@@ -1027,26 +1182,18 @@
     )
     x_all, gu_part = start_exchange(x, gu, 0)
     w_gu = over_rows(gu_part)
-    dt = group([w_down.T, empty[:, :, : -ff_own % 128]], n_f)
-    w_dt = over_rows(lax.all_to_all(after(dt, x_all), "fsdp", 0, 0, tiled=True))
+    dt = group([*halves(w_down.T), empty[:, :, : -ff_own % 128]], n_f)
     gain_one = attn[:, gain_at].astype(F32)
     gain_two = attn[:, gain_at + 1].astype(F32)
-    keep = (jnp.arange(qkv_cols) < used)[None, :]
-    w_qkv = jnp.where(keep, attn[:, :qkv_cols], jnp.zeros((), BF16))
-    w_o = lax.all_to_all(attn[:, qkv_cols:], "fsdp", 0, 1, tiled=True)
-
     places = jnp.arange(length, dtype=jnp.int32)
     seg = jnp.sum((doc_starts[0][None, :] <= places[:, None]).astype(jnp.int32), 1)
-
-    normed_one, _ = rms_apply(x_all.astype(F32), gain_one)
-    act_one = normed_one.astype(BF16)
-    qkv, mixed, full, den = attend(x_all, gain_one, w_qkv, seg, heads, wide)
-    x_f = x.astype(F32)
-    resid = x_f + product_sum(mixed, w_o, False, 2)
-    normed_two, factor_two = rms_apply(resid, gain_two)
-    act_two = row_all(normed_two.astype(BF16), 3)
-
-    cot_all, gate_up, hidden, g_dt = feed(cot, act_two, w_gu, ff_own, 1)
+    qkv, mixed, full, den, act_one, dt_part, w_o, cot_all = attend(
+        x_all, gain_one, attn, seg, heads, wide, dt, cot, 3
+    )
+    w_dt = over_rows(dt_part)
+    resid, act_two = product_sum(mixed, w_o, False, 2, x, gain_two)
+    factor_two = lax.rsqrt(jnp.mean(resid * resid, -1, keepdims=True) + EPS)
+    act_two, gate_up, hidden, g_dt = feed(cot_all, act_two, w_gu, ff_own, 1)
     d_act_two, g_gu = feed_back(cot_all, gate_up, act_two, w_gu, w_dt, ff_own, 4)
     g_dt = sum_rows(g_dt)
     g_gu = sum_rows(after(g_gu, g_dt))
@@ -1054,12 +1201,16 @@
     d_norm, _ = rms_back(d_act_two, resid, factor_two, gain_two)
     d_resid = cot.astype(F32) + d_norm
     d_att, out_part, g_out = project_back(d_resid.astype(BF16), hidden, w_dt, w_o, mixed, 5)
-    d_qkv, out_sum = attend_back(qkv, seg, heads, wide, d_att, full, den, out_part, 7)
+    d_qkv, out_sum, g_dt, g_out = attend_back(
+        qkv, seg, heads, wide, d_att, full, den, out_part, blocked(g_dt), g_out, 7
+    )
     g_qkv = dot_tn(act_one, d_qkv).astype(BF16)
-    d_act_one = product_sum(after(d_qkv, g_qkv, g_gu), w_qkv, True, 6)
-
-    g_out = sum_rows(after(lax.all_to_all(g_out, "fsdp", 1, 0, tiled=True), g_gu, d_qkv))
-    g_qkv = sum_rows(after(g_qkv, g_out))
+    grad_input, moved_gu = product_sum(
+        after(d_qkv, g_qkv), attn, True, 6, x, gain_one, d_resid, blocked(g_gu)
+    )
+
+    g_out = sum_rows(after(g_out, g_gu))
+    g_qkv = sum_rows(after(g_qkv, g_gu))
     own_rows = lax.axis_index("dp") * (width // lax.axis_size("dp"))
 
     def gain_grad(weights, grads, gain):
@@ -1067,33 +1218,30 @@
         inner = jnp.sum(part.astype(F32) * grads.astype(F32), 1)
         return inner / lax.dynamic_slice_in_dim(gain, own_rows, grads.shape[0], 0)
 
-    gains = jnp.stack([gain_grad(w_qkv, g_qkv, gain_one), gain_grad(w_gu, g_gu, gain_two)], 1)
+    gains = jnp.stack([gain_grad(attn[:, :qkv_cols], g_qkv, gain_one), gain_grad(w_gu, g_gu, gain_two)], 1)
     filler = jnp.zeros((g_qkv.shape[0], qkv_cols - used - 2), BF16)
     g_attn = jnp.concatenate([g_qkv[:, :used], gains.astype(BF16), filler, g_out], 1)
-    g_dt = to_owners(g_dt, n_f)
-    g_gu = to_owners(g_gu, n_f)
+    moved_gu, g_dt, _ = lax.optimization_barrier((moved_gu, g_dt, g_attn))
+    g_gu, g_dt = jnp.transpose(moved_gu, (1, 0, 2)), jnp.transpose(g_dt, (1, 0, 2))
     g_attn = to_owners(g_attn, n_f)
 
-    def from_halves(at, tail):
-        both = [g_gu[:, :, at : at + main], g_gu[:, :, tail : tail + ff_own - main]]
-        return jnp.concatenate(both, 2).reshape(rows, ff)
+    def from_halves(grads, at, tail):
+        parts = [grads[:, :, at : at + main], grads[:, :, tail : tail + ff_own - main]]
+        return jnp.concatenate([columns(g, 0, g.shape[2]) for g in parts], 1).astype(F32)
 
     output = (resid + out_sum).astype(BF16)[None]
-    factor_one = lax.rsqrt(jnp.mean(x_f * x_f, -1, keepdims=True) + EPS)
-    d_norm, _ = rms_back(d_act_one, x_f, factor_one, gain_one)
-    grad_input = (d_resid + d_norm)[None]
     return (
         output,
-        grad_input,
+        grad_input[None],
         jnp.sum(g_attn[:, :, gain_at], 1),
         columns(g_attn, v_own, v_own + qk_own),
         columns(g_attn, v_own + qk_own, used),
         columns(g_attn, 0, v_own),
         columns(g_attn, qkv_cols, att_cols),
         jnp.sum(g_attn[:, :, gain_at + 1], 1),
-        from_halves(0, 2 * main),
-        from_halves(main, main + ff_own),
-        columns(g_dt, 0, ff_own).T,
+        from_halves(g_gu, 0, 2 * main),
+        from_halves(g_gu, main, main + ff_own),
+        from_halves(g_dt, 0, main).T,
     )
 
 

time: 591 us -> 556 us (0.941)
  starting transfers between devices: 27.8 us -> 9.14 us
  Pallas kernels: 432 us -> 449 us
  other arithmetic: 33.9 us -> 17.1 us
  waiting for transfers between devices: 24.1 us -> 11.1 us
    pallas_call x1, Pallas kernels: 52 us -> 63.9 us  [attend_back(): pl.pallas_call(functools.partial(attend_back_kernel, heads, wide, blocks,...]
    all_to_all x3 -> x0, starting transfers between devices: 10.7 us -> none  [the longest x1 3.56 us: on_device(): w_o = lax.all_to_all(attn[:, qkv_cols:], 'fsdp', 0, 1, tiled=True)]
    all_to_all x3 -> x0, waiting for transfers between devices: 10.6 us -> none  [the longest x1 10.6 us: on_device(): w_dt = over_rows(lax.all_to_all(after(dt, x_all), 'fsdp', 0, 0, tiled=True))]
    reduce_sum x3 -> x1, other arithmetic: 10 us -> 0.22 us  [on_device(): factor_two = lax.rsqrt(jnp.mean(resid * resid, -1, keepdims=True) + EPS)]
    all_to_all x3 -> x1, starting transfers between devices: 11.4 us -> 3.55 us  [to_owners(): lax.all_to_all(part, 'fsdp', 0, 0, tiled=True)]
    unnamed x78 -> x52, local copies, waits for them, and re-layouts: 10.4 us -> 16.8 us
    pallas_call x4 -> x3, Pallas kernels: 168 us -> 170 us  [the longest x2 106 us: product_sum(): pl.pallas_call(functools.partial(product_sum_kernel, turned, base is None...]
  transfers between devices with their start and end apart: 14 -> 9, of which waited for: 6 -> 3; matrix products, arithmetic and copies ran while one was open for 11% -> 6% of each run, Pallas kernels for 74% -> 82%
where the time goes in v4:
time: 556 us; the launch traced here: 548 us
  Pallas kernels  449 us (81%)
  local copies, waits for them, and re-layouts  36.4 us (7%)
  other arithmetic  17.1 us (3%)
  between operations  14.9 us (3%)
  waiting for transfers between devices  11.1 us (2%)
  matrix products  9.48 us (2%)
  starting transfers between devices  9.14 us (2%)
    pallas_call x2, Pallas kernels, product_sum(): pl.pallas_call(functools.partial(product_sum_kernel, turned, base is None...  106 us
    pallas_call x1, Pallas kernels, attend(): pl.pallas_call(functools.partial(attend_kernel, heads, wide, blocks, link...  64 us
    pallas_call x1, Pallas kernels, attend_back(): pl.pallas_call(functools.partial(attend_back_kernel, heads, wide, blocks,...  63.9 us
    pallas_call x1, Pallas kernels, feed_back(): pl.pallas_call(functools.partial(feed_back_kernel, ff), out_shape=(jax.Sh...  60.3 us
    pallas_call x1, Pallas kernels, feed(): pl.pallas_call(functools.partial(feed_kernel, ff), out_shape=(jax.ShapeDt...  56.1 us
    pallas_call x1, Pallas kernels, start_exchange(): pl.pallas_call(start_kernel, out_shape=(jax.ShapeDtypeStruct((8,) + x.sha...  55.6 us
    pallas_call x1, Pallas kernels, project_back(): pl.pallas_call(project_back_kernel, out_shape=(jax.ShapeDtypeStruct((8 *...  43.6 us
    unnamed x52, local copies, waits for them, and re-layouts  16.8 us
  transfers between devices with their start and end apart: 9, of which 3 were waited for; matrix products, arithmetic and copies ran while one was open for 6% of the time, Pallas kernels for 82%

profile of v4, /device:TPU:0, one launch (start us, length us, event | category | flops | bytes accessed | tf_op | source)
XLA Modules:
  0.0 547.5 jit_solution(1919864567754659578)
XLA Ops:
  7.2 0.9 copy.148
  8.2 0.9 copy.149
  9.2 1.1 copy_bitcast_fusion.3
  10.3 0.7 broadcast_in_dim.14
  11.0 0.7 broadcast_in_dim.15
  11.8 1.1 concatenate.23
  13.0 5.3 all-to-all-start
  18.7 0.6 slice-done.1
  19.4 0.2 slice-done.3
  19.6 0.9 copy_bitcast_fusion.1
  20.5 3.5 concatenate.22
  24.0 5.4 all-to-all-done
  29.4 0.8 copy-done.11
  30.3 55.6 %start_exchange.1 = (bf16[8,256,2048]{2,1,0:T(8,128)(2,1)}, bf16[8,64,1408]{2,1,0:T(8,128)(2,1)}) custom-call(bf16[256,2048]{1,0:T(8,128)(2,1)} %bitcast.109, bf16[8,64,1408]{2,1,0:T(8,128)(2,1)} %bitcast.92), custom_call_target="tpu_custom_call" | custom-call | flops 44999999488 | bytes 100000000 | tf_op jit(solution)/shard_map/start_exchange/pallas_call | solution.py:353
  86.1 0.5 copy-done.21
  86.7 0.6 slice.102
  87.3 0.4 copy.158.refs_3_.refs_1_
  88.2 1.7 compare_convert_fusion.refs_5_.refs_3_
  89.9 2.6 fusion.2
  92.4 64.0 %attend.1 = (bf16[2048,384]{1,0:T(8,128)(2,1)}, bf16[2048,256]{1,0:T(8,128)(2,1)S(1)}, f32[2048,256]{1,0:T(8,128)}, f32[2048,2]{1,0:T(8,128)S(1)}, bf16[2048,204...) custom-call(bf16[2048,2048]{1,0:T(8,128)(2,1)} %bitcast.114, ...), custom_call_target="tpu_custom_call" | custom-call | flops 44999999488 | bytes 100000000 | tf_op jit(solution)/shard_map/attend/pallas_call | solution.py:678
  156.5 1.0 copy-done.3
  157.5 1.0 copy-done.6
  158.4 1.0 copy-done.7
  159.5 46.6 %product_sum.2 = (f32[256,2048]{1,0:T(8,128)}, bf16[256,2048]{1,0:T(8,128)(2,1)}) custom-call(bf16[2048,256]{1,0:T(8,128)(2,1)} %copy-done.6, bf16[256,2048]{1,0:T(8,128)(2,1)} %copy-done.7, bf16[256,2048]{1,0:T(8,128)(2,1)} %bitcast.110, f32[1,2048]{1,0:T(1,128)} %bitcast.107), custom_call_target="tpu_custom_call" | custom-call | flops 44999999488 | bytes 100000000 | tf_op jit(solution)/shard_map/product_sum/pallas_call | solution.py:311
  206.1 56.1 %feed.1 = (bf16[8,256,2048]{2,1,0:T(8,128)(2,1)}, f32[2048,1408]{1,0:T(8,128)}, bf16[8,256,768]{2,1,0:T(8,128)(2,1)}, bf16[2048,768]{1,0:T(8,128)(2,1)}) custom-call(bf16[8,256,2048]{2,1,0:T(8,128)(2,1)} %get-tuple-element.49.cot_ref, bf16[256,2048]{1,0:T(8,128)(2,1)} %get-tuple-element.50.act_ref, bf16[2048,1408]{1,0:T(8,128)(2,1)} %all-gather.6.cloned.1.call-done.w_ref), custom_call_target="tpu_custom_call" | custom-call | flops 44999999488 | bytes 100000000 | tf_op jit(solution)/shard_map/feed/pallas_call | solution.py:890
  262.3 60.3 %feed_back.1 = (f32[256,2048]{1,0:T(8,128)}, bf16[2048,1408]{1,0:T(8,128)(2,1)}) custom-call(bf16[8,256,2048]{2,1,0:T(8,128)(2,1)} %get-tuple-element.49.cot_ref, f32[8,256,1408]{2,1,0:T(8,128)} %bitcast.113, bf16[2048,2048]{1,0:T(8,128)(2,1)} %bitcast.115, bf16[2048,1408]{1,0:T(8,128)(2,1)} %all-gather.6.cloned.1.call-done.w_ref, ...), custom_call_target="tpu_custom_call" | custom-call | flops 44999999488 | bytes 100000000 | tf_op jit(solution)/shard_map/feed_back/pallas_call | solution.py:1011
  322.7 0.3 reduce-scatter.5.cloned.1.call-done
  323.1 1.5 copy-done.8
  324.6 0.2 multiply_reduce_fusion.2
  324.8 0.4 copy-done.9
  325.2 0.4 multiply_reduce_fusion.1
  325.6 0.8 copy-done.16
  326.5 1.9 fusion.3
  328.4 43.6 %project_back.1 = (bf16[2048,256]{1,0:T(8,128)(2,1)S(1)}, bf16[8,256,2048]{2,1,0:T(8,128)(2,1)}, bf16[256,2048]{1,0:T(8,128)(2,1)S(1)}) custom-call(bf16[256,2048]{1,0:T(8,128)(2,1)S(1)} %get-tuple-element.136.p_ref, bf16[2048,768]{1,0:T(8,128)(2,1)} %bitcast.116, bf16[2048,768]{1,0:T(8,128)(2,1)} %all-gather.8.cloned.1.call-done.d_ref, ...), custom_call_target="tpu_custom_call" | custom-call | flops 44999999488 | bytes 100000000 | tf_op jit(solution)/shard_map/project_back/pallas_call | solution.py:1093
  372.0 1.0 copy-done.4
  373.0 1.0 copy-done.5
  374.0 63.9 %attend_back.1 = (bf16[2048,384]{1,0:T(8,128)(2,1)}, f32[256,2048]{1,0:T(8,128)}, bf16[8,64,768]{2,1,0:T(8,128)(2,1)}, bf16[8,256,256]{2,1,0:T(8,128)(2,1)}) custom-call(bf16[2048,384]{1,0:T(8,128)(2,1)} %get-tuple-element.48.refs_0_, s32[2048,1]{1,0:T(8,128)} %copy-done, s32[8,1,256]{2,1,0:T(1,128)} %bitcast.75, ...), custom_call_target="tpu_custom_call" | custom-call | flops 44999999488 | bytes 100000000 | tf_op jit(solution)/shard_map/attend_back/pallas_call | solution.py:726
  437.9 9.5 %convolution_convert_fusion = bf16[2048,384]{1,0:T(8,128)(2,1)} fusion(bf16[2048,2048]{1,0:T(8,128)(2,1)} %get-tuple-element.65, bf16[2048,384]{1,0:T(8,128)(2,1)} %get-tuple-element.66.l_ref), kind=kOutput, calls=%fused_computation.1 | convolution fusion | flops 3222011904 | bytes 11534336 | tf_op jit(solution)/shard_map/dot_general | solution.py:31
  447.4 1.7 copy-done.10
  449.2 0.3 slice_convert_fusion
  449.5 0.2 dynamic-slice_reduce_fusion.1
  449.8 0.9 copy-done.13
  450.8 1.3 fusion
  452.1 59.2 %product_sum.3 = (f32[256,2048]{1,0:T(8,128)}, bf16[8,64,1408]{2,1,0:T(8,128)(2,1)}) custom-call(bf16[2048,384]{1,0:T(8,128)(2,1)} %get-tuple-element.66.l_ref, bf16[2048,640]{1,0:T(8,128)(2,1)} %all-gather.4.cloned.1.call-done.refs_2_.r_ref, bf16[256,2048]{1,0:T(8,128)(2,1)} %bitcast.111, f32[1,2048]{1,0:T(1,128)} %bitcast.77, ...), custom_call_target="tpu_custom_call" | custom-call | flops 44999999488 | bytes 100000000 | tf_op jit(solution)/shard_map/product_sum/pallas_call | solution.py:311
  511.3 1.9 multiply_reduce_fusion
  513.4 1.3 multiply_reduce_fusion.3
  514.9 2.0 concatenate.25
  517.0 0.7 fusion.4
  517.7 0.2 slice_bitcast_fusion.1
  517.9 0.3 copy-done.17
  518.2 3.6 all-to-all-start.1
  521.9 0.8 reshape.203
  523.4 2.0 maximum_convert_fusion
  525.3 1.2 maximum_convert_fusion.1
  526.5 1.2 convert_bitcast_fusion
  527.7 5.2 all-to-all-done.1
  533.0 0.8 slice_reduce_fusion
  533.8 0.8 fusion.5
  534.7 1.2 copy.162
  535.9 0.7 copy.172
  536.8 0.7 copy.173
  537.5 0.8 copy.179
  538.3 0.8 copy.180
  539.2 1.3 copy.191
  (97 shorter events, 3.4 us)
Async XLA Ops:
  13.0 5.4 slice-start.2
  13.0 5.6 %slice-start.4 = ((bf16[64,5504]{1,0:T(8,128)(2,1)}), bf16[64,384]{1,0:T(8,128)(2,1)S(1)}, s32[]{:S(2)}) async-start(bf16[64,5504]{1,0:T(8,128)(2,1)} %param.21), calls=%async_computation.17 | async-start | bytes 98304 | tf_op jit(solution)/shard_map/slice | solution.py:1176
  13.0 16.5 %all-to-all-start = ((bf16[8,64,640]{2,1,0:T(8,128)(2,1)}), bf16[8,64,640]{2,1,0:T(8,128)(2,1)S(1)}, u32[]{:S(2)}, u32[]{:S(2)}) async-start(bf16[8,64,640]{2,1,0:T(8,128)(2,1)} %bitcast.5), calls=%async_computation | async-start | bytes 1310720 | tf_op jit(solution)/shard_map/all_to_all | solution.py:1172
  18.3 1.1 slice-start.1
  18.3 1.3 slice-start.3
  18.3 71.6 %all-gather.4.cloned.1.call-start = ((), (), s32[]{:S(2)}) async-start(), calls=%async_computation.6 | async-start | bytes 3276800 | tf_op jit(solution)/shard_map/all_gather | solution.py:1121
  29.4 0.8 copy-start.11
  30.3 175.9 %all-gather.6.cloned.1.call-start = ((), (), s32[]{:S(2)}) async-start(), calls=%async_computation.7 | async-start | bytes 7208960 | tf_op jit(solution)/shard_map/all_gather | solution.py:1121
  30.3 55.7 %copy-start.18 = (bf16[5504,64]{0,1:T(8,128)(2,1)S(1)}, bf16[5504,64]{0,1:T(8,128)(2,1)}, u32[]{:S(2)}) copy-start(bf16[5504,64]{0,1:T(8,128)(2,1)} %param.22) | copy-start | bytes 2113540
  86.0 0.7 copy-start.21
  86.0 176.3 %all-gather.8.cloned.1.call-start = ((), (), s32[]{:S(2)}) async-start(), calls=%async_computation.8 | async-start | bytes 3932160 | tf_op jit(solution)/shard_map/all_gather | solution.py:1121
  86.7 5.7 %copy-start.1 = (s32[2048]{0:T(1024)}, s32[2048]{0:T(1024)S(1)}, u32[]{:S(2)}) copy-start(s32[2048]{0:T(1024)S(1)} %convert_reduce_fusion) | copy-start | bytes 24580
  87.7 4.8 copy-start
  92.4 64.1 %copy-start.2 = (f32[2048]{0:T(1024)}, f32[2048]{0:T(1024)S(1)}, u32[]{:S(2)}) copy-start(f32[2048]{0:T(1024)S(1)} %get-tuple-element.133) | copy-start | bytes 24580
  156.5 1.0 copy-start.3
  157.5 1.0 copy-start.6
  158.4 1.0 copy-start.7
  159.4 163.5 %reduce-scatter.5.cloned.1.call-start = ((), (), s32[]{:S(2)}) async-start(), calls=%async_computation.9 | async-start | bytes 3932160 | tf_op jit(solution)/shard_map/reduce_scatter | solution.py:1125
  262.3 185.1 %reduce-scatter.7.cloned.1.call-start = ((), (), s32[]{:S(2)}) async-start(), calls=%async_computation.10 | async-start | bytes 7208960 | tf_op jit(solution)/shard_map/reduce_scatter | solution.py:1125
  323.0 1.6 copy-start.8
  323.0 1.8 copy-start.20
  323.0 190.4 %reduce-scatter.9.cloned.1.call-start = ((), (), s32[]{:S(2)}) async-start(), calls=%async_computation.11 | async-start | bytes 1966080 | tf_op jit(solution)/shard_map/reduce_scatter | solution.py:1125
  323.1 2.2 copy-start.9
  325.2 1.2 copy-start.16
  372.0 1.0 copy-start.4
  373.0 1.0 copy-start.5
  447.4 67.5 %reduce-scatter.11.cloned.1.call-start = ((), (), s32[]{:S(2)}) async-start(), calls=%async_computation.12 | async-start | bytes 1310720 | tf_op jit(solution)/shard_map/reduce_scatter | solution.py:1125
  447.4 1.7 copy-start.10
  449.2 1.6 copy-start.13
  452.1 59.2 %copy-start.15 = (bf16[512,1408]{1,0:T(8,128)(2,1)S(1)}, bf16[512,1408]{1,0:T(8,128)(2,1)}, u32[]{:S(2)}) copy-start(bf16[512,1408]{1,0:T(8,128)(2,1)} %reduce-scatter.7.cloned.1.call-done) | copy-start | bytes 4325380
  511.3 2.1 slice-start
  513.2 3.7 copy-start.14
  517.0 1.2 copy-start.17
  517.9 4.0 copy-start.19
  518.2 14.6 %all-to-all-start.1 = ((bf16[8,64,640]{2,1,0:T(8,128)(2,1)}), bf16[8,64,640]{2,1,0:T(8,128)(2,1)S(1)}, u32[]{:S(2)}, u32[]{:S(2)}) async-start(bf16[8,64,640]{2,1,0:T(8,128)(2,1)} %bitcast.24), calls=%async_computation.5 | async-start | bytes 1310720 | tf_op jit(solution)/shard_map/all_to_all | solution.py:1130
  534.7 4.5 copy-start.12
Sparse Core Ops, SparseCore 0:
  30.4 54.1 all-gather.3
  86.2 106.9 all-gather.5
  194.8 61.7 all-gather.7
  262.4 60.5 reduce-scatter.4
  325.1 102.2 reduce-scatter.6
  447.5 34.5 reduce-scatter.8
  484.4 26.0 reduce-scatter.10

commit v5 on v4

--- a/solution.py
+++ b/solution.py
@@ -216,16 +216,35 @@
     ]
 
 
+def regroup(body, end, main, tail, o_ref):
+    width = 8 * tail
+    lane = lax.broadcasted_iota(jnp.int32, (o_ref.shape[0], width), 1)
+    tails = jnp.zeros((o_ref.shape[0], width), F32)
+    for j in range(8):
+        o_ref[:, j * main : (j + 1) * main] = body(j).astype(F32)
+        piece = jnp.concatenate([end(j), jnp.zeros((o_ref.shape[0], width - 128), F32)], 1)
+        piece = pltpu.roll(piece, j * tail, 1) if j else piece
+        tails = jnp.where((lane >= j * tail) & (lane < (j + 1) * tail), piece, tails)
+    o_ref[:, 8 * main :] = tails
+
+
 def product_sum_kernel(turned, normed, l_ref, r_ref, *refs):
     if normed:
         x_ref, gain_ref, o_ref, act, out, mine, got, ex, ey, fx, fy, send, recv = refs
         _, sib, xn, yn, _, _ = neighbours()
         greet([sib, xn, yn])
     else:
-        x_ref, gain_ref, base_ref, e_ref, o_ref, e_out_ref = refs[:6]
-        out, mine, got, ex, ey, fx, fy, send, recv = refs[6:15]
+        x_ref, gain_ref, base_ref, e_ref, dt_ref, w_ref, o_ref, gate_ref, up_ref, down_ref, along_ref = refs[:11]
+        out, mine, got, ex, ey, fx, fy, send, recv = refs[11:20]
+        own_gu, gu, w, load_gu, load_w = refs[20:25]
+        loads = [
+            pltpu.make_async_copy(e_ref, gu, load_gu),
+            pltpu.make_async_copy(w_ref.at[pl.ds(lax.axis_index("dp") * w.shape[0], w.shape[0])], w, load_w),
+        ]
+        for load in loads:
+            load.start()
         greet(everyone())
-        moved = Exchange(e_ref, e_out_ref, *refs[15:])
+        moved = Exchange(e_ref, own_gu, *refs[25:])
         moved.start()
     rows, cols = o_ref.shape
     depth = l_ref.shape[1]
@@ -260,6 +279,16 @@
     s.second()
     home(3)
     s.own()
+    if not normed:
+        for load in loads:
+            load.wait()
+        some_rows = gu.shape[1]
+        for j in range(8):
+            here = slice(j * some_rows, (j + 1) * some_rows)
+            along_ref[here, :] = jnp.sum(w[here, :].astype(F32) * gu[j].astype(F32), 1, keepdims=True)
+        main = down_ref.shape[1] // 8 // 128 * 128
+        tail = down_ref.shape[1] // 8 - main
+        regroup(lambda j: dt_ref[j, :, :main], lambda j: dt_ref[j, :, main:].astype(F32), main, tail, down_ref)
     s.finish()
     if not normed:
         @pl.loop(0, rows // 64)
@@ -273,6 +302,14 @@
             o_ref[some, :] = base_ref[some, :] + factor * (inner - value * along)
 
         moved.finish()
+
+        def turned_tail(j):
+            return pltpu.roll(own_gu[j, :, 2 * main :].astype(F32), 128 - tail, 1)
+
+        regroup(
+            lambda j: own_gu[j, :, :main], lambda j: own_gu[j, :, 2 * main :].astype(F32), main, tail, gate_ref
+        )
+        regroup(lambda j: own_gu[j, :, main : 2 * main], turned_tail, main, tail, up_ref)
     else:
         @pl.loop(0, rows // 64)
         def _(n):
@@ -283,15 +320,28 @@
             act[some, :] = (value * factor * gain_ref[...]).astype(BF16)
 
 
-def product_sum(left, right, turned, cid, x, gain, base=None, moved=None):
+def product_sum(left, right, turned, cid, x, gain, base=None, moved=None, down=None, w_gu=None, ff=0):
     depth = left.shape[1]
     if lax.axis_size("fsdp") != 8:
         part = (dot_nt(left, right[:, :depth]) if turned else dot(left, right)).astype(BF16)
         part = lax.psum_scatter(part, "fsdp", scatter_dimension=0, tiled=True).astype(F32)
         if base is not None:
+            n_f, some, columns_own = moved.shape
             x = x.astype(F32)
             part, _ = rms_back(part, x, rms_apply(x, gain)[1], gain)
-            return base + part, lax.all_to_all(moved, "fsdp", 0, 0, tiled=True)
+            at = lax.axis_index("dp") * n_f * some
+            w = lax.dynamic_slice_in_dim(w_gu, at, n_f * some, 0).reshape(moved.shape)
+            along = jnp.sum(w.astype(F32) * moved.astype(F32), 2).reshape(-1, 1)
+            moved = lax.all_to_all(moved, "fsdp", 0, 0, tiled=True)
+            main = ff // 128 * 128
+
+            def owner(grads, at, end):
+                parts = [grads[:, :, at : at + main], grads[:, :, end : end + ff - main]]
+                parts = [jnp.transpose(p, (1, 0, 2)).reshape(some, -1) for p in parts]
+                return jnp.concatenate(parts, 1).astype(F32)
+
+            grads = owner(moved, 0, 2 * main), owner(moved, main, main + ff), owner(down, 0, main)
+            return base + part, *grads, along
         part = part + x.astype(F32)
         act = rms_apply(part, gain)[0].astype(BF16)
         return part, act
@@ -303,11 +353,15 @@
         outs.append(jax.ShapeDtypeStruct((rows, cols), BF16))
         out_specs.append(WHOLE)
     else:
-        args += [base, moved]
-        specs += [WHOLE, ANY]
-        outs.append(jax.ShapeDtypeStruct(moved.shape, moved.dtype))
-        out_specs.append(ANY)
-        scratch += exchange_scratch()
+        args += [base, moved, down, w_gu]
+        specs += [WHOLE, ANY, WHOLE, ANY]
+        some = moved.shape[1]
+        outs += [jax.ShapeDtypeStruct((some, 8 * ff), F32)] * 3 + [jax.ShapeDtypeStruct((8 * some, 1), F32)]
+        out_specs += [WHOLE] * 4
+        scratch += [
+            VMEM(moved.shape, BF16), VMEM(moved.shape, BF16), VMEM((8 * some, moved.shape[2]), BF16),
+            pltpu.SemaphoreType.DMA(()), pltpu.SemaphoreType.DMA(()),
+        ] + exchange_scratch()
     got = pl.pallas_call(
         functools.partial(product_sum_kernel, turned, base is None),
         out_shape=outs,
@@ -522,9 +576,12 @@
     qkv_ref, sc_ref, sr_ref, edge_ref, da_ref, full_ref, den_ref = refs[:7]
     refs = refs[7:]
     if with_sum:
-        part_ref, e_ref, c_ref, d_ref, o_ref, e_out_ref, c_out_ref = refs[:7]
-        qz, vx, kt, near_dn, far_dn, qk_acc, v_acc = refs[7:14]
-        mine, got, ex, ey, fx, fy, send, recv, local = refs[14:23]
+        part_ref, e_ref, c_ref, act_ref, d_ref, o_ref, e_out_ref, c_out_ref, grad_ref = refs[:9]
+        qz, vx, kt, near_dn, far_dn, qk_acc, v_acc = refs[9:16]
+        mine, got, ex, ey, fx, fy, send, recv, local = refs[16:25]
+        acts, load_act = refs[31:]
+        whole = pltpu.make_async_copy(act_ref, acts, load_act)
+        whole.start()
         flip = neighbours()[5]
         greet(everyone())
         s = Sum(
@@ -534,7 +591,7 @@
         for k in range(4):
             s.swaps[k].start()
             loads[k].start()
-        moved = [Exchange(c_ref, c_out_ref, *refs[26:]), Exchange(e_ref, e_out_ref, *refs[23:26])]
+        moved = [Exchange(c_ref, c_out_ref, *refs[28:31]), Exchange(e_ref, e_out_ref, *refs[25:28])]
         for one_move in moved:
             one_move.start()
 
@@ -630,6 +687,13 @@
         queries = d_ref[here, heads * wide :].astype(F32)
         d_ref[here, heads * wide :] = (queries + 2.0 * qk_acc[here, :]).astype(BF16)
     if with_sum:
+        whole.wait()
+
+        @pl.loop(0, acts.shape[1] // 256)
+        def _(n):
+            part = pl.ds(pl.multiple_of(n * 256, 256), 256)
+            grad_ref[part, :] = dot_tn(acts[:, part], d_ref[...]).astype(BF16)
+
         s.finish()
         for one_move in moved:
             one_move.finish()
@@ -695,7 +759,7 @@
     )
 
 
-def attend_back(qkv, seg, heads, wide, da, full, den, part, moved, across, cid):
+def attend_back(qkv, seg, heads, wide, da, full, den, part, moved, across, act, cid):
     length, columns = qkv.shape
     blocks = length // BLK
     width = heads * wide
@@ -710,14 +774,16 @@
     ]
     if with_sum:
         rows, cols = length // 8, part.shape[1]
-        args += [part.reshape(8, rows, cols), moved, across]
-        specs += [ANY] * 3
+        args += [part.reshape(8, rows, cols), moved, across, act]
+        specs += [ANY] * 4
         outs += [
             jax.ShapeDtypeStruct((rows, cols), F32),
             jax.ShapeDtypeStruct(moved.shape, moved.dtype),
             jax.ShapeDtypeStruct((8, across.shape[0], across.shape[1] // 8), across.dtype),
+            jax.ShapeDtypeStruct((act.shape[1], columns), BF16),
         ]
         scratch += sum_scratch(rows, cols) + [pltpu.SemaphoreType.DMA((4,))] + 2 * exchange_scratch()
+        scratch += [VMEM(act.shape, BF16), pltpu.SemaphoreType.DMA(())]
         params = pltpu.CompilerParams(
             vmem_limit_bytes=60 << 20, collective_id=cid, has_side_effects=True
         )
@@ -727,19 +793,20 @@
         functools.partial(attend_back_kernel, heads, wide, blocks, with_sum),
         out_shape=outs,
         in_specs=specs,
-        out_specs=[WHOLE, WHOLE, ANY, ANY][: len(outs)],
+        out_specs=[WHOLE, WHOLE, ANY, ANY, WHOLE][: len(outs)],
         scratch_shapes=scratch,
         compiler_params=params,
         cost_estimate=LINKED,
         name="attend_back",
     )(*args)
     if with_sum:
-        return *got[:3], got[3].reshape(-1, got[3].shape[2])
+        return *got[:3], got[3].reshape(-1, got[3].shape[2]), got[4]
     return (
         got[0],
         lax.psum_scatter(part, "fsdp", scatter_dimension=0, tiled=True).astype(F32),
         lax.all_to_all(moved, "fsdp", 0, 0, tiled=True),
         lax.all_to_all(across, "fsdp", 1, 0, tiled=True),
+        dot_tn(act, got[0]).astype(BF16),
     )
 
 
@@ -1201,33 +1268,30 @@
     d_norm, _ = rms_back(d_act_two, resid, factor_two, gain_two)
     d_resid = cot.astype(F32) + d_norm
     d_att, out_part, g_out = project_back(d_resid.astype(BF16), hidden, w_dt, w_o, mixed, 5)
-    d_qkv, out_sum, g_dt, g_out = attend_back(
-        qkv, seg, heads, wide, d_att, full, den, out_part, blocked(g_dt), g_out, 7
+    d_qkv, out_sum, g_dt, g_out, g_qkv = attend_back(
+        qkv, seg, heads, wide, d_att, full, den, out_part, blocked(g_dt), g_out, act_one, 7
     )
-    g_qkv = dot_tn(act_one, d_qkv).astype(BF16)
-    grad_input, moved_gu = product_sum(
-        after(d_qkv, g_qkv), attn, True, 6, x, gain_one, d_resid, blocked(g_gu)
+    grad_input, grad_gate, grad_up, grad_dt, along = product_sum(
+        after(d_qkv, g_qkv), attn, True, 6, x, gain_one, d_resid, blocked(g_gu), g_dt, w_gu, ff_own
     )
 
     g_out = sum_rows(after(g_out, g_gu))
     g_qkv = sum_rows(after(g_qkv, g_gu))
     own_rows = lax.axis_index("dp") * (width // lax.axis_size("dp"))
 
-    def gain_grad(weights, grads, gain):
-        part = lax.dynamic_slice_in_dim(weights, own_rows, grads.shape[0], 0)
-        inner = jnp.sum(part.astype(F32) * grads.astype(F32), 1)
-        return inner / lax.dynamic_slice_in_dim(gain, own_rows, grads.shape[0], 0)
-
-    gains = jnp.stack([gain_grad(attn[:, :qkv_cols], g_qkv, gain_one), gain_grad(w_gu, g_gu, gain_two)], 1)
+    def mine(value):
+        return lax.dynamic_slice_in_dim(value, own_rows, g_qkv.shape[0], 0)
+
+    gains = jnp.stack(
+        [
+            jnp.sum(mine(attn)[:, :qkv_cols].astype(F32) * g_qkv.astype(F32), 1) / mine(gain_one),
+            along[:, 0] / mine(gain_two),
+        ],
+        1,
+    )
     filler = jnp.zeros((g_qkv.shape[0], qkv_cols - used - 2), BF16)
     g_attn = jnp.concatenate([g_qkv[:, :used], gains.astype(BF16), filler, g_out], 1)
-    moved_gu, g_dt, _ = lax.optimization_barrier((moved_gu, g_dt, g_attn))
-    g_gu, g_dt = jnp.transpose(moved_gu, (1, 0, 2)), jnp.transpose(g_dt, (1, 0, 2))
     g_attn = to_owners(g_attn, n_f)
-
-    def from_halves(grads, at, tail):
-        parts = [grads[:, :, at : at + main], grads[:, :, tail : tail + ff_own - main]]
-        return jnp.concatenate([columns(g, 0, g.shape[2]) for g in parts], 1).astype(F32)
 
     output = (resid + out_sum).astype(BF16)[None]
     return (
@@ -1239,9 +1303,9 @@
         columns(g_attn, 0, v_own),
         columns(g_attn, qkv_cols, att_cols),
         jnp.sum(g_attn[:, :, gain_at + 1], 1),
-        from_halves(g_gu, 0, 2 * main),
-        from_halves(g_gu, main, main + ff_own),
-        from_halves(g_dt, 0, main).T,
+        grad_gate,
+        grad_up,
+        grad_dt.T,
     )
 
 

time: 556 us -> 548 us (0.986)
  matrix products: 9.48 us -> 0 us
    dot_general x1 -> x0, matrix products: 9.48 us -> none  [dot_tn(): return lax.dot_general(a, b, TN, preferred_element_type=F32)]
    unnamed x52 -> x47, local copies, waits for them, and re-layouts: 16.8 us -> 19.2 us
  transfers between devices with their start and end apart: 9 -> 9, of which waited for: 3 -> 3; matrix products, arithmetic and copies ran while one was open for 6% -> 4% of each run, Pallas kernels for 82% -> 84%
where the time goes in v5:
time: 548 us; the launch traced here: 540 us
  Pallas kernels  451 us (82%)
  local copies, waits for them, and re-layouts  36.3 us (7%)
  between operations  14.8 us (3%)
  other arithmetic  14.7 us (3%)
  waiting for transfers between devices  14.2 us (3%)
  starting transfers between devices  9.13 us (2%)
    pallas_call x2, Pallas kernels, product_sum(): pl.pallas_call(functools.partial(product_sum_kernel, turned, base is None...  107 us
    pallas_call x1, Pallas kernels, attend_back(): pl.pallas_call(functools.partial(attend_back_kernel, heads, wide, blocks,...  64.4 us
    pallas_call x1, Pallas kernels, attend(): pl.pallas_call(functools.partial(attend_kernel, heads, wide, blocks, link...  64 us
    pallas_call x1, Pallas kernels, feed_back(): pl.pallas_call(functools.partial(feed_back_kernel, ff), out_shape=(jax.Sh...  60.3 us
    pallas_call x1, Pallas kernels, feed(): pl.pallas_call(functools.partial(feed_kernel, ff), out_shape=(jax.ShapeDt...  56.1 us
    pallas_call x1, Pallas kernels, start_exchange(): pl.pallas_call(start_kernel, out_shape=(jax.ShapeDtypeStruct((8,) + x.sha...  55.6 us
    pallas_call x1, Pallas kernels, project_back(): pl.pallas_call(project_back_kernel, out_shape=(jax.ShapeDtypeStruct((8 *...  43.6 us
    unnamed x47, local copies, waits for them, and re-layouts  19.2 us
  transfers between devices with their start and end apart: 9, of which 3 were waited for; matrix products, arithmetic and copies ran while one was open for 4% of the time, Pallas kernels for 84%

profile of v5, /device:TPU:0, one launch (start us, length us, event | category | flops | bytes accessed | tf_op | source)
XLA Modules:
  0.0 540.1 jit_solution(6946367682990172822)
XLA Ops:
  7.2 0.9 copy.120
  8.2 0.9 copy.121
  9.2 1.1 copy_bitcast_fusion.3
  10.3 0.7 broadcast_in_dim.14
  11.0 0.7 broadcast_in_dim.15
  11.8 1.1 concatenate.14
  13.0 5.3 all-to-all-start
  18.3 0.1 reshape.162
  18.5 0.1 reshape.163
  18.7 0.6 slice-done
  19.4 0.2 slice-done.2
  19.6 0.9 copy_bitcast_fusion.1
  20.5 3.5 concatenate.13
  24.0 5.4 all-to-all-done
  29.4 0.8 copy-done.10
  30.3 55.6 %start_exchange.1 = (bf16[8,256,2048]{2,1,0:T(8,128)(2,1)}, bf16[8,64,1408]{2,1,0:T(8,128)(2,1)}) custom-call(bf16[256,2048]{1,0:T(8,128)(2,1)} %bitcast.89, bf16[8,64,1408]{2,1,0:T(8,128)(2,1)} %bitcast.72), custom_call_target="tpu_custom_call" | custom-call | flops 44999999488 | bytes 100000000 | tf_op jit(solution)/shard_map/start_exchange/pallas_call | solution.py:407
  86.1 0.5 copy-done.18
  86.7 0.6 slice.78
  87.3 0.4 copy.130.refs_3_.refs_1_
  87.7 0.1 reshape.172
  88.0 0.1 maximum_bitcast_fusion.refs_6_
  88.2 1.7 compare_convert_fusion.refs_5_.refs_3_
  89.9 2.6 fusion.2
  92.5 64.0 %attend.1 = (bf16[2048,384]{1,0:T(8,128)(2,1)}, bf16[2048,256]{1,0:T(8,128)(2,1)S(1)}, f32[2048,256]{1,0:T(8,128)}, f32[2048,2]{1,0:T(8,128)S(1)}, bf16[2048,204...) custom-call(bf16[2048,2048]{1,0:T(8,128)(2,1)} %bitcast.94, ...), custom_call_target="tpu_custom_call" | custom-call | flops 44999999488 | bytes 100000000 | tf_op jit(solution)/shard_map/attend/pallas_call | solution.py:742
  156.5 1.0 copy-done.3
  157.5 1.0 copy-done.6
  158.5 1.0 copy-done.7
  159.5 46.6 %product_sum.2 = (f32[256,2048]{1,0:T(8,128)}, bf16[256,2048]{1,0:T(8,128)(2,1)}) custom-call(bf16[2048,256]{1,0:T(8,128)(2,1)} %copy-done.6, bf16[256,2048]{1,0:T(8,128)(2,1)} %copy-done.7, bf16[256,2048]{1,0:T(8,128)(2,1)} %bitcast.90, f32[1,2048]{1,0:T(1,128)} %bitcast.86), custom_call_target="tpu_custom_call" | custom-call | flops 44999999488 | bytes 100000000 | tf_op jit(solution)/shard_map/product_sum/pallas_call | solution.py:365
  206.2 56.1 %feed.1 = (bf16[8,256,2048]{2,1,0:T(8,128)(2,1)}, f32[2048,1408]{1,0:T(8,128)}, bf16[8,256,768]{2,1,0:T(8,128)(2,1)}, bf16[2048,768]{1,0:T(8,128)(2,1)}) custom-call(bf16[8,256,2048]{2,1,0:T(8,128)(2,1)} %get-tuple-element.51.cot_ref, bf16[256,2048]{1,0:T(8,128)(2,1)} %get-tuple-element.52.act_ref, bf16[2048,1408]{1,0:T(8,128)(2,1)} %all-gather.6.cloned.1.call-done.w_ref.refs_5_), custom_call_target="tpu_custom_call" | custom-call | flops 44999999488 | bytes 100000000 | tf_op jit(solution)/shard_map/feed/pallas_call | solution.py:957
  262.4 60.3 %feed_back.1 = (f32[256,2048]{1,0:T(8,128)}, bf16[2048,1408]{1,0:T(8,128)(2,1)}) custom-call(bf16[8,256,2048]{2,1,0:T(8,128)(2,1)} %get-tuple-element.51.cot_ref, f32[8,256,1408]{2,1,0:T(8,128)} %bitcast.93, bf16[2048,2048]{1,0:T(8,128)(2,1)} %bitcast.95, bf16[2048,1408]{1,0:T(8,128)(2,1)} %all-gather.6.cloned.1.call-done.w_ref.refs_5_, ...), custom_call_target="tpu_custom_call" | custom-call | flops 44999999488 | bytes 100000000 | tf_op jit(solution)/shard_map/feed_back/pallas_call | solution.py:1078
  322.7 0.3 reduce-scatter.5.cloned.1.call-done
  323.1 1.5 copy-done.8
  324.6 0.2 multiply_reduce_fusion.1
  324.8 0.4 copy-done.9
  325.2 0.4 multiply_reduce_fusion
  325.7 0.8 copy-done.15
  326.5 1.9 fusion.3
  328.4 43.6 %project_back.1 = (bf16[2048,256]{1,0:T(8,128)(2,1)S(1)}, bf16[8,256,2048]{2,1,0:T(8,128)(2,1)}, bf16[256,2048]{1,0:T(8,128)(2,1)S(1)}) custom-call(bf16[256,2048]{1,0:T(8,128)(2,1)S(1)} %get-tuple-element.140.p_ref, bf16[2048,768]{1,0:T(8,128)(2,1)} %bitcast.96, bf16[2048,768]{1,0:T(8,128)(2,1)} %all-gather.8.cloned.1.call-done.d_ref, ...), custom_call_target="tpu_custom_call" | custom-call | flops 44999999488 | bytes 100000000 | tf_op jit(solution)/shard_map/project_back/pallas_call | solution.py:1160
  372.1 1.0 copy-done.4
  373.0 1.0 copy-done.5
  374.0 64.4 %attend_back.1 = (bf16[2048,384]{1,0:T(8,128)(2,1)}, f32[256,2048]{1,0:T(8,128)}, bf16[8,64,768]{2,1,0:T(8,128)(2,1)}, bf16[8,256,256]{2,1,0:T(8,128)(2,1)}, bf16[2048,384]{1,0:T(8,128)(2,1)}) custom-call(bf16[2048,384]{1,0:T(8,128)(2,1)} %get-tuple-element.50.refs_0_, s32[2048,1]{1,0:T(8,128)} %copy-done, s32[8,1,256]{2,1,0:T(1,128)} %bitcast.61, ...), custom_call_target="tpu_custom_call" | custom-call | flops 44999999488 | bytes 100000000 | tf_op jit(solution)/shard_map/attend_back/pallas_call | solution.py:792
  438.5 1.6 slice_convert_fusion
  440.1 0.2 dynamic-slice_reduce_fusion
  440.3 60.4 %product_sum.3 = (f32[256,2048]{1,0:T(8,128)}, f32[64,5504]{1,0:T(8,128)}, f32[64,5504]{1,0:T(8,128)}, f32[64,5504]{1,0:T(8,128)}, f32[512,1]{1,0:T(8,128)}) custom-call(bf16[2048,384]{1,0:T(8,128)(2,1)} %get-tuple-element.69.l_ref, bf16[2048,640]{1,0:T(8,128)(2,1)} %all-gather.4.cloned.1.call-done.refs_2_.r_ref, bf16[256,2048]{1,0:T(8,128)(2,1)} %bitcast.91, ...), custom_call_target="tpu_custom_call" | custom-call | flops 44999999488 | bytes 100000000 | tf_op jit(solution)/shard_map/product_sum/pallas_call | solution.py:365
  500.7 1.0 divide_convert_fusion
  501.7 1.3 multiply_reduce_fusion.2
  503.2 2.0 concatenate.16
  505.3 3.5 all-to-all-start.1
  508.8 2.8 fusion
  511.6 8.3 %all-to-all-done.1 = bf16[8,64,640]{2,1,0:T(8,128)(2,1)S(1)} async-done(((bf16[8,64,640]{2,1,0:T(8,128)(2,1)}), bf16[8,64,640]{2,1,0:T(8,128)(2,1)S(1)}, u32[]{:S(2)}, u32[]{:S(2)}) %all-to-all-start.1) | async-done | bytes 655392 | tf_op jit(solution)/shard_map/all_to_all | solution.py:1197
  520.0 0.8 slice_reduce_fusion
  520.8 0.8 fusion.4
  521.7 1.2 copy.133
  522.9 0.7 copy.137
  523.8 0.7 copy.138
  524.5 0.8 copy.144
  525.3 0.8 copy.145
  526.2 1.3 copy.156
  527.5 0.8 copy-done.14
  528.3 1.1 copy.157
  529.4 0.8 copy-done.13
  530.2 1.1 copy.158
  531.3 0.8 copy-done.12
  532.0 1.1 copy.159
  (72 shorter events, 1.7 us)
Async XLA Ops:
  13.0 5.4 slice-start.1
  13.0 5.6 %slice-start.3 = ((bf16[64,5504]{1,0:T(8,128)(2,1)}), bf16[64,384]{1,0:T(8,128)(2,1)S(1)}, s32[]{:S(2)}) async-start(bf16[64,5504]{1,0:T(8,128)(2,1)} %param.21), calls=%async_computation.16 | async-start | bytes 98304 | tf_op jit(solution)/shard_map/slice | solution.py:1243
  13.0 16.5 %all-to-all-start = ((bf16[8,64,640]{2,1,0:T(8,128)(2,1)}), bf16[8,64,640]{2,1,0:T(8,128)(2,1)S(1)}, u32[]{:S(2)}, u32[]{:S(2)}) async-start(bf16[8,64,640]{2,1,0:T(8,128)(2,1)} %bitcast.5), calls=%async_computation | async-start | bytes 1310720 | tf_op jit(solution)/shard_map/all_to_all | solution.py:1239
  18.3 1.1 slice-start
  18.3 1.3 slice-start.2
  18.3 71.6 %all-gather.4.cloned.1.call-start = ((), (), s32[]{:S(2)}) async-start(), calls=%async_computation.6 | async-start | bytes 3276800 | tf_op jit(solution)/shard_map/all_gather | solution.py:1188
  29.4 0.8 copy-start.10
  30.3 175.9 %all-gather.6.cloned.1.call-start = ((), (), s32[]{:S(2)}) async-start(), calls=%async_computation.7 | async-start | bytes 7208960 | tf_op jit(solution)/shard_map/all_gather | solution.py:1188
  30.3 55.7 %copy-start.16 = (bf16[5504,64]{0,1:T(8,128)(2,1)S(1)}, bf16[5504,64]{0,1:T(8,128)(2,1)}, u32[]{:S(2)}) copy-start(bf16[5504,64]{0,1:T(8,128)(2,1)} %param.22) | copy-start | bytes 2113540
  86.0 0.7 copy-start.18
  86.0 176.3 %all-gather.8.cloned.1.call-start = ((), (), s32[]{:S(2)}) async-start(), calls=%async_computation.8 | async-start | bytes 3932160 | tf_op jit(solution)/shard_map/all_gather | solution.py:1188
  86.7 5.7 %copy-start.1 = (s32[2048]{0:T(1024)}, s32[2048]{0:T(1024)S(1)}, u32[]{:S(2)}) copy-start(s32[2048]{0:T(1024)S(1)} %convert_reduce_fusion) | copy-start | bytes 24580
  87.7 4.8 copy-start
  92.5 64.0 %copy-start.2 = (f32[2048]{0:T(1024)}, f32[2048]{0:T(1024)S(1)}, u32[]{:S(2)}) copy-start(f32[2048]{0:T(1024)S(1)} %get-tuple-element.137) | copy-start | bytes 24580
  156.5 1.0 copy-start.3
  157.5 1.0 copy-start.6
  158.5 1.0 copy-start.7
  159.5 163.5 %reduce-scatter.5.cloned.1.call-start = ((), (), s32[]{:S(2)}) async-start(), calls=%async_computation.9 | async-start | bytes 3932160 | tf_op jit(solution)/shard_map/reduce_scatter | solution.py:1192
  262.3 176.1 %reduce-scatter.7.cloned.1.call-start = ((), (), s32[]{:S(2)}) async-start(), calls=%async_computation.10 | async-start | bytes 7208960 | tf_op jit(solution)/shard_map/reduce_scatter | solution.py:1192
  323.0 1.6 copy-start.8
  323.0 1.8 copy-start.17
  323.0 178.7 %reduce-scatter.9.cloned.1.call-start = ((), (), s32[]{:S(2)}) async-start(), calls=%async_computation.11 | async-start | bytes 1966080 | tf_op jit(solution)/shard_map/reduce_scatter | solution.py:1192
  323.1 2.2 copy-start.9
  325.2 1.2 copy-start.15
  372.1 1.0 copy-start.4
  373.0 1.0 copy-start.5
  438.4 64.8 %reduce-scatter.11.cloned.1.call-start = ((), (), s32[]{:S(2)}) async-start(), calls=%async_computation.12 | async-start | bytes 1310720 | tf_op jit(solution)/shard_map/reduce_scatter | solution.py:1192
  505.3 14.6 %all-to-all-start.1 = ((bf16[8,64,640]{2,1,0:T(8,128)(2,1)}), bf16[8,64,640]{2,1,0:T(8,128)(2,1)S(1)}, u32[]{:S(2)}, u32[]{:S(2)}) async-start(bf16[8,64,640]{2,1,0:T(8,128)(2,1)} %bitcast.24), calls=%async_computation.5 | async-start | bytes 1310720 | tf_op jit(solution)/shard_map/all_to_all | solution.py:1197
  521.7 4.5 copy-start.11
  526.2 2.1 copy-start.14
  528.3 1.9 copy-start.13
  530.2 1.9 copy-start.12
Sparse Core Ops, SparseCore 0:
  30.4 54.1 all-gather.3
  86.2 106.9 all-gather.5
  194.8 61.7 all-gather.7
  262.4 60.5 reduce-scatter.4
  325.1 102.2 reduce-scatter.6
  438.5 34.5 reduce-scatter.8
  475.4 26.0 reduce-scatter.10

commit v6 on v5

--- a/solution.py
+++ b/solution.py
@@ -221,11 +221,11 @@
     lane = lax.broadcasted_iota(jnp.int32, (o_ref.shape[0], width), 1)
     tails = jnp.zeros((o_ref.shape[0], width), F32)
     for j in range(8):
-        o_ref[:, j * main : (j + 1) * main] = body(j).astype(F32)
+        o_ref[:, j * main : (j + 1) * main] = body(j)
         piece = jnp.concatenate([end(j), jnp.zeros((o_ref.shape[0], width - 128), F32)], 1)
         piece = pltpu.roll(piece, j * tail, 1) if j else piece
         tails = jnp.where((lane >= j * tail) & (lane < (j + 1) * tail), piece, tails)
-    o_ref[:, 8 * main :] = tails
+    o_ref[:, 8 * main :] = tails.astype(BF16)
 
 
 def product_sum_kernel(turned, normed, l_ref, r_ref, *refs):
@@ -234,9 +234,9 @@
         _, sib, xn, yn, _, _ = neighbours()
         greet([sib, xn, yn])
     else:
-        x_ref, gain_ref, base_ref, e_ref, dt_ref, w_ref, o_ref, gate_ref, up_ref, down_ref, along_ref = refs[:11]
-        out, mine, got, ex, ey, fx, fy, send, recv = refs[11:20]
-        own_gu, gu, w, load_gu, load_w = refs[20:25]
+        x_ref, gain_ref, e_ref, dt_ref, w_ref, o_ref, gate_ref, up_ref, down_ref, along_ref = refs[:10]
+        out, mine, got, ex, ey, fx, fy, send, recv = refs[10:19]
+        own_gu, gu, w, load_gu, load_w = refs[19:24]
         loads = [
             pltpu.make_async_copy(e_ref, gu, load_gu),
             pltpu.make_async_copy(w_ref.at[pl.ds(lax.axis_index("dp") * w.shape[0], w.shape[0])], w, load_w),
@@ -244,7 +244,7 @@
         for load in loads:
             load.start()
         greet(everyone())
-        moved = Exchange(e_ref, own_gu, *refs[25:])
+        moved = Exchange(e_ref, own_gu, *refs[24:])
         moved.start()
     rows, cols = o_ref.shape
     depth = l_ref.shape[1]
@@ -299,7 +299,7 @@
             value = value * factor
             inner = o_ref[some, :] * gain_ref[...]
             along = jnp.sum(inner * value, 1, keepdims=True) * (1.0 / cols)
-            o_ref[some, :] = base_ref[some, :] + factor * (inner - value * along)
+            o_ref[some, :] = factor * (inner - value * along)
 
         moved.finish()
 
@@ -320,12 +320,12 @@
             act[some, :] = (value * factor * gain_ref[...]).astype(BF16)
 
 
-def product_sum(left, right, turned, cid, x, gain, base=None, moved=None, down=None, w_gu=None, ff=0):
+def product_sum(left, right, turned, cid, x, gain, moved=None, down=None, w_gu=None, ff=0):
     depth = left.shape[1]
     if lax.axis_size("fsdp") != 8:
         part = (dot_nt(left, right[:, :depth]) if turned else dot(left, right)).astype(BF16)
         part = lax.psum_scatter(part, "fsdp", scatter_dimension=0, tiled=True).astype(F32)
-        if base is not None:
+        if moved is not None:
             n_f, some, columns_own = moved.shape
             x = x.astype(F32)
             part, _ = rms_back(part, x, rms_apply(x, gain)[1], gain)
@@ -338,10 +338,10 @@
             def owner(grads, at, end):
                 parts = [grads[:, :, at : at + main], grads[:, :, end : end + ff - main]]
                 parts = [jnp.transpose(p, (1, 0, 2)).reshape(some, -1) for p in parts]
-                return jnp.concatenate(parts, 1).astype(F32)
+                return jnp.concatenate(parts, 1)
 
             grads = owner(moved, 0, 2 * main), owner(moved, main, main + ff), owner(down, 0, main)
-            return base + part, *grads, along
+            return part, *grads, along
         part = part + x.astype(F32)
         act = rms_apply(part, gain)[0].astype(BF16)
         return part, act
@@ -349,21 +349,21 @@
     args, specs = [left, right, x, gain[None, :]], [WHOLE] * 4
     outs, out_specs = [jax.ShapeDtypeStruct((rows, cols), F32)], [WHOLE]
     scratch = [VMEM((4, rows, cols), BF16)] + sum_scratch(rows, cols)
-    if base is None:
+    if moved is None:
         outs.append(jax.ShapeDtypeStruct((rows, cols), BF16))
         out_specs.append(WHOLE)
     else:
-        args += [base, moved, down, w_gu]
-        specs += [WHOLE, ANY, WHOLE, ANY]
+        args += [moved, down, w_gu]
+        specs += [ANY, WHOLE, ANY]
         some = moved.shape[1]
-        outs += [jax.ShapeDtypeStruct((some, 8 * ff), F32)] * 3 + [jax.ShapeDtypeStruct((8 * some, 1), F32)]
+        outs += [jax.ShapeDtypeStruct((some, 8 * ff), BF16)] * 3 + [jax.ShapeDtypeStruct((8 * some, 1), F32)]
         out_specs += [WHOLE] * 4
         scratch += [
             VMEM(moved.shape, BF16), VMEM(moved.shape, BF16), VMEM((8 * some, moved.shape[2]), BF16),
             pltpu.SemaphoreType.DMA(()), pltpu.SemaphoreType.DMA(()),
         ] + exchange_scratch()
     got = pl.pallas_call(
-        functools.partial(product_sum_kernel, turned, base is None),
+        functools.partial(product_sum_kernel, turned, moved is None),
         out_shape=outs,
         in_specs=specs,
         out_specs=out_specs,
@@ -1272,7 +1272,7 @@
         qkv, seg, heads, wide, d_att, full, den, out_part, blocked(g_dt), g_out, act_one, 7
     )
     grad_input, grad_gate, grad_up, grad_dt, along = product_sum(
-        after(d_qkv, g_qkv), attn, True, 6, x, gain_one, d_resid, blocked(g_gu), g_dt, w_gu, ff_own
+        after(d_qkv, g_qkv), attn, True, 6, x, gain_one, blocked(g_gu), g_dt, w_gu, ff_own
     )
 
     g_out = sum_rows(after(g_out, g_gu))
@@ -1291,21 +1291,24 @@
     )
     filler = jnp.zeros((g_qkv.shape[0], qkv_cols - used - 2), BF16)
     g_attn = jnp.concatenate([g_qkv[:, :used], gains.astype(BF16), filler, g_out], 1)
+    grad_input, grad_gate, grad_up, grad_dt, _ = lax.optimization_barrier(
+        (grad_input, grad_gate, grad_up, grad_dt, g_attn)
+    )
     g_attn = to_owners(g_attn, n_f)
 
     output = (resid + out_sum).astype(BF16)[None]
     return (
         output,
-        grad_input[None],
+        (d_resid + grad_input)[None],
         jnp.sum(g_attn[:, :, gain_at], 1),
         columns(g_attn, v_own, v_own + qk_own),
         columns(g_attn, v_own + qk_own, used),
         columns(g_attn, 0, v_own),
         columns(g_attn, qkv_cols, att_cols),
         jnp.sum(g_attn[:, :, gain_at + 1], 1),
-        grad_gate,
-        grad_up,
-        grad_dt.T,
+        grad_gate.astype(F32),
+        grad_up.astype(F32),
+        grad_dt.T.astype(F32),
     )
 
 

time: 548 us -> 540 us (0.985)
  local copies, waits for them, and re-layouts: 36.3 us -> 27.6 us
  other arithmetic: 14.7 us -> 22.9 us
  waiting for transfers between devices: 14.2 us -> 6.91 us
    all_to_all x1, waiting for transfers between devices: 8.28 us -> 1.03 us  [to_owners(): lax.all_to_all(part, 'fsdp', 0, 0, tiled=True)]
    convert_element_type x0 -> x3, other arithmetic: none -> 7.15 us  [the longest x1 2.43 us: on_device(): grad_up.astype(F32)]
    unnamed x47 -> x41, local copies, waits for them, and re-layouts: 19.2 us -> 12.3 us
  transfers between devices with their start and end apart: 9 -> 9, of which waited for: 3 -> 3; matrix products, arithmetic and copies ran while one was open for 4% -> 5% of each run, Pallas kernels for 84% -> 85%
where the time goes in v6:
time: 540 us; the launch traced here: 532 us
  Pallas kernels  450 us (83%)
  local copies, waits for them, and re-layouts  27.6 us (5%)
  other arithmetic  22.9 us (4%)
  between operations  14.8 us (3%)
  starting transfers between devices  9.79 us (2%)
  waiting for transfers between devices  6.91 us (1%)
    pallas_call x2, Pallas kernels, product_sum(): pl.pallas_call(functools.partial(product_sum_kernel, turned, moved is Non...  106 us
    pallas_call x1, Pallas kernels, attend(): pl.pallas_call(functools.partial(attend_kernel, heads, wide, blocks, link...  64.1 us
    pallas_call x1, Pallas kernels, attend_back(): pl.pallas_call(functools.partial(attend_back_kernel, heads, wide, blocks,...  63.8 us
    pallas_call x1, Pallas kernels, feed_back(): pl.pallas_call(functools.partial(feed_back_kernel, ff), out_shape=(jax.Sh...  60.3 us
    pallas_call x1, Pallas kernels, feed(): pl.pallas_call(functools.partial(feed_kernel, ff), out_shape=(jax.ShapeDt...  56.1 us
    pallas_call x1, Pallas kernels, start_exchange(): pl.pallas_call(start_kernel, out_shape=(jax.ShapeDtypeStruct((8,) + x.sha...  55.6 us
    pallas_call x1, Pallas kernels, project_back(): pl.pallas_call(project_back_kernel, out_shape=(jax.ShapeDtypeStruct((8 *...  43.7 us
    unnamed x41, local copies, waits for them, and re-layouts  12.3 us
  transfers between devices with their start and end apart: 9, of which 3 were waited for; matrix products, arithmetic and copies ran while one was open for 5% of the time, Pallas kernels for 85%

profile of v6, /device:TPU:0, one launch (start us, length us, event | category | flops | bytes accessed | tf_op | source)
XLA Modules:
  0.0 531.7 jit_solution(3576182956367198256)
XLA Ops:
  7.2 0.9 copy.120
  8.1 0.1 copy.123
  8.2 0.9 copy.121
  9.1 0.1 copy.124
  9.2 1.1 copy_bitcast_fusion.3
  10.3 0.7 broadcast_in_dim.14
  11.0 0.7 broadcast_in_dim.15
  11.8 1.1 concatenate.14
  13.0 5.3 all-to-all-start
  18.3 0.1 reshape.162
  18.5 0.1 reshape.163
  18.7 0.6 slice-done
  19.4 0.2 slice-done.2
  19.6 0.9 copy_bitcast_fusion.1
  20.5 3.5 concatenate.13
  24.0 5.4 %all-to-all-done = bf16[8,64,640]{2,1,0:T(8,128)(2,1)S(1)} async-done(((bf16[8,64,640]{2,1,0:T(8,128)(2,1)}), bf16[8,64,640]{2,1,0:T(8,128)(2,1)S(1)}, u32[]{:S(2)}, u32[]{:S(2)}) %all-to-all-start) | async-done | bytes 655392 | tf_op jit(solution)/shard_map/all_to_all | solution.py:1239
  29.4 0.8 copy-done.12
  30.3 55.6 %start_exchange.1 = (bf16[8,256,2048]{2,1,0:T(8,128)(2,1)}, bf16[8,64,1408]{2,1,0:T(8,128)(2,1)}) custom-call(bf16[256,2048]{1,0:T(8,128)(2,1)} %bitcast.93, bf16[8,64,1408]{2,1,0:T(8,128)(2,1)} %bitcast.78), custom_call_target="tpu_custom_call" | custom-call | flops 44999999488 | bytes 100000000 | tf_op jit(solution)/shard_map/start_exchange/pallas_call | solution.py:407
  86.1 0.5 copy-done.17
  86.7 0.6 slice.78
  87.3 0.4 copy.130.refs_3_.refs_1_
  87.7 0.1 reshape.172
  88.0 0.1 maximum_bitcast_fusion.refs_6_
  88.2 1.7 compare_convert_fusion.refs_5_.refs_3_
  89.9 2.6 fusion.2
  92.5 64.1 %attend.1 = (bf16[2048,384]{1,0:T(8,128)(2,1)}, bf16[2048,256]{1,0:T(8,128)(2,1)S(1)}, f32[2048,256]{1,0:T(8,128)}, f32[2048,2]{1,0:T(8,128)S(1)}, bf16[2048,204...) custom-call(bf16[2048,2048]{1,0:T(8,128)(2,1)} %bitcast.98, ...), custom_call_target="tpu_custom_call" | custom-call | flops 44999999488 | bytes 100000000 | tf_op jit(solution)/shard_map/attend/pallas_call | solution.py:742
  156.6 1.0 copy-done.3
  157.6 1.0 copy-done.6
  158.6 1.0 copy-done.7
  159.6 46.7 %product_sum.2 = (f32[256,2048]{1,0:T(8,128)}, bf16[256,2048]{1,0:T(8,128)(2,1)}) custom-call(bf16[2048,256]{1,0:T(8,128)(2,1)} %copy-done.6, bf16[256,2048]{1,0:T(8,128)(2,1)} %copy-done.7, bf16[256,2048]{1,0:T(8,128)(2,1)} %bitcast.94, f32[1,2048]{1,0:T(1,128)} %bitcast.90), custom_call_target="tpu_custom_call" | custom-call | flops 44999999488 | bytes 100000000 | tf_op jit(solution)/shard_map/product_sum/pallas_call | solution.py:365
  206.3 56.1 %feed.1 = (bf16[8,256,2048]{2,1,0:T(8,128)(2,1)}, f32[2048,1408]{1,0:T(8,128)}, bf16[8,256,768]{2,1,0:T(8,128)(2,1)}, bf16[2048,768]{1,0:T(8,128)(2,1)}) custom-call(bf16[8,256,2048]{2,1,0:T(8,128)(2,1)} %get-tuple-element.55.cot_ref, bf16[256,2048]{1,0:T(8,128)(2,1)} %get-tuple-element.56.act_ref, bf16[2048,1408]{1,0:T(8,128)(2,1)} %all-gather.6.cloned.1.call-done.w_ref.refs_4_), custom_call_target="tpu_custom_call" | custom-call | flops 44999999488 | bytes 100000000 | tf_op jit(solution)/shard_map/feed/pallas_call | solution.py:957
  262.5 60.3 %feed_back.1 = (f32[256,2048]{1,0:T(8,128)}, bf16[2048,1408]{1,0:T(8,128)(2,1)}) custom-call(bf16[8,256,2048]{2,1,0:T(8,128)(2,1)} %get-tuple-element.55.cot_ref, f32[8,256,1408]{2,1,0:T(8,128)} %bitcast.97, bf16[2048,2048]{1,0:T(8,128)(2,1)} %bitcast.99, bf16[2048,1408]{1,0:T(8,128)(2,1)} %all-gather.6.cloned.1.call-done.w_ref.refs_4_, ...), custom_call_target="tpu_custom_call" | custom-call | flops 44999999488 | bytes 100000000 | tf_op jit(solution)/shard_map/feed_back/pallas_call | solution.py:1078
  322.8 0.3 reduce-scatter.5.cloned.1.call-done
  323.2 1.5 copy-done.8
  324.7 0.2 multiply_reduce_fusion.1
  324.9 0.4 copy-done.9
  325.4 0.4 multiply_reduce_fusion
  325.8 0.8 copy-done.11
  326.6 0.6 fusion.3.p_ref
  327.2 43.7 %project_back.1 = (bf16[2048,256]{1,0:T(8,128)(2,1)S(1)}, bf16[8,256,2048]{2,1,0:T(8,128)(2,1)}, bf16[256,2048]{1,0:T(8,128)(2,1)S(1)}) custom-call(bf16[256,2048]{1,0:T(8,128)(2,1)S(1)} %fusion.3.p_ref, bf16[2048,768]{1,0:T(8,128)(2,1)} %bitcast.100, bf16[2048,768]{1,0:T(8,128)(2,1)} %all-gather.8.cloned.1.call-done.d_ref, bf16[256,2048]{1,0:T(8,128)(2,1)} %copy-done.7, ...), custom_call_target="tpu_custom_call" | custom-call | flops 44999999488 | bytes 100000000 | tf_op jit(solution)/shard_map/project_back/pallas_call | solution.py:1160
  370.9 1.0 copy-done.4
  371.9 1.0 copy-done.5
  372.9 63.8 %attend_back.1 = (bf16[2048,384]{1,0:T(8,128)(2,1)}, f32[256,2048]{1,0:T(8,128)}, bf16[8,64,768]{2,1,0:T(8,128)(2,1)}, bf16[8,256,256]{2,1,0:T(8,128)(2,1)}, bf16[2048,384]{1,0:T(8,128)(2,1)}) custom-call(bf16[2048,384]{1,0:T(8,128)(2,1)} %get-tuple-element.54.refs_0_, s32[2048,1]{1,0:T(8,128)} %copy-done, s32[8,1,256]{2,1,0:T(1,128)} %bitcast.66, ...), custom_call_target="tpu_custom_call" | custom-call | flops 44999999488 | bytes 100000000 | tf_op jit(solution)/shard_map/attend_back/pallas_call | solution.py:792
  436.8 2.6 slice_convert_fusion
  439.4 0.1 dynamic-slice_reduce_fusion
  439.5 59.5 %product_sum.3 = (f32[256,2048]{1,0:T(8,128)}, bf16[64,5504]{1,0:T(8,128)(2,1)}, bf16[64,5504]{1,0:T(8,128)(2,1)}, bf16[64,5504]{1,0:T(8,128)(2,1)}, f32[512,1]{1,0:T(8,128)}) custom-call(bf16[2048,384]{1,0:T(8,128)(2,1)} %get-tuple-element.73.l_ref, bf16[2048,640]{1,0:T(8,128)(2,1)} %all-gather.4.cloned.1.call-done.refs_2_.r_ref, ...), custom_call_target="tpu_custom_call" | custom-call | flops 44999999488 | bytes 100000000 | tf_op jit(solution)/shard_map/product_sum/pallas_call | solution.py:365
  499.0 1.1 divide_convert_fusion
  500.1 1.3 multiply_reduce_fusion.2
  501.4 0.1 stack.8
  501.6 2.0 concatenate.16
  503.7 4.2 all-to-all-start.1
  507.9 2.4 convert_element_type.99
  510.3 2.4 convert_element_type.100
  512.8 2.3 convert_bitcast_fusion
  515.1 3.0 add_bitcast_fusion
  518.0 1.0 all-to-all-done.1
  519.0 1.2 convert_bitcast_fusion.1
  520.2 0.8 slice_reduce_fusion
  521.1 0.1 fusion.4
  521.3 0.1 copy.133
  521.4 0.7 copy.137
  522.3 0.7 copy.138
  523.0 0.8 copy.144
  523.8 0.8 copy.145
  (69 shorter events, 1.2 us)
Async XLA Ops:
  13.0 5.4 %slice-start.1 = ((bf16[64,5504]{1,0:T(8,128)(2,1)}), bf16[64,384]{1,0:T(8,128)(2,1)S(1)}, s32[]{:S(2)}) async-start(bf16[64,5504]{1,0:T(8,128)(2,1)} %param.20), calls=%async_computation.14 | async-start | bytes 98304 | tf_op jit(solution)/shard_map/slice | solution.py:1243
  13.0 5.6 %slice-start.3 = ((bf16[64,5504]{1,0:T(8,128)(2,1)}), bf16[64,384]{1,0:T(8,128)(2,1)S(1)}, s32[]{:S(2)}) async-start(bf16[64,5504]{1,0:T(8,128)(2,1)} %param.21), calls=%async_computation.16 | async-start | bytes 98304 | tf_op jit(solution)/shard_map/slice | solution.py:1243
  13.0 16.5 %all-to-all-start = ((bf16[8,64,640]{2,1,0:T(8,128)(2,1)}), bf16[8,64,640]{2,1,0:T(8,128)(2,1)S(1)}, u32[]{:S(2)}, u32[]{:S(2)}) async-start(bf16[8,64,640]{2,1,0:T(8,128)(2,1)} %bitcast.5), calls=%async_computation | async-start | bytes 1310720 | tf_op jit(solution)/shard_map/all_to_all | solution.py:1239
  18.3 1.1 slice-start
  18.3 1.3 slice-start.2
  18.3 71.6 %all-gather.4.cloned.1.call-start = ((), (), s32[]{:S(2)}) async-start(), calls=%async_computation.6 | async-start | bytes 3276800 | tf_op jit(solution)/shard_map/all_gather | solution.py:1188
  29.4 0.8 copy-start.12
  30.3 176.0 %all-gather.6.cloned.1.call-start = ((), (), s32[]{:S(2)}) async-start(), calls=%async_computation.7 | async-start | bytes 7208960 | tf_op jit(solution)/shard_map/all_gather | solution.py:1188
  30.3 55.7 %copy-start.15 = (bf16[5504,64]{0,1:T(8,128)(2,1)S(1)}, bf16[5504,64]{0,1:T(8,128)(2,1)}, u32[]{:S(2)}) copy-start(bf16[5504,64]{0,1:T(8,128)(2,1)} %param.22) | copy-start | bytes 2113540
  86.0 0.7 copy-start.17
  86.0 176.5 %all-gather.8.cloned.1.call-start = ((), (), s32[]{:S(2)}) async-start(), calls=%async_computation.8 | async-start | bytes 3932160 | tf_op jit(solution)/shard_map/all_gather | solution.py:1188
  86.7 5.8 %copy-start.1 = (s32[2048]{0:T(1024)}, s32[2048]{0:T(1024)S(1)}, u32[]{:S(2)}) copy-start(s32[2048]{0:T(1024)S(1)} %convert_reduce_fusion) | copy-start | bytes 24580
  87.7 4.8 copy-start
  92.5 64.1 %copy-start.2 = (f32[2048]{0:T(1024)}, f32[2048]{0:T(1024)S(1)}, u32[]{:S(2)}) copy-start(f32[2048]{0:T(1024)S(1)} %get-tuple-element.145) | copy-start | bytes 24580
  156.6 1.0 copy-start.3
  157.6 1.0 copy-start.6
  158.6 1.0 copy-start.7
  159.5 163.6 %reduce-scatter.5.cloned.1.call-start = ((), (), s32[]{:S(2)}) async-start(), calls=%async_computation.9 | async-start | bytes 3932160 | tf_op jit(solution)/shard_map/reduce_scatter | solution.py:1192
  262.4 174.2 %reduce-scatter.7.cloned.1.call-start = ((), (), s32[]{:S(2)}) async-start(), calls=%async_computation.10 | async-start | bytes 7208960 | tf_op jit(solution)/shard_map/reduce_scatter | solution.py:1192
  323.1 1.6 copy-start.8
  323.1 1.8 copy-start.16
  323.1 177.0 %reduce-scatter.9.cloned.1.call-start = ((), (), s32[]{:S(2)}) async-start(), calls=%async_computation.11 | async-start | bytes 1966080 | tf_op jit(solution)/shard_map/reduce_scatter | solution.py:1192
  323.2 2.2 copy-start.9
  325.4 1.2 copy-start.11
  370.9 1.0 copy-start.4
  371.9 1.0 copy-start.5
  436.7 64.9 %reduce-scatter.11.cloned.1.call-start = ((), (), s32[]{:S(2)}) async-start(), calls=%async_computation.12 | async-start | bytes 1310720 | tf_op jit(solution)/shard_map/reduce_scatter | solution.py:1192
  503.7 15.4 %all-to-all-start.1 = ((bf16[8,64,640]{2,1,0:T(8,128)(2,1)}), bf16[8,64,640]{2,1,0:T(8,128)(2,1)}, u32[]{:S(2)}, u32[]{:S(2)}) async-start(bf16[8,64,640]{2,1,0:T(8,128)(2,1)} %bitcast.73), calls=%async_computation.5 | async-start | bytes 1310720 | tf_op jit(solution)/shard_map/all_to_all | solution.py:1197
  507.9 7.2 %copy-start.14 = (f32[256,2048]{1,0:T(8,128)S(1)}, f32[256,2048]{1,0:T(8,128)}, u32[]{:S(2)}) copy-start(f32[256,2048]{1,0:T(8,128)} %get-tuple-element.85) | copy-start | bytes 6291460
  510.3 4.7 copy-start.10
  510.3 4.7 copy-start.13
Sparse Core Ops, SparseCore 0:
  30.4 54.1 all-gather.3
  86.2 106.9 all-gather.5
  194.8 61.7 all-gather.7
  262.5 60.5 reduce-scatter.4
  325.3 102.3 reduce-scatter.6
  436.8 34.4 reduce-scatter.8
  473.7 26.0 reduce-scatter.10
